TPU v7x, 256 devices: a whole 4x4x8 slice. The times are simulated.
256 devices in a mesh: seq: 32 (over y, z), tp: 8 (over x, core).
Axes of the slice: x: 4, y: 4, z: 8, core: 2. Of those that a mesh axis runs over, the one named last changes fastest.
Arguments:
- hidden: bfloat16 [16384, 8192], P('seq', 'tp'), may hold values from -6 to 6
- value_weight: bfloat16 [8192, 4096], P('seq', 'tp'), may hold values from -0.0625 to 0.0625
- gate: bfloat16 [16384, 4096], P('seq', 'tp'), may hold values from -6 to 6
- filters: bfloat16 [16384, 32], P('seq', 'tp'), may hold values from -1 to 1
- skip_gain: float32 [4096], P('tp'), may hold values from 0.5 to 1.5
Outputs:
- mixed: bfloat16 [16384, 4096], P('seq', 'tp')
All inputs are finite; a program needn't handle non-finite values.
Results may differ from a plain program's by a relative error of at most 0.0051.
Values may be sent and summed in bfloat16 or wider, within the bound.
No kernel may reach another device: no remote copies, remote signals or barrier semaphores. Data moves between devices by JAX's collectives and lax.ppermute only.
A program may use at most 128 MiB of HBM per device.

v0:
```python
import math

import jax
import jax.numpy as jnp
from jax import lax
from jax.sharding import PartitionSpec as P


def across(table, projected_entries):
    return jnp.einsum("ak,ajc->jkc", table, projected_entries, precision=lax.Precision.HIGHEST)


def backward_across(table, projected_entries):
    return jnp.einsum("ak,jkc->jac", table, projected_entries, precision=lax.Precision.HIGHEST)


def within(table, projected_entries):
    return jnp.einsum("jm,jkc->mkc", table, projected_entries, precision=lax.Precision.HIGHEST)


def local_forward(cosine, sine, real_part, imag_part):
    return (
        within(cosine, real_part) + within(sine, imag_part),
        within(cosine, imag_part) - within(sine, real_part),
    )


def on_device(hidden, value_weight, gate, filters, skip_gain):
    whole = lax.all_gather(hidden, "tp", axis=1, tiled=True)
    tok = whole.shape[0]
    chan = value_weight.shape[1]
    groups = filters.shape[1]
    width = chan // groups
    value = jnp.dot(
        whole,
        lax.all_gather(value_weight, "seq", axis=0, tiled=True),
        preferred_element_type=jnp.float32,
    ).astype(jnp.bfloat16)
    peers = lax.axis_size("seq")
    index = lax.axis_index("seq")
    span = 2 * peers
    points = span * tok
    block = tok // peers
    moved, taps_moved = (
        lax.all_to_all(value[None], "seq", split_axis=1, concat_axis=0, tiled=True),
        lax.all_to_all(filters[None], "seq", split_axis=1, concat_axis=0, tiled=True),
    )
    moved = moved.astype(jnp.float32)
    taps_moved = taps_moved.astype(jnp.float32)
    offsets = jnp.arange(peers, dtype=jnp.int32)
    classes = jnp.arange(span, dtype=jnp.int32)
    first_angle = (
        2.0 * math.pi / span * (offsets[:, None] * classes[None, :] % span).astype(jnp.float32)
    )
    cosine_first = jnp.cos(first_angle)
    sine_first = jnp.sin(first_angle)
    spec_re = across(cosine_first, moved)
    spectrum_imaginary = -across(sine_first, moved)
    taps_re = across(cosine_first, taps_moved)
    taps_im = -across(sine_first, taps_moved)
    rows_global = index * block + jnp.arange(block, dtype=jnp.int32)
    twist_angle = (
        2.0
        * math.pi
        / points
        * (rows_global[:, None] * classes[None, :] % points).astype(jnp.float32)
    )
    twist_cos = jnp.cos(twist_angle)[:, :, None]
    twist_sin = jnp.sin(twist_angle)[:, :, None]
    turned_re = spec_re * twist_cos + spectrum_imaginary * twist_sin
    turned_im = spectrum_imaginary * twist_cos - spec_re * twist_sin
    tapped_re = taps_re * twist_cos + taps_im * twist_sin
    tapped_im = taps_im * twist_cos - taps_re * twist_sin
    sig_re, sig_im, fil_re, fil_im = (
        lax.all_to_all(turned_re, "seq", split_axis=1, concat_axis=0, tiled=True),
        lax.all_to_all(turned_im, "seq", split_axis=1, concat_axis=0, tiled=True),
        lax.all_to_all(tapped_re, "seq", split_axis=1, concat_axis=0, tiled=True),
        lax.all_to_all(tapped_im, "seq", split_axis=1, concat_axis=0, tiled=True),
    )
    positions = jnp.arange(tok, dtype=jnp.int32)
    local_angle = (
        2.0 * math.pi / tok * (positions[:, None] * positions[None, :] % tok).astype(jnp.float32)
    )
    cosine_local = jnp.cos(local_angle)
    sine_local = jnp.sin(local_angle)
    freq_re, freq_im = local_forward(cosine_local, sine_local, sig_re, sig_im)
    resp_re, resp_im = local_forward(cosine_local, sine_local, fil_re, fil_im)
    resp_re = jnp.repeat(resp_re, width, axis=2)
    resp_im = jnp.repeat(resp_im, width, axis=2)
    multiplied_realpart = freq_re * resp_re - freq_im * resp_im
    prod_im = freq_re * resp_im + freq_im * resp_re
    back_re = within(cosine_local, multiplied_realpart) - within(sine_local, prod_im)
    back_im = within(cosine_local, prod_im) + within(sine_local, multiplied_realpart)
    own_classes = 2 * index + jnp.arange(2, dtype=jnp.int32)
    return_angle = (
        2.0
        * math.pi
        / points
        * (positions[:, None] * own_classes[None, :] % points).astype(jnp.float32)
    )
    return_cos = jnp.cos(return_angle)[:, :, None]
    return_sin = jnp.sin(return_angle)[:, :, None]
    reverted_re = back_re * return_cos - back_im * return_sin
    reverted_im = back_im * return_cos + back_re * return_sin
    gathered_re, gathered_im = (
        lax.all_to_all(reverted_re, "seq", split_axis=0, concat_axis=1, tiled=True),
        lax.all_to_all(reverted_im, "seq", split_axis=0, concat_axis=1, tiled=True),
    )
    real_out = (
        backward_across(cosine_first, gathered_re) - backward_across(sine_first, gathered_im)
    ) / points
    arrived = lax.all_to_all(real_out, "seq", split_axis=1, concat_axis=0, tiled=True).reshape(
        tok, chan
    )
    mixed = gate.astype(jnp.float32) * (arrived + skip_gain[None, :] * value.astype(jnp.float32))
    return mixed.astype(jnp.bfloat16)


def solution(mesh):
    in_specs = (P("seq", "tp"), P("seq", "tp"), P("seq", "tp"), P("seq", "tp"), P("tp"))
    out_specs = P("seq", "tp")
    return jax.shard_map(
        on_device, mesh=mesh, in_specs=in_specs, out_specs=out_specs, check_vma=False
    )
```

profile of v0, /device:TPU:32, one launch (start us, length us, event | category | flops | bytes accessed | tf_op | source)
XLA Modules:
  0.0 563.6 jit_solution(5382735052400518620)
XLA Ops:
  9.6 11.4 %all-to-all-start.3 = ((bf16[1,512,4]{2,0,1:T(2,128)(2,1)}), bf16[1,512,4]{2,0,1:T(2,128)(2,1)S(1)}, u32[]{:S(2)}, u32[]{:S(2)}) async-start(bf16[1,512,4]{2,0,1:T(2,128)(2,1)} %copy.73), calls=%async_computation.3 | async-start | bytes 524288 | tf_op jit(solution)/shard_map/all_to_all | solution.py:46
  21.0 43.1 %all-gather.3.cloned.1.call-done = bf16[512,8192]{1,0:T(8,128)(2,1)} async-done(((bf16[512,1024]{1,0:T(8,128)(2,1)}), bf16[512,8192]{1,0:T(8,128)(2,1)}) %all-gather.3.cloned.1.call-update) | async-done | bytes 8388624 | tf_op jit(solution)/shard_map/all_gather | solution.py:29
  64.1 99.6 %all-gather.5.cloned.1.call-done = bf16[8192,512]{1,0:T(8,128)(2,1)} async-done(((bf16[256,512]{1,0:T(8,128)(2,1)}), bf16[8192,512]{1,0:T(8,128)(2,1)}) %all-gather.5.cloned.1.call-update) | async-done | bytes 8388624 | tf_op jit(solution)/shard_map/all_gather | solution.py:36
  163.7 10.2 %convolution_convert_fusion = bf16[512,512]{1,0:T(8,128)(2,1)S(1)} fusion(bf16[512,8192]{1,0:T(8,128)(2,1)} %all-gather.3.cloned.1.call-done, bf16[8192,512]{1,0:T(8,128)(2,1)} %all-gather.5.cloned.1.call-done), kind=kOutput, calls=%fused_computation.18 | convolution fusion | flops 4295229440 | bytes 17301504 | tf_op jit(solution)/shard_map/dot_general | solution.py:34
  180.3 7.6 %all-to-all-start = ((bf16[32,2,4096]{2,1,0:T(2,128)(2,1)}), bf16[32,2,4096]{2,1,0:T(2,128)(2,1)S(1)}, u32[]{:S(2)}, u32[]{:S(2)}) async-start(bf16[32,2,4096]{2,1,0:T(2,128)(2,1)} %reshape.140), calls=%async_computation | async-start | bytes 1048576 | tf_op jit(solution)/shard_map/all_to_all | solution.py:45
  190.4 14.7 %all-to-all-done = bf16[32,2,4096]{2,1,0:T(2,128)(2,1)S(1)} async-done(((bf16[32,2,4096]{2,1,0:T(2,128)(2,1)}), bf16[32,2,4096]{2,1,0:T(2,128)(2,1)S(1)}, u32[]{:S(2)}, u32[]{:S(2)}) %all-to-all-start) | async-done | bytes 524320 | tf_op jit(solution)/shard_map/all_to_all | solution.py:45
  205.1 4.8 all-to-all-start.5
  211.9 6.7 %all-to-all-done.5 = f32[32,1,128]{2,1,0:T(1,128)S(1)} async-done(((f32[32,1,128]{2,1,0:T(1,128)}), f32[32,1,128]{2,1,0:T(1,128)S(1)}, u32[]{:S(2)}, u32[]{:S(2)}) %all-to-all-start.5) | async-done | bytes 16416 | tf_op jit(solution)/shard_map/all_to_all | solution.py:78
  218.6 5.1 all-to-all-start.4
  232.4 6.9 %all-to-all-start.1 = ((f32[16,64,512]{2,0,1:T(8,128)}), f32[16,64,512]{2,0,1:T(8,128)S(1)}, u32[]{:S(2)}, u32[]{:S(2)}) async-start(f32[16,64,512]{2,0,1:T(8,128)} %copy.69), calls=%async_computation.1 | async-start | bytes 4194304 | tf_op jit(solution)/shard_map/all_to_all | solution.py:75
  239.3 4.1 copy.71
  243.4 44.3 %all-to-all-done.1 = f32[16,64,512]{2,0,1:T(8,128)S(1)} async-done(((f32[16,64,512]{2,0,1:T(8,128)}), f32[16,64,512]{2,0,1:T(8,128)S(1)}, u32[]{:S(2)}, u32[]{:S(2)}) %all-to-all-start.1) | async-done | bytes 2097184 | tf_op jit(solution)/shard_map/all_to_all | solution.py:75
  289.1 5.5 all-to-all-start.2
  297.3 5.2 fusion.16
  302.5 5.2 convolution_add_fusion.2
  308.0 5.2 fusion.14
  313.2 5.2 convolution_subtract_fusion.3
  331.5 9.5 %fusion.24 = f32[512,2,512]{2,0,1:T(8,128)} fusion(f32[512,2,512]{2,0,1:T(8,128)S(1)} %bitcast.137), kind=kOutput, calls=%fused_computation.46 | convolution fusion | flops 3224895488 | bytes 4194304 | tf_op jit(solution)/shard_map/jm,jkc->mkc/dot_general | solution.py:18
  345.0 7.3 %fusion.22 = f32[512,2,512]{2,0,1:T(8,128)S(1)} fusion(f32[512,2,512]{2,0,1:T(8,128)S(1)} %bitcast.139), kind=kOutput, calls=%fused_computation.44 | convolution fusion | flops 3224895488 | bytes 4194304 | tf_op jit(solution)/shard_map/jm,jkc->mkc/dot_general | solution.py:18
  352.4 7.6 %convolution_add_fusion.1 = f32[512,2,512]{2,0,1:T(8,128)S(1)} fusion(f32[512,2,512]{2,0,1:T(8,128)S(1)} %copy-done.4, f32[512,2,512]{2,0,1:T(8,128)S(1)} %bitcast.140), kind=kOutput, calls=%fused_computation.11 | convolution fusion | flops 3225419776 | bytes 6291456 | tf_op jit(solution)/shard_map/jm,jkc->mkc/dot_general | solution.py:18
  360.0 8.1 %multiply_subtract_fusion.1 = (f32[512,2,512]{2,0,1:T(8,128)S(1)}, f32[512,2,512]{2,0,1:T(8,128)S(1)}) fusion(f32[512,2,512]{2,0,1:T(8,128)S(1)} %reshape.130, f32[512,2,512]{2,0,1:T(8,128)S(1)} %convolution_add_fusion.1, f32[512,2,512]{2,0,1:T(8,128)S(1)} %copy-done, f32[512,2,512]{2,0,1:T(8,128)S(1)} %fusion.22, f32[512,2,512]{2,0,1:T(8,128)S(1)} %bitcast.138), kind=kOutput, calls=%fused_computation.5 | convolution fusion | flops 3228565504 | bytes 14680064 | tf_op jit(solution)/shard_map/jm,jkc->mkc/dot_general | solution.py:18
  368.1 7.5 %fusion.20 = f32[512,2,512]{2,0,1:T(8,128)S(1)} fusion(f32[512,2,512]{2,0,1:T(8,128)S(1)} %get-tuple-element.5), kind=kOutput, calls=%fused_computation.42 | convolution fusion | flops 3224895488 | bytes 4194304 | tf_op jit(solution)/shard_map/jm,jkc->mkc/dot_general | solution.py:18
  375.6 7.8 %fusion.18 = f32[512,2,512]{2,0,1:T(8,128)S(1)} fusion(f32[512,2,512]{2,0,1:T(8,128)S(1)} %get-tuple-element.6), kind=kOutput, calls=%fused_computation.40 | convolution fusion | flops 3224895488 | bytes 4194304 | tf_op jit(solution)/shard_map/jm,jkc->mkc/dot_general | solution.py:18
  383.4 7.4 %convolution_add_fusion = f32[512,2,512]{2,0,1:T(8,128)S(1)} fusion(f32[512,2,512]{2,0,1:T(8,128)S(1)} %fusion.18, f32[512,2,512]{2,0,1:T(8,128)S(1)} %get-tuple-element.5), kind=kOutput, calls=%fused_computation.8 | convolution fusion | flops 3225419776 | bytes 6291456 | tf_op jit(solution)/shard_map/jm,jkc->mkc/dot_general | solution.py:18
  390.8 9.6 %multiply_add_fusion = (f32[512,2,512]{2,0,1:T(8,128)S(1)}, f32[512,2,512]{2,0,1:T(8,128)}) fusion(f32[512,2,512]{2,0,1:T(8,128)S(1)} %convolution_add_fusion, f32[512,2]{0,1:T(2,128)S(1)} %get-tuple-element.14, f32[512,2]{0,1:T(2,128)S(1)} %get-tuple-element.13, f32[512,2,512]{2,0,1:T(8,128)S(1)} %fusion.20, f32[512,2,512]{2,0,1:T(8,128)S(1)} %get-tuple-element.6), kind=kOutput, calls=%fused_computation.2 | convolution fusion | flops 3228565504 | bytes 10493952 | tf_op jit(solution)/shard_map/jm,jkc->mkc/dot_general | solution.py:18
  403.4 7.7 %all-to-all-start.7 = ((f32[512,2,512]{2,1,0:T(2,128)}), f32[512,2,512]{2,1,0:T(2,128)S(1)}, u32[]{:S(2)}, u32[]{:S(2)}) async-start(f32[512,2,512]{2,1,0:T(2,128)} %copy.91), calls=%async_computation.7 | async-start | bytes 4194304 | tf_op jit(solution)/shard_map/all_to_all | solution.py:107
  411.1 4.5 copy.89
  415.6 43.5 %all-to-all-done.7 = f32[512,2,512]{2,1,0:T(2,128)S(1)} async-done(((f32[512,2,512]{2,1,0:T(2,128)}), f32[512,2,512]{2,1,0:T(2,128)S(1)}, u32[]{:S(2)}, u32[]{:S(2)}) %all-to-all-start.7) | async-done | bytes 2097184 | tf_op jit(solution)/shard_map/all_to_all | solution.py:107
  459.1 5.3 all-to-all-start.6
  469.6 41.8 %all-to-all-done.6 = f32[512,2,512]{2,1,0:T(2,128)} async-done(((f32[512,2,512]{2,1,0:T(2,128)}), f32[512,2,512]{2,1,0:T(2,128)}, u32[]{:S(2)}, u32[]{:S(2)}) %all-to-all-start.6) | async-done | bytes 2097184 | tf_op jit(solution)/shard_map/all_to_all | solution.py:106
  511.5 4.0 copy.115
  524.3 31.3 %all_to_all.147 = f32[16,32,512]{2,0,1:T(8,128)S(1)} all-to-all(f32[16,32,512]{2,0,1:T(8,128)S(1)} %copy.93), channel_id=1, replica_groups=mesh['seq'=32,'tp'=8] {'seq'}, dimensions={1} | all-to-all | bytes 2097152 | tf_op jit(solution)/shard_map/all_to_all | solution.py:112
  (70 shorter events, 61.6 us)
Async XLA Ops:
  6.5 57.5 %all-gather.3.cloned.1.call-start = ((), (), s32[]{:S(2)}) async-start(), calls=%async_computation.9 | async-start | bytes 9437184 | tf_op jit(solution)/shard_map/all_gather | solution.py:29
  7.3 156.4 %all-gather.5.cloned.1.call-start = ((), (), s32[]{:S(2)}) async-start(), calls=%async_computation.10 | async-start | bytes 8650752 | tf_op jit(solution)/shard_map/all_gather | solution.py:36
  9.6 170.7 %all-to-all-start.3 = ((bf16[1,512,4]{2,0,1:T(2,128)(2,1)}), bf16[1,512,4]{2,0,1:T(2,128)(2,1)S(1)}, u32[]{:S(2)}, u32[]{:S(2)}) async-start(bf16[1,512,4]{2,0,1:T(2,128)(2,1)} %copy.73), calls=%async_computation.3 | async-start | bytes 524288 | tf_op jit(solution)/shard_map/all_to_all | solution.py:46
  180.3 24.9 %all-to-all-start = ((bf16[32,2,4096]{2,1,0:T(2,128)(2,1)}), bf16[32,2,4096]{2,1,0:T(2,128)(2,1)S(1)}, u32[]{:S(2)}, u32[]{:S(2)}) async-start(bf16[32,2,4096]{2,1,0:T(2,128)(2,1)} %reshape.140), calls=%async_computation | async-start | bytes 1048576 | tf_op jit(solution)/shard_map/all_to_all | solution.py:45
  205.1 13.5 %all-to-all-start.5 = ((f32[32,1,128]{2,1,0:T(1,128)}), f32[32,1,128]{2,1,0:T(1,128)S(1)}, u32[]{:S(2)}, u32[]{:S(2)}) async-start(f32[32,1,128]{2,1,0:T(1,128)} %reshape.144), calls=%async_computation.5 | async-start | bytes 32768 | tf_op jit(solution)/shard_map/all_to_all | solution.py:78
  218.6 13.8 %all-to-all-start.4 = ((f32[32,1,128]{2,1,0:T(1,128)}), f32[32,1,128]{2,1,0:T(1,128)S(1)}, u32[]{:S(2)}, u32[]{:S(2)}) async-start(f32[32,1,128]{2,1,0:T(1,128)} %reshape.142), calls=%async_computation.4 | async-start | bytes 32768 | tf_op jit(solution)/shard_map/all_to_all | solution.py:77
  232.4 55.3 %all-to-all-start.1 = ((f32[16,64,512]{2,0,1:T(8,128)}), f32[16,64,512]{2,0,1:T(8,128)S(1)}, u32[]{:S(2)}, u32[]{:S(2)}) async-start(f32[16,64,512]{2,0,1:T(8,128)} %copy.69), calls=%async_computation.1 | async-start | bytes 4194304 | tf_op jit(solution)/shard_map/all_to_all | solution.py:75
  287.7 1.4 copy-start.3
  289.1 54.0 %all-to-all-start.2 = ((f32[16,64,512]{2,0,1:T(8,128)}), f32[16,64,512]{2,0,1:T(8,128)}, u32[]{:S(2)}, u32[]{:S(2)}) async-start(f32[16,64,512]{2,0,1:T(8,128)} %copy.71), calls=%async_computation.2 | async-start | bytes 4194304 | tf_op jit(solution)/shard_map/all_to_all | solution.py:76
  330.1 1.4 copy-start.1
  345.0 7.4 %copy-start.4 = (f32[512,2,512]{2,0,1:T(8,128)S(1)}, f32[512,2,512]{2,0,1:T(8,128)}, u32[]{:S(2)}) copy-start(f32[512,2,512]{2,0,1:T(8,128)} %fusion.24) | copy-start | bytes 6291460
  352.4 7.6 %copy-start = (f32[512,2,512]{2,0,1:T(8,128)S(1)}, f32[512,2,512]{2,0,1:T(8,128)}, u32[]{:S(2)}) copy-start(f32[512,2,512]{2,0,1:T(8,128)} %reshape.129) | copy-start | bytes 6291460
  352.4 7.6 %copy-start.2 = (f32[16,32,2,512]{3,0,1,2:T(8,128)S(1)}, f32[16,32,2,512]{3,0,1,2:T(8,128)}, u32[]{:S(2)}) copy-start(f32[16,32,2,512]{3,0,1,2:T(8,128)} %copy-done.1) | copy-start | bytes 6291460
  403.4 55.7 %all-to-all-start.7 = ((f32[512,2,512]{2,1,0:T(2,128)}), f32[512,2,512]{2,1,0:T(2,128)S(1)}, u32[]{:S(2)}, u32[]{:S(2)}) async-start(f32[512,2,512]{2,1,0:T(2,128)} %copy.91), calls=%async_computation.7 | async-start | bytes 4194304 | tf_op jit(solution)/shard_map/all_to_all | solution.py:107
  459.1 52.4 %all-to-all-start.6 = ((f32[512,2,512]{2,1,0:T(2,128)}), f32[512,2,512]{2,1,0:T(2,128)}, u32[]{:S(2)}, u32[]{:S(2)}) async-start(f32[512,2,512]{2,1,0:T(2,128)} %copy.89), calls=%async_computation.6 | async-start | bytes 4194304 | tf_op jit(solution)/shard_map/all_to_all | solution.py:106
  523.6 31.9 %copy-start.5 = (bf16[512,512]{1,0:T(8,128)(2,1)S(1)}, bf16[512,512]{1,0:T(8,128)(2,1)}, u32[]{:S(2)}) copy-start(bf16[512,512]{1,0:T(8,128)(2,1)} %param.7) | copy-start | bytes 1572868
  523.6 31.9 %copy-start.6 = (f32[512]{0:T(512)S(1)}, f32[512]{0:T(512)}, u32[]{:S(2)}) copy-start(f32[512]{0:T(512)} %param.9) | copy-start | bytes 6148
Sparse Core Ops, SparseCore 0:
  9.2 54.8 all-gather.2
  66.7 96.9 all-gather.4
where the time goes:
time: 573 us; the launch traced here: 564 us
  waiting for transfers between devices  300 us (52%)
  matrix products  105 us (18%)
  starting transfers between devices  54.4 us (9%)
  local copies, waits for them, and re-layouts  51.9 us (9%)
  blocking collectives  31.3 us (5%)
  between operations  14.1 us (2%)
  other arithmetic  6.5 us (1%)
    all_gather x1, waiting for transfers between devices, on_device(): lax.all_gather(value_weight, 'seq', axis=0, tiled=True)  99.6 us
    dot_general x12, matrix products, within(): jnp.einsum('jm,jkc->mkc', table, projected_entries, precision=lax.Precisi...  85.7 us
    all_to_all x1, waiting for transfers between devices, on_device(): lax.all_to_all(turned_re, 'seq', split_axis=1, concat_axis=0, tiled=True)  44.3 us
    all_to_all x1, waiting for transfers between devices, on_device(): lax.all_to_all(reverted_im, 'seq', split_axis=0, concat_axis=1, tiled=True)  43.5 us
    all_gather x1, waiting for transfers between devices, on_device(): whole = lax.all_gather(hidden, 'tp', axis=1, tiled=True)  43.1 us
    all_to_all x1, waiting for transfers between devices, on_device(): lax.all_to_all(reverted_re, 'seq', split_axis=0, concat_axis=1, tiled=True)  41.8 us
    all_to_all x1, blocking collectives, on_device(): lax.all_to_all(real_out, 'seq', split_axis=1, concat_axis=0, tiled=True)  31.3 us
    all_to_all x1, waiting for transfers between devices, on_device(): lax.all_to_all(value[None], 'seq', split_axis=1, concat_axis=0, tiled=True)  14.7 us
  transfers between devices with their start and end apart: 10, of which 9 were waited for; matrix products, arithmetic and copies ran while one was open for 15% of the time, Pallas kernels for 0%

commit v1 on v0

v1 whole, which is shorter than its diff:
```python
import functools

import jax
import jax.numpy as jnp
from jax import lax
from jax.experimental import pallas as pl
from jax.experimental.pallas import tpu as pltpu
from jax.sharding import PartitionSpec as P

NY, NZ = 4, 8
FIRST = 112
TAP_ROWS = 16
WHOLE_VMEM = 60 * 1000 * 1000
VMEM_LIMIT = 16 * 1024 * 1024


def take_from(array, dy, dz):
    pairs = [
        (((y + dy) % NY) * NZ + (z + dz) % NZ, y * NZ + z) for y in range(NY) for z in range(NZ)
    ]
    return lax.ppermute(array, "seq", pairs)


def gather_weight(weight, filters):
    taps = jnp.tile(filters.T, (TAP_ROWS // filters.shape[1], 1))
    first = jnp.concatenate([weight[:FIRST], taps], axis=0)
    second = weight[FIRST:]

    def halves(one, other, dy, dz):
        half = one.shape[0] // 2
        return take_from(one[:half], dy, dz), take_from(other[half:], -dy, -dz)

    line = {0: first}
    up, down = take_from(second, 1, 0), take_from(second, -1, 0)
    for k in (1, 2, 3):
        line[k] = take_from(line[k - 1], 0, 1)
        line[-k] = take_from(line[1 - k], 0, -1)
    far = jnp.concatenate(halves(up, down, 1, 0), axis=0)
    column = jnp.stack([second, up, far, down])
    column, line[3], line[-3] = lax.optimization_barrier((column, line[3], line[-3]))
    line[4] = jnp.concatenate(halves(line[3], line[-3], 0, 1), axis=0)
    mine = jnp.stack([line[k] for k in (0, 1, 2, 3, 4, -3, -2, -1)])
    above, below = take_from(mine, 1, 0), take_from(mine, -1, 0)
    firsts = [mine, above, below, *halves(above, below, 1, 0)]
    ring = {0: column}
    for k in (1, 2, 3):
        ring[k] = take_from(ring[k - 1], 0, 1)
        ring[-k] = take_from(ring[1 - k], 0, -1)
    seconds = [ring[k] for k in (0, 1, 2, 3, -3, -2, -1)] + list(halves(ring[3], ring[-3], 0, 1))
    across = jnp.concatenate([firsts[3][:, FIRST:], firsts[4][:, FIRST:]], axis=0)
    taps = jnp.stack([mine[:, FIRST:], above[:, FIRST:], across, below[:, FIRST:]])
    return firsts, seconds, taps


def sources_of(dy, dz):
    one = (3 + dz // 4, dz % 4) if dy == 2 else ({0: 0, 1: 1, 3: 2}[dy], dz)
    other = (12 + dy // 2, dy % 2) if dz == 4 else (5 + (dz if dz < 4 else dz - 1), dy)
    return one, other


def project_kernel(steps, names, last, *refs):
    place, hidden_source = refs[:2]
    arrays = dict(zip(names, refs[2 : 2 + len(names)], strict=True))
    refs = refs[2 + len(names) :]
    before = None
    if last:
        before, refs = refs[0], refs[1:]
    out, hidden, weight, sem = refs
    y, z = place[0], place[1]
    copies = []
    for count, step in enumerate(steps):
        started = []
        for n, (dy, dz) in enumerate(step):
            row = (sum(len(s) for s in steps[:count]) + n) * 256
            block = lax.rem(y + dy, NY) * NZ + lax.rem(z + dz, NZ)
            pairs = [
                (
                    hidden_source.at[:, pl.ds(pl.multiple_of(block * 256, 256), 256)],
                    hidden.at[:, row : row + 256],
                )
            ]
            for (name, at), lo, hi in zip(sources_of(dy, dz), (0, FIRST), (FIRST, 256), strict=True):
                target = weight.at[row + lo : row + hi, :]
                pairs.append((arrays[name].at[at, 0 : hi - lo, :], target))
            for k, (source, target) in enumerate(pairs):
                copy = pltpu.make_async_copy(source, target, sem.at[row // 256, k])
                copy.start()
                started.append(copy)
        copies.append(started)
    total = before[...] if last else jnp.zeros((512, 512), jnp.float32)
    row = 0
    for step, started in zip(steps, copies, strict=True):
        for copy in started:
            copy.wait()
        rows = slice(row, row + 256 * len(step))
        total += jnp.dot(hidden[:, rows], weight[rows, :], preferred_element_type=jnp.float32)
        row += 256 * len(step)
    if last:
        out[...] = total.T.reshape(32, 16, 512).astype(jnp.bfloat16)
    else:
        out[...] = total


def project(place, hidden, pieces, steps, before=None):
    last = before is not None
    names = sorted(
        {name for step in steps for at in step for name, _ in sources_of(*at)}
    )
    count = sum(len(step) for step in steps)
    shape = (
        jax.ShapeDtypeStruct((32, 16, 512), jnp.bfloat16)
        if last
        else jax.ShapeDtypeStruct((512, 512), jnp.float32)
    )
    whole = pl.BlockSpec(memory_space=pltpu.VMEM)
    apart = pl.BlockSpec(memory_space=pl.ANY)
    return pl.pallas_call(
        functools.partial(project_kernel, steps, names, last),
        out_shape=shape,
        in_specs=[pl.BlockSpec(memory_space=pltpu.SMEM)]
        + [apart] * (1 + len(names))
        + [whole] * last,
        out_specs=whole,
        scratch_shapes=[
            pltpu.VMEM((512, 256 * count), jnp.bfloat16),
            pltpu.VMEM((256 * count, 512), jnp.bfloat16),
            pltpu.SemaphoreType.DMA((count, 3)),
        ],
        compiler_params=pltpu.CompilerParams(vmem_limit_bytes=WHOLE_VMEM),
        cost_estimate=pl.CostEstimate(
            flops=2 * 512 * 512 * 256 * count,
            bytes_accessed=count * 512 * 1024,
            transcendentals=0,
        ),
        name="project_last" if last else "project_early",
    )(place, hidden, *[pieces[name] for name in names], *([before] if last else []))


EARLY = [[(dy, dz) for dz in dzs] for dy in (0, 1, 3) for dzs in ((0, 1, 2, 3), (5, 6, 7))]
LATE = [
    [(2, 0), (2, 1), (2, 2), (2, 3)],
    [(0, 4), (1, 4), (3, 4), (2, 4)],
    [(2, 5), (2, 6), (2, 7)],
]


def strip_kernel(place, taps, out):
    rows, step = 256, 512
    y, z, which = place[0], place[1], place[2]
    pick = lax.broadcasted_iota(jnp.int32, (TAP_ROWS, step), 0) == which

    def chunk(i, before):
        dy = lax.rem(lax.div(i, NZ) - y + NY, NY)
        dz = lax.rem(lax.rem(i, NZ) - z + NZ, NZ)
        held = taps[dy, dz].astype(jnp.float32)
        block = jnp.sum(jnp.where(pick, held, 0.0), axis=0, keepdims=True)
        window = jnp.concatenate([before, block], axis=1)
        window = jnp.broadcast_to(window, (rows, step + rows))
        rolled = pltpu.roll(window, 0, 1, stride=1, stride_axis=0)
        out[:, pl.ds(pl.multiple_of(i * step, step), step)] = rolled[:, rows:].astype(jnp.bfloat16)
        return block[:, step - rows :]

    lax.fori_loop(0, out.shape[1] // step, chunk, jnp.zeros((1, rows), jnp.float32))


def strip(place, taps):
    vmem = pl.BlockSpec(memory_space=pltpu.VMEM)
    return pl.pallas_call(
        strip_kernel,
        out_shape=jax.ShapeDtypeStruct((256, 16384), jnp.bfloat16),
        in_specs=[pl.BlockSpec(memory_space=pltpu.SMEM), vmem],
        out_specs=vmem,
        compiler_params=pltpu.CompilerParams(vmem_limit_bytes=VMEM_LIMIT),
        cost_estimate=pl.CostEstimate(flops=10 << 20, bytes_accessed=8 << 20, transcendentals=0),
        name="strip",
    )(place, taps)


def conv_kernel(value, strip_ref, out, stacked, total):
    for e in range(4):
        for b in range(64):
            rows = slice(16 * b, 16 * b + 16)
            cols = slice(256 * e, 256 * e + 256)
            if b - e < 0:
                stacked[rows, cols] = jnp.zeros((16, 256), jnp.bfloat16)
            else:
                j, m = divmod(b - e, 2)
                stacked[rows, cols] = value[j, :, 256 * m : 256 * m + 256]
    for g in range(16):
        taps = jnp.concatenate(
            [strip_ref[:, 256 * (4 * g + e) : 256 * (4 * g + e + 1)] for e in range(4)], axis=0
        )
        term = jnp.dot(stacked[: 1024 - 64 * g], taps, preferred_element_type=jnp.float32)
        if g == 0:
            total[...] = term
        else:
            total[64 * g :] += term
    for b in range(64):
        j, m = divmod(b, 2)
        out[j, :, 256 * m : 256 * m + 256] = total[16 * b : 16 * b + 16].astype(jnp.bfloat16)


def convolve(value, taps_strip):
    vmem = pl.BlockSpec(memory_space=pltpu.VMEM)
    return pl.pallas_call(
        conv_kernel,
        out_shape=jax.ShapeDtypeStruct((32, 16, 512), jnp.bfloat16),
        in_specs=[vmem, vmem],
        out_specs=vmem,
        scratch_shapes=[
            pltpu.VMEM((1024, 1024), jnp.bfloat16),
            pltpu.VMEM((1024, 256), jnp.float32),
        ],
        compiler_params=pltpu.CompilerParams(vmem_limit_bytes=VMEM_LIMIT),
        cost_estimate=pl.CostEstimate(
            flops=4_500_000_000, bytes_accessed=10 << 20, transcendentals=0
        ),
        name="convolve",
    )(value, taps_strip)


def mix_kernel(conv, value, gain, gate, out):
    column = jnp.transpose(jnp.broadcast_to(gain[...], (8, gain.shape[1])))[:, :1]
    total = conv[...].astype(jnp.float32) + column * value[...].astype(jnp.float32)
    out[...] = (gate[...].astype(jnp.float32) * total.T).astype(jnp.bfloat16)


def mix(conv, value, gain, gate):
    return pl.pallas_call(
        mix_kernel,
        out_shape=jax.ShapeDtypeStruct((512, 512), jnp.bfloat16),
        grid=(4,),
        in_specs=[
            pl.BlockSpec((128, 512), lambda i: (i, 0)),
            pl.BlockSpec((128, 512), lambda i: (i, 0)),
            pl.BlockSpec((1, 128), lambda i: (0, i)),
            pl.BlockSpec((512, 128), lambda i: (0, i)),
        ],
        out_specs=pl.BlockSpec((512, 128), lambda i: (0, i)),
        compiler_params=pltpu.CompilerParams(vmem_limit_bytes=VMEM_LIMIT),
        name="mix",
    )(conv, value, gain, gate)


def on_device(hidden, value_weight, gate, filters, skip_gain):
    index = lax.axis_index("seq")
    place = jnp.stack([index // NZ, index % NZ, index // 8]).astype(jnp.int32)
    whole = lax.all_gather(hidden, "tp", axis=1, tiled=True)
    firsts, seconds, taps = gather_weight(value_weight, filters)
    pieces = [*firsts, *seconds]
    early = project(place, whole, pieces, EARLY)
    value = project(place, whole, pieces, LATE, early)
    value, taps = lax.optimization_barrier((value, taps))
    taps_strip = strip(place, taps)
    value, taps_strip = lax.optimization_barrier((value, taps_strip))
    moved = lax.all_to_all(value, "seq", split_axis=0, concat_axis=0, tiled=True)
    conv = convolve(moved, taps_strip)
    arrived = lax.all_to_all(conv, "seq", split_axis=0, concat_axis=0, tiled=True)
    return mix(arrived.reshape(512, 512), value.reshape(512, 512), skip_gain[None], gate)


def solution(mesh):
    in_specs = (P("seq", "tp"), P("seq", "tp"), P("seq", "tp"), P("seq", "tp"), P("tp"))
    out_specs = P("seq", "tp")
    return jax.shard_map(
        on_device, mesh=mesh, in_specs=in_specs, out_specs=out_specs, check_vma=False
    )
```

time: 573 us -> 169 us (0.29); the launches traced: 564 us -> 169 us
  waiting for transfers between devices: 300 us -> 48.7 us
  matrix products: 105 us -> 0 us
  local copies, waits for them, and re-layouts: 51.9 us -> 9.18 us
  Pallas kernels: 0 us -> 25.3 us
  starting transfers between devices: 54.4 us -> 32 us
  blocking collectives: 31.3 us -> 38.3 us
    all_to_all x8 -> x0, waiting for transfers between devices: 156 us -> none  [the longest x1 44.3 us: on_device(): lax.all_to_all(turned_re, 'seq', split_axis=1, concat_axis=0, tiled=True)]
    dot_general x19 -> x0, matrix products: 105 us -> none  [the longest x12 85.7 us: within(): jnp.einsum('jm,jkc->mkc', table, projected_entries, precision=lax.Precisi...]
    all_gather x1 -> x0, waiting for transfers between devices: 99.6 us -> none  [on_device(): lax.all_gather(value_weight, 'seq', axis=0, tiled=True)]
    all_to_all x8 -> x0, starting transfers between devices: 54.4 us -> none  [the longest x1 11.4 us: on_device(): lax.all_to_all(filters[None], 'seq', split_axis=1, concat_axis=0, tiled=T...]
    ppermute x0 -> x24, waiting for transfers between devices: none -> 48 us  [take_from(): return lax.ppermute(array, 'seq', pairs)]
    all_gather x1, waiting for transfers between devices: 43.1 us -> 0.02 us  [on_device(): whole = lax.all_gather(hidden, 'tp', axis=1, tiled=True)]
    ppermute x0 -> x24, starting transfers between devices: none -> 32 us  [take_from(): return lax.ppermute(array, 'seq', pairs)]
    pallas_call x0 -> x5, Pallas kernels: none -> 25.3 us  [the longest x2 13.3 us: project(): pl.pallas_call(functools.partial(project_kernel, steps, names, last), out...]
  transfers between devices with their start and end apart: 10 -> 25, of which waited for: 9 -> 9; matrix products, arithmetic and copies ran while one was open for 15% -> 6% of each run, Pallas kernels for 0% -> 4%
where the time goes in v1:
time: 169 us
  waiting for transfers between devices  48.7 us (29%)
  blocking collectives  38.3 us (23%)
  starting transfers between devices  32 us (19%)
  Pallas kernels  25.3 us (15%)
  between operations  13.7 us (8%)
  local copies, waits for them, and re-layouts  9.18 us (5%)
  other arithmetic  2.05 us (1%)
    ppermute x24, waiting for transfers between devices, take_from(): return lax.ppermute(array, 'seq', pairs)  48 us
    ppermute x24, starting transfers between devices, take_from(): return lax.ppermute(array, 'seq', pairs)  32 us
    all_to_all x1, blocking collectives, on_device(): lax.all_to_all(value, 'seq', split_axis=0, concat_axis=0, tiled=True)  20.3 us
    all_to_all x1, blocking collectives, on_device(): lax.all_to_all(conv, 'seq', split_axis=0, concat_axis=0, tiled=True)  18 us
    pallas_call x2, Pallas kernels, project(): pl.pallas_call(functools.partial(project_kernel, steps, names, last), out...  13.3 us
    pallas_call x1, Pallas kernels, strip(): pl.pallas_call(strip_kernel, out_shape=jax.ShapeDtypeStruct((256, 16384),...  4.92 us
    pallas_call x1, Pallas kernels, convolve(): pl.pallas_call(conv_kernel, out_shape=jax.ShapeDtypeStruct((32, 16, 512),...  4.8 us
    unnamed x27, local copies, waits for them, and re-layouts  4.13 us
  transfers between devices with their start and end apart: 25, of which 9 were waited for; matrix products, arithmetic and copies ran while one was open for 6% of the time, Pallas kernels for 4%

profile of v1, /device:TPU:32, one launch (start us, length us, event | category | flops | bytes accessed | tf_op | source)
XLA Modules:
  0.0 169.1 jit_solution(16861886608332988865)
XLA Ops:
  7.3 0.9 slice_bitcast_fusion.3
  8.2 1.7 collective-permute-start.4
  9.8 1.7 collective-permute-start.2
  11.5 0.9 slice.45
  13.1 1.9 %collective-permute-start = (bf16[128,512]{1,0:T(8,128)(2,1)S(1)}, bf16[128,512]{1,0:T(8,128)(2,1)S(1)}, u32[]{:S(2)}, u32[]{:S(2)}) collective-permute-start(bf16[128,512]{1,0:T(8,128)(2,1)S(1)} %pad_maximum_fusion.2), channel_id=1, source_target_pairs={{8,0},{16,8},{24,16},{32,24},{40,32},{48,40},{56,48},{0,56},{72,64... | collective-permute-start | bytes 393224 | tf_op jit(solution)/shard_map/ppermute | solution.py:21
  15.9 2.3 %collective-permute-done = bf16[128,512]{1,0:T(8,128)(2,1)S(1)} collective-permute-done((bf16[128,512]{1,0:T(8,128)(2,1)S(1)}, bf16[128,512]{1,0:T(8,128)(2,1)S(1)}, u32[]{:S(2)}, u32[]{:S(2)}) %collective-permute-start) | collective-permute-done | bytes 131104 | tf_op jit(solution)/shard_map/ppermute | solution.py:21
  18.2 3.5 %collective-permute-start.1 = (bf16[128,512]{1,0:T(8,128)(2,1)S(1)}, bf16[128,512]{1,0:T(8,128)(2,1)S(1)}, u32[]{:S(2)}, u32[]{:S(2)}) collective-permute-start(bf16[128,512]{1,0:T(8,128)(2,1)S(1)} %collective-permute-done), channel_id=1, source_target_pairs={{8,0},{16,8},{24,16},{32,24},{40,32},{48,40},{56,48},{0,56},{72,64... | collective-permute-start | bytes 393224 | tf_op jit(solution)/shard_map/ppermute | solution.py:21
  22.2 2.9 %collective-permute-start.3 = (bf16[72,512]{1,0:T(8,128)(2,1)S(1)}, bf16[72,512]{1,0:T(8,128)(2,1)S(1)}, u32[]{:S(2)}, u32[]{:S(2)}) collective-permute-start(bf16[72,512]{1,0:T(8,128)(2,1)S(1)} %slice.60), channel_id=1, source_target_pairs={{64,0},{72,8},{80,16},{88,24},{96,32},{104,40},{112,48},{120,56},{... | collective-permute-start | bytes 221192 | tf_op jit(solution)/shard_map/ppermute | solution.py:21
  25.8 1.6 collective-permute-done.5
  27.5 3.7 %collective-permute-start.6 = (bf16[128,512]{1,0:T(8,128)(2,1)S(1)}, bf16[128,512]{1,0:T(8,128)(2,1)S(1)}, u32[]{:S(2)}, u32[]{:S(2)}) collective-permute-start(bf16[128,512]{1,0:T(8,128)(2,1)S(1)} %collective-permute-done.1), channel_id=1, source_target_pairs={{8,0},{16,8},{24,16},{32,24},{40,32},{48,40},{56,48},{0,56},{72,64... | collective-permute-start | bytes 393224 | tf_op jit(solution)/shard_map/ppermute | solution.py:21
  31.2 1.2 collective-permute-done.8
  33.7 4.8 %collective-permute-done.9 = bf16[128,512]{1,0:T(8,128)(2,1)S(1)} collective-permute-done((bf16[128,512]{1,0:T(8,128)(2,1)S(1)}, bf16[128,512]{1,0:T(8,128)(2,1)S(1)}, u32[]{:S(2)}, u32[]{:S(2)}) %collective-permute-start.9) | collective-permute-done | bytes 131104 | tf_op jit(solution)/shard_map/ppermute | solution.py:21
  38.6 3.5 %collective-permute-start.16 = (bf16[4,144,512]{2,1,0:T(8,128)(2,1)S(1)}, bf16[4,144,512]{2,1,0:T(8,128)(2,1)}, u32[]{:S(2)}, u32[]{:S(2)}) collective-permute-start(bf16[4,144,512]{2,1,0:T(8,128)(2,1)S(1)} %pad_maximum_fusion.refs_5_.refs_7_), channel_id=1, source_target_pairs={{8,0},{16,8},{24,16},{32,24},{40,32},{48,40},{56,48},{0,56},{72,64... | collective-permute-start | bytes 1769480 | tf_op jit(solution)/shard_map/ppermute | solution.py:21
  42.2 2.0 %collective-permute-start.10 = (bf16[64,512]{1,0:T(8,128)(2,1)S(1)}, bf16[64,512]{1,0:T(8,128)(2,1)S(1)}, u32[]{:S(2)}, u32[]{:S(2)}) collective-permute-start(bf16[64,512]{1,0:T(8,128)(2,1)S(1)} %slice.49), channel_id=1, source_target_pairs={{8,0},{16,8},{24,16},{32,24},{40,32},{48,40},{56,48},{0,56},{72,64... | collective-permute-start | bytes 196616 | tf_op jit(solution)/shard_map/ppermute | solution.py:21
  44.8 9.3 %collective-permute-done.11 = bf16[64,512]{1,0:T(8,128)(2,1)S(1)} collective-permute-done((bf16[64,512]{1,0:T(8,128)(2,1)S(1)}, bf16[64,512]{1,0:T(8,128)(2,1)S(1)}, u32[]{:S(2)}, u32[]{:S(2)}) %collective-permute-start.11) | collective-permute-done | bytes 65568 | tf_op jit(solution)/shard_map/ppermute | solution.py:21
  57.2 1.6 collective-permute-start.13
  58.8 1.8 %collective-permute-start.17 = (bf16[4,144,512]{2,1,0:T(8,128)(2,1)}, bf16[4,144,512]{2,1,0:T(8,128)(2,1)}, u32[]{:S(2)}, u32[]{:S(2)}) collective-permute-start(bf16[4,144,512]{2,1,0:T(8,128)(2,1)} %collective-permute-done.16.refs_6_.refs_8_), channel_id=1, source_target_pairs={{8,0},{16,8},{24,16},{32,24},{40,32},{48,40},{56,48},{0,56},{72,64... | collective-permute-start | bytes 1769480 | tf_op jit(solution)/shard_map/ppermute | solution.py:21
  61.4 18.7 %collective-permute-done.12.refs_3_ = bf16[8,128,512]{2,1,0:T(8,128)(2,1)S(1)} collective-permute-done((bf16[8,128,512]{2,1,0:T(8,128)(2,1)}, bf16[8,128,512]{2,1,0:T(8,128)(2,1)S(1)}, u32[]{:S(2)}, u32[]{:S(2)}) %collective-permute-start.12) | collective-permute-done | bytes 1048608 | tf_op jit(solution)/shard_map/ppermute | solution.py:21
  80.8 1.5 collective-permute-start.15
  82.3 1.9 %collective-permute-start.18 = (bf16[4,144,512]{2,1,0:T(8,128)(2,1)}, bf16[4,144,512]{2,1,0:T(8,128)(2,1)S(1)}, u32[]{:S(2)}, u32[]{:S(2)}) collective-permute-start(bf16[4,144,512]{2,1,0:T(8,128)(2,1)} %collective-permute-done.17.refs_7_.refs_9_), channel_id=1, source_target_pairs={{8,0},{16,8},{24,16},{32,24},{40,32},{48,40},{56,48},{0,56},{72,64... | collective-permute-start | bytes 1769480 | tf_op jit(solution)/shard_map/ppermute | solution.py:21
  84.4 0.9 slice_bitcast_fusion.2
  85.3 5.9 %collective-permute-done.15.refs_6_ = bf16[4,128,512]{2,1,0:T(8,128)(2,1)S(1)} collective-permute-done((bf16[4,128,512]{2,1,0:T(8,128)(2,1)S(1)}, bf16[4,128,512]{2,1,0:T(8,128)(2,1)S(1)}, u32[]{:S(2)}, u32[]{:S(2)}) %collective-permute-start.15) | collective-permute-done | bytes 524320 | tf_op jit(solution)/shard_map/ppermute | solution.py:21
  92.1 3.5 %collective-permute-done.18.refs_8_.refs_10_ = bf16[4,144,512]{2,1,0:T(8,128)(2,1)S(1)} collective-permute-done((bf16[4,144,512]{2,1,0:T(8,128)(2,1)}, bf16[4,144,512]{2,1,0:T(8,128)(2,1)S(1)}, u32[]{:S(2)}, u32[]{:S(2)}) %collective-permute-start.18) | collective-permute-done | bytes 589856 | tf_op jit(solution)/shard_map/ppermute | solution.py:21
  95.6 1.9 %collective-permute-start.22 = (bf16[2,144,512]{2,1,0:T(8,128)(2,1)S(1)}, bf16[2,144,512]{2,1,0:T(8,128)(2,1)}, u32[]{:S(2)}, u32[]{:S(2)}) collective-permute-start(bf16[2,144,512]{2,1,0:T(8,128)(2,1)S(1)} %slice.64), channel_id=1, source_target_pairs={{8,0},{16,8},{24,16},{32,24},{40,32},{48,40},{56,48},{0,56},{72,64... | collective-permute-start | bytes 884744 | tf_op jit(solution)/shard_map/ppermute | solution.py:21
  97.6 0.8 slice.65
  98.6 7.5 %project_early.1.refs_16_ = f32[512,512]{1,0:T(8,128)} custom-call(s32[3]{0:T(128)} %pad_add_fusion.refs_0_.place, bf16[512,8192]{1,0:T(8,128)(2,1)} %all-gather.2.cloned.1.call-done.refs_1_, bf16[8,128,512]{2,1,0:T(8,128)(2,1)} %bitcast_dynamic-update-slice_fusion.refs_2_, bf16[8,128,512]{2,1,0:T(8,128)(2,1)} %copy-done.4, bf16[8,128,512]{2,1,0:T(8,128)(2,1)} %copy-done.5, ...), custom_call_target="tpu_custom_call" | custom-call | flops 2818572288 | bytes 11010048 | tf_op jit(solution)/shard_map/project_early/pallas_call | solution.py:117
  106.2 5.8 %project_last.1 = bf16[32,16,512]{2,1,0:T(8,128)(2,1)} custom-call(s32[3]{0:T(128)} %pad_add_fusion.refs_0_.place, bf16[512,8192]{1,0:T(8,128)(2,1)} %all-gather.2.cloned.1.call-done.refs_1_, bf16[8,128,512]{2,1,0:T(8,128)(2,1)} %bitcast_dynamic-update-slice_fusion.refs_2_, bf16[8,128,512]{2,1,0:T(8,128)(2,1)} %copy-done.4, bf16[8,128,512]{2,1,0:T(8,128)(2,1)} %copy-done.5, ...), custom_call_target="tpu_custom_call" | custom-call | flops 1476395008 | bytes 5767168 | tf_op jit(solution)/shard_map/project_last/pallas_call | solution.py:117
  112.0 4.9 %strip.1.strip_ref = bf16[256,16384]{1,0:T(8,128)(2,1)S(1)} custom-call(s32[3]{0:T(128)S(1)} %copy-done.2, bf16[4,8,16,512]{3,2,1,0:T(8,128)(2,1)S(1)} %pad_maximum_fusion.1.taps), custom_call_target="tpu_custom_call" | custom-call | flops 10485760 | bytes 8388608 | tf_op jit(solution)/shard_map/strip/pallas_call | solution.py:168
  117.0 20.3 %all_to_all.10.value = bf16[32,16,512]{2,1,0:T(8,128)(2,1)S(1)} all-to-all(bf16[32,16,512]{2,1,0:T(8,128)(2,1)S(1)} %copy-done), channel_id=1, replica_groups=mesh['seq'=32,'tp'=8] {'seq'}, dimensions={0} | all-to-all | bytes 1048576 | tf_op jit(solution)/shard_map/all_to_all | solution.py:256
  137.3 4.8 %convolve.1 = bf16[32,16,512]{2,1,0:T(8,128)(2,1)S(1)} custom-call(bf16[32,16,512]{2,1,0:T(8,128)(2,1)S(1)} %all_to_all.10.value, bf16[256,16384]{1,0:T(8,128)(2,1)S(1)} %strip.1.strip_ref), custom_call_target="tpu_custom_call" | custom-call | flops 4499999744 | bytes 10485760 | tf_op jit(solution)/shard_map/convolve/pallas_call | solution.py:205
  142.1 18.0 %all_to_all.11 = bf16[32,16,512]{2,1,0:T(8,128)(2,1)S(1)} all-to-all(bf16[32,16,512]{2,1,0:T(8,128)(2,1)S(1)} %convolve.1), channel_id=1, replica_groups=mesh['seq'=32,'tp'=8] {'seq'}, dimensions={0} | all-to-all | bytes 1048576 | tf_op jit(solution)/shard_map/all_to_all | solution.py:258
  160.1 2.2 %mix.1 = bf16[512,512]{1,0:T(8,128)(2,1)} custom-call(bf16[512,512]{1,0:T(8,128)(2,1)S(1)} %bitcast.39, bf16[512,512]{1,0:T(8,128)(2,1)S(1)} %bitcast.38, f32[1,512]{1,0:T(1,128)S(1)} %bitcast.40, bf16[512,512]{1,0:T(8,128)(2,1)S(1)} %copy-done.1), custom_call_target="tpu_custom_call" | custom-call | tf_op jit(solution)/shard_map/mix/pallas_call | solution.py:229
  (79 shorter events, 11.5 us)
Async XLA Ops:
  6.5 92.1 %all-gather.2.cloned.1.call-start = ((), (), s32[]{:S(2)}) async-start(), calls=%async_computation.2 | async-start | bytes 9437184 | tf_op jit(solution)/shard_map/all_gather | solution.py:248
  8.2 13.5 %collective-permute-start.4 = (bf16[144,512]{1,0:T(8,128)(2,1)S(1)}, bf16[144,512]{1,0:T(8,128)(2,1)S(1)}, u32[]{:S(2)}, u32[]{:S(2)}) collective-permute-start(bf16[144,512]{1,0:T(8,128)(2,1)S(1)} %get-tuple-element.20), channel_id=1, source_target_pairs={{192,0},{200,8},{208,16},{216,24},{224,32},{232,40},{240,48},{248,... | collective-permute-start | bytes 442376 | tf_op jit(solution)/shard_map/ppermute | solution.py:21
  9.8 12.3 %collective-permute-start.2 = (bf16[144,512]{1,0:T(8,128)(2,1)S(1)}, bf16[144,512]{1,0:T(8,128)(2,1)S(1)}, u32[]{:S(2)}, u32[]{:S(2)}) collective-permute-start(bf16[144,512]{1,0:T(8,128)(2,1)S(1)} %get-tuple-element.20), channel_id=1, source_target_pairs={{64,0},{72,8},{80,16},{88,24},{96,32},{104,40},{112,48},{120,56},{... | collective-permute-start | bytes 442376 | tf_op jit(solution)/shard_map/ppermute | solution.py:21
  13.1 5.1 %collective-permute-start = (bf16[128,512]{1,0:T(8,128)(2,1)S(1)}, bf16[128,512]{1,0:T(8,128)(2,1)S(1)}, u32[]{:S(2)}, u32[]{:S(2)}) collective-permute-start(bf16[128,512]{1,0:T(8,128)(2,1)S(1)} %pad_maximum_fusion.2), channel_id=1, source_target_pairs={{8,0},{16,8},{24,16},{32,24},{40,32},{48,40},{56,48},{0,56},{72,64... | collective-permute-start | bytes 393224 | tf_op jit(solution)/shard_map/ppermute | solution.py:21
  15.1 10.7 %collective-permute-start.7 = (bf16[128,512]{1,0:T(8,128)(2,1)S(1)}, bf16[128,512]{1,0:T(8,128)(2,1)S(1)}, u32[]{:S(2)}, u32[]{:S(2)}) collective-permute-start(bf16[128,512]{1,0:T(8,128)(2,1)S(1)} %pad_maximum_fusion.2), channel_id=1, source_target_pairs={{56,0},{0,8},{8,16},{16,24},{24,32},{32,40},{40,48},{48,56},{120,6... | collective-permute-start | bytes 393224 | tf_op jit(solution)/shard_map/ppermute | solution.py:21
  18.2 9.3 %collective-permute-start.1 = (bf16[128,512]{1,0:T(8,128)(2,1)S(1)}, bf16[128,512]{1,0:T(8,128)(2,1)S(1)}, u32[]{:S(2)}, u32[]{:S(2)}) collective-permute-start(bf16[128,512]{1,0:T(8,128)(2,1)S(1)} %collective-permute-done), channel_id=1, source_target_pairs={{8,0},{16,8},{24,16},{32,24},{40,32},{48,40},{56,48},{0,56},{72,64... | collective-permute-start | bytes 393224 | tf_op jit(solution)/shard_map/ppermute | solution.py:21
  21.7 5.6 %collective-permute-start.5 = (bf16[72,512]{1,0:T(8,128)(2,1)S(1)}, bf16[72,512]{1,0:T(8,128)(2,1)S(1)}, u32[]{:S(2)}, u32[]{:S(2)}) collective-permute-start(bf16[72,512]{1,0:T(8,128)(2,1)S(1)} %slice.61), channel_id=1, source_target_pairs={{192,0},{200,8},{208,16},{216,24},{224,32},{232,40},{240,48},{248,... | collective-permute-start | bytes 221192 | tf_op jit(solution)/shard_map/ppermute | solution.py:21
  22.2 5.2 %collective-permute-start.3 = (bf16[72,512]{1,0:T(8,128)(2,1)S(1)}, bf16[72,512]{1,0:T(8,128)(2,1)S(1)}, u32[]{:S(2)}, u32[]{:S(2)}) collective-permute-start(bf16[72,512]{1,0:T(8,128)(2,1)S(1)} %slice.60), channel_id=1, source_target_pairs={{64,0},{72,8},{80,16},{88,24},{96,32},{104,40},{112,48},{120,56},{... | collective-permute-start | bytes 221192 | tf_op jit(solution)/shard_map/ppermute | solution.py:21
  25.8 6.6 %collective-permute-start.8 = (bf16[128,512]{1,0:T(8,128)(2,1)S(1)}, bf16[128,512]{1,0:T(8,128)(2,1)S(1)}, u32[]{:S(2)}, u32[]{:S(2)}) collective-permute-start(bf16[128,512]{1,0:T(8,128)(2,1)S(1)} %collective-permute-done.7), channel_id=1, source_target_pairs={{56,0},{0,8},{8,16},{16,24},{24,32},{32,40},{40,48},{48,56},{120,6... | collective-permute-start | bytes 393224 | tf_op jit(solution)/shard_map/ppermute | solution.py:21
  27.5 71.1 %copy-start.6 = (bf16[4,144,512]{2,1,0:T(8,128)(2,1)}, bf16[4,144,512]{2,1,0:T(8,128)(2,1)S(1)}, u32[]{:S(2)}) copy-start(bf16[4,144,512]{2,1,0:T(8,128)(2,1)S(1)} %pad_maximum_fusion.refs_5_.refs_7_) | copy-start | bytes 1769476
  27.5 6.3 %collective-permute-start.6 = (bf16[128,512]{1,0:T(8,128)(2,1)S(1)}, bf16[128,512]{1,0:T(8,128)(2,1)S(1)}, u32[]{:S(2)}, u32[]{:S(2)}) collective-permute-start(bf16[128,512]{1,0:T(8,128)(2,1)S(1)} %collective-permute-done.1), channel_id=1, source_target_pairs={{8,0},{16,8},{24,16},{32,24},{40,32},{48,40},{56,48},{0,56},{72,64... | collective-permute-start | bytes 393224 | tf_op jit(solution)/shard_map/ppermute | solution.py:21
  32.4 6.2 %collective-permute-start.9 = (bf16[128,512]{1,0:T(8,128)(2,1)S(1)}, bf16[128,512]{1,0:T(8,128)(2,1)S(1)}, u32[]{:S(2)}, u32[]{:S(2)}) collective-permute-start(bf16[128,512]{1,0:T(8,128)(2,1)S(1)} %collective-permute-done.8), channel_id=1, source_target_pairs={{56,0},{0,8},{8,16},{16,24},{24,32},{32,40},{40,48},{48,56},{120,6... | collective-permute-start | bytes 393224 | tf_op jit(solution)/shard_map/ppermute | solution.py:21
  38.6 20.2 %collective-permute-start.16 = (bf16[4,144,512]{2,1,0:T(8,128)(2,1)S(1)}, bf16[4,144,512]{2,1,0:T(8,128)(2,1)}, u32[]{:S(2)}, u32[]{:S(2)}) collective-permute-start(bf16[4,144,512]{2,1,0:T(8,128)(2,1)S(1)} %pad_maximum_fusion.refs_5_.refs_7_), channel_id=1, source_target_pairs={{8,0},{16,8},{24,16},{32,24},{40,32},{48,40},{56,48},{0,56},{72,64... | collective-permute-start | bytes 1769480 | tf_op jit(solution)/shard_map/ppermute | solution.py:21
  42.0 18.5 %collective-permute-start.19 = (bf16[4,144,512]{2,1,0:T(8,128)(2,1)S(1)}, bf16[4,144,512]{2,1,0:T(8,128)(2,1)}, u32[]{:S(2)}, u32[]{:S(2)}) collective-permute-start(bf16[4,144,512]{2,1,0:T(8,128)(2,1)S(1)} %pad_maximum_fusion.refs_5_.refs_7_), channel_id=1, source_target_pairs={{56,0},{0,8},{8,16},{16,24},{24,32},{32,40},{40,48},{48,56},{120,6... | collective-permute-start | bytes 1769480 | tf_op jit(solution)/shard_map/ppermute | solution.py:21
  42.0 12.0 %collective-permute-start.11 = (bf16[64,512]{1,0:T(8,128)(2,1)S(1)}, bf16[64,512]{1,0:T(8,128)(2,1)S(1)}, u32[]{:S(2)}, u32[]{:S(2)}) collective-permute-start(bf16[64,512]{1,0:T(8,128)(2,1)S(1)} %slice.50), channel_id=1, source_target_pairs={{56,0},{0,8},{8,16},{16,24},{24,32},{32,40},{40,48},{48,56},{120,6... | collective-permute-start | bytes 196616 | tf_op jit(solution)/shard_map/ppermute | solution.py:21
  42.2 11.9 %collective-permute-start.10 = (bf16[64,512]{1,0:T(8,128)(2,1)S(1)}, bf16[64,512]{1,0:T(8,128)(2,1)S(1)}, u32[]{:S(2)}, u32[]{:S(2)}) collective-permute-start(bf16[64,512]{1,0:T(8,128)(2,1)S(1)} %slice.49), channel_id=1, source_target_pairs={{8,0},{16,8},{24,16},{32,24},{40,32},{48,40},{56,48},{0,56},{72,64... | collective-permute-start | bytes 196616 | tf_op jit(solution)/shard_map/ppermute | solution.py:21
  56.8 23.3 %collective-permute-start.12 = (bf16[8,128,512]{2,1,0:T(8,128)(2,1)}, bf16[8,128,512]{2,1,0:T(8,128)(2,1)S(1)}, u32[]{:S(2)}, u32[]{:S(2)}) collective-permute-start(bf16[8,128,512]{2,1,0:T(8,128)(2,1)} %bitcast_dynamic-update-slice_fusion.refs_2_), channel_id=1, source_target_pairs={{64,0},{72,8},{80,16},{88,24},{96,32},{104,40},{112,48},{120,56},{... | collective-permute-start | bytes 3145736 | tf_op jit(solution)/shard_map/ppermute | solution.py:21
  57.2 23.5 %collective-permute-start.13 = (bf16[8,128,512]{2,1,0:T(8,128)(2,1)}, bf16[8,128,512]{2,1,0:T(8,128)(2,1)S(1)}, u32[]{:S(2)}, u32[]{:S(2)}) collective-permute-start(bf16[8,128,512]{2,1,0:T(8,128)(2,1)} %bitcast_dynamic-update-slice_fusion.refs_2_), channel_id=1, source_target_pairs={{192,0},{200,8},{208,16},{216,24},{224,32},{232,40},{240,48},{248,... | collective-permute-start | bytes 3145736 | tf_op jit(solution)/shard_map/ppermute | solution.py:21
  58.8 23.6 %collective-permute-start.17 = (bf16[4,144,512]{2,1,0:T(8,128)(2,1)}, bf16[4,144,512]{2,1,0:T(8,128)(2,1)}, u32[]{:S(2)}, u32[]{:S(2)}) collective-permute-start(bf16[4,144,512]{2,1,0:T(8,128)(2,1)} %collective-permute-done.16.refs_6_.refs_8_), channel_id=1, source_target_pairs={{8,0},{16,8},{24,16},{32,24},{40,32},{48,40},{56,48},{0,56},{72,64... | collective-permute-start | bytes 1769480 | tf_op jit(solution)/shard_map/ppermute | solution.py:21
  60.5 23.7 %collective-permute-start.20 = (bf16[4,144,512]{2,1,0:T(8,128)(2,1)}, bf16[4,144,512]{2,1,0:T(8,128)(2,1)}, u32[]{:S(2)}, u32[]{:S(2)}) collective-permute-start(bf16[4,144,512]{2,1,0:T(8,128)(2,1)} %collective-permute-done.19.refs_11_.refs_13_), channel_id=1, source_target_pairs={{56,0},{0,8},{8,16},{16,24},{24,32},{32,40},{40,48},{48,56},{120,6... | collective-permute-start | bytes 1769480 | tf_op jit(solution)/shard_map/ppermute | solution.py:21
  80.1 18.5 %copy-start.4 = (bf16[8,128,512]{2,1,0:T(8,128)(2,1)}, bf16[8,128,512]{2,1,0:T(8,128)(2,1)S(1)}, u32[]{:S(2)}) copy-start(bf16[8,128,512]{2,1,0:T(8,128)(2,1)S(1)} %collective-permute-done.12.refs_3_) | copy-start | bytes 3145732
  80.1 11.2 %collective-permute-start.14 = (bf16[4,128,512]{2,1,0:T(8,128)(2,1)S(1)}, bf16[4,128,512]{2,1,0:T(8,128)(2,1)S(1)}, u32[]{:S(2)}, u32[]{:S(2)}) collective-permute-start(bf16[4,128,512]{2,1,0:T(8,128)(2,1)S(1)} %slice.62), channel_id=1, source_target_pairs={{64,0},{72,8},{80,16},{88,24},{96,32},{104,40},{112,48},{120,56},{... | collective-permute-start | bytes 1572872 | tf_op jit(solution)/shard_map/ppermute | solution.py:21
  80.7 17.9 %copy-start.5 = (bf16[8,128,512]{2,1,0:T(8,128)(2,1)}, bf16[8,128,512]{2,1,0:T(8,128)(2,1)S(1)}, u32[]{:S(2)}) copy-start(bf16[8,128,512]{2,1,0:T(8,128)(2,1)S(1)} %collective-permute-done.13.refs_4_) | copy-start | bytes 3145732
  80.8 10.5 %collective-permute-start.15 = (bf16[4,128,512]{2,1,0:T(8,128)(2,1)S(1)}, bf16[4,128,512]{2,1,0:T(8,128)(2,1)S(1)}, u32[]{:S(2)}, u32[]{:S(2)}) collective-permute-start(bf16[4,128,512]{2,1,0:T(8,128)(2,1)S(1)} %slice.63), channel_id=1, source_target_pairs={{192,0},{200,8},{208,16},{216,24},{224,32},{232,40},{240,48},{248,... | collective-permute-start | bytes 1572872 | tf_op jit(solution)/shard_map/ppermute | solution.py:21
  82.3 13.3 %collective-permute-start.18 = (bf16[4,144,512]{2,1,0:T(8,128)(2,1)}, bf16[4,144,512]{2,1,0:T(8,128)(2,1)S(1)}, u32[]{:S(2)}, u32[]{:S(2)}) collective-permute-start(bf16[4,144,512]{2,1,0:T(8,128)(2,1)} %collective-permute-done.17.refs_7_.refs_9_), channel_id=1, source_target_pairs={{8,0},{16,8},{24,16},{32,24},{40,32},{48,40},{56,48},{0,56},{72,64... | collective-permute-start | bytes 1769480 | tf_op jit(solution)/shard_map/ppermute | solution.py:21
  84.2 13.4 %collective-permute-start.21 = (bf16[4,144,512]{2,1,0:T(8,128)(2,1)}, bf16[4,144,512]{2,1,0:T(8,128)(2,1)S(1)}, u32[]{:S(2)}, u32[]{:S(2)}) collective-permute-start(bf16[4,144,512]{2,1,0:T(8,128)(2,1)} %collective-permute-done.20.refs_10_.refs_12_), channel_id=1, source_target_pairs={{56,0},{0,8},{8,16},{16,24},{24,32},{32,40},{40,48},{48,56},{120,6... | collective-permute-start | bytes 1769480 | tf_op jit(solution)/shard_map/ppermute | solution.py:21
  91.3 7.2 %copy-start.9 = (bf16[4,128,512]{2,1,0:T(8,128)(2,1)}, bf16[4,128,512]{2,1,0:T(8,128)(2,1)S(1)}, u32[]{:S(2)}) copy-start(bf16[4,128,512]{2,1,0:T(8,128)(2,1)S(1)} %collective-permute-done.14.refs_5_) | copy-start | bytes 1572868
  95.6 10.6 %collective-permute-start.22 = (bf16[2,144,512]{2,1,0:T(8,128)(2,1)S(1)}, bf16[2,144,512]{2,1,0:T(8,128)(2,1)}, u32[]{:S(2)}, u32[]{:S(2)}) collective-permute-start(bf16[2,144,512]{2,1,0:T(8,128)(2,1)S(1)} %slice.64), channel_id=1, source_target_pairs={{8,0},{16,8},{24,16},{32,24},{40,32},{48,40},{56,48},{0,56},{72,64... | collective-permute-start | bytes 884744 | tf_op jit(solution)/shard_map/ppermute | solution.py:21
  98.3 7.9 %collective-permute-start.23 = (bf16[2,144,512]{2,1,0:T(8,128)(2,1)}, bf16[2,144,512]{2,1,0:T(8,128)(2,1)}, u32[]{:S(2)}, u32[]{:S(2)}) collective-permute-start(bf16[2,144,512]{2,1,0:T(8,128)(2,1)} %slice.65), channel_id=1, source_target_pairs={{56,0},{0,8},{8,16},{16,24},{24,32},{32,40},{40,48},{48,56},{120,6... | collective-permute-start | bytes 884744 | tf_op jit(solution)/shard_map/ppermute | solution.py:21
  106.2 5.8 %copy-start.2 = (s32[3]{0:T(128)S(1)}, s32[3]{0:T(128)}, u32[]{:S(2)}) copy-start(s32[3]{0:T(128)} %pad_add_fusion.refs_0_.place) | copy-start | bytes 40
  137.3 22.8 %copy-start.1 = (bf16[512,512]{1,0:T(8,128)(2,1)S(1)}, bf16[512,512]{1,0:T(8,128)(2,1)}, u32[]{:S(2)}) copy-start(bf16[512,512]{1,0:T(8,128)(2,1)} %gate.1) | copy-start | bytes 1572868
  137.3 22.8 %copy-start.3 = (f32[512]{0:T(512)S(1)}, f32[512]{0:T(512)}, u32[]{:S(2)}) copy-start(f32[512]{0:T(512)} %param.9) | copy-start | bytes 6148
  (4 other events, 9.4 us)
Sparse Core Ops, SparseCore 0:
  9.2 54.8 all-gather.1

commit v2 on v1

v2 whole, which is shorter than its diff:
```python
import functools

import jax
import jax.numpy as jnp
from jax import lax
from jax.experimental import pallas as pl
from jax.experimental.pallas import tpu as pltpu
from jax.sharding import PartitionSpec as P

NY, NZ = 4, 8
FIRST = 128
TAP_ROWS = 16
VMEM_LIMIT = 16 * 1024 * 1024


def take_from(array, dy, dz):
    pairs = [
        (((y + dy) % NY) * NZ + (z + dz) % NZ, y * NZ + z) for y in range(NY) for z in range(NZ)
    ]
    return lax.ppermute(array, "seq", pairs)


def project_kernel(parts, first, last, place, hidden, *refs):
    refs = list(refs)
    out = refs.pop()
    total = jnp.zeros((512, 512), jnp.float32) if first else refs.pop()[...]
    y, z = place[0], place[1]
    pieces = []
    for ref, part in zip(refs, parts, strict=True):
        for at, (dy, dz, second) in enumerate(part):
            block = lax.rem(y + dy, NY) * NZ + lax.rem(z + dz, NZ)
            start = pl.multiple_of(block * 256 + FIRST * second, FIRST)
            pieces.append((start, ref, at))
    for n in range(0, len(pieces), 8):
        group = pieces[n : n + 8]
        left = [hidden[:, pl.ds(start, FIRST)] for start, _, _ in group]
        right = [ref[at, 0:FIRST, :] for _, ref, at in group]
        total += jnp.dot(
            jnp.concatenate(left, axis=1),
            jnp.concatenate(right, axis=0),
            preferred_element_type=jnp.float32,
        )
    out[...] = total.T.reshape(32, 16, 512).astype(jnp.bfloat16) if last else total


def project(place, hidden, held, before=None, last=False):
    arrays = [array for array, _ in held]
    parts = [part for _, part in held]
    count = sum(len(part) for part in parts)
    shape = (
        jax.ShapeDtypeStruct((32, 16, 512), jnp.bfloat16)
        if last
        else jax.ShapeDtypeStruct((512, 512), jnp.float32)
    )
    vmem = pl.BlockSpec(memory_space=pltpu.VMEM)
    extra = [] if before is None else [before]
    return pl.pallas_call(
        functools.partial(project_kernel, parts, before is None, last),
        out_shape=shape,
        in_specs=[pl.BlockSpec(memory_space=pltpu.SMEM)] + [vmem] * (1 + len(arrays) + len(extra)),
        out_specs=vmem,
        compiler_params=pltpu.CompilerParams(vmem_limit_bytes=VMEM_LIMIT),
        cost_estimate=pl.CostEstimate(
            flops=2 * 512 * 512 * FIRST * count,
            bytes_accessed=count * 256 * 1024,
            transcendentals=0,
        ),
        name=f"project_{count}",
    )(place, hidden, *arrays, *extra)


def halves(one, other, dy, dz):
    half = one.shape[0] // 2
    return take_from(one[:half], dy, dz), take_from(other[half:], -dy, -dz)


def gather_and_project(place, hidden, weight, filters):
    taps = jnp.tile(filters.T, (TAP_ROWS // filters.shape[1], 1))
    first = jnp.concatenate([weight[:FIRST], taps], axis=0)
    second = weight[FIRST:]
    line = {0: first, 1: take_from(first, 0, 1), -1: take_from(first, 0, -1)}
    column = jnp.stack([second, *(take_from(second, k, 0) for k in (1, 2, 3))])
    line[2], line[-2] = take_from(line[1], 0, 1), take_from(line[-1], 0, -1)
    line[2], line[-2], column = lax.optimization_barrier((line[2], line[-2], column))
    line[3], line[-3] = take_from(line[2], 0, 1), take_from(line[-2], 0, -1)
    ring = {0: column, 1: take_from(column, 0, 1), -1: take_from(column, 0, -1)}
    line[3], line[-3], ring[1], ring[-1] = lax.optimization_barrier(
        (line[3], line[-3], ring[1], ring[-1])
    )
    line[4] = jnp.concatenate(halves(line[3], line[-3], 0, 1), axis=0)
    mine = jnp.stack([line[k] for k in (0, 1, 2, 3, 4, -3, -2, -1)])
    above, below = take_from(mine, 1, 0), take_from(mine, -1, 0)

    def row(dy, start=0, stop=NZ):
        return [(dy, dz, 0) for dz in range(start, stop)]

    def stack(dz, start=0, stop=NY):
        return [(dy, dz % NZ, 1) for dy in range(start, stop)]

    ring[2], ring[-2] = take_from(ring[1], 0, 1), take_from(ring[-1], 0, -1)
    held = [(mine, row(0))] + [(ring[k], stack(k)) for k in (0, 1, -1)]
    total = project(place, hidden, held)
    total, ring[2], ring[-2] = lax.optimization_barrier((total, ring[2], ring[-2]))
    ring[3], ring[-3] = take_from(ring[2], 0, 1), take_from(ring[-2], 0, -1)
    total = project(place, hidden, [(ring[k], stack(k)) for k in (2, -2)], total)
    total, above, below = lax.optimization_barrier((total, above, below))
    across = halves(above, below, 1, 0)
    total = project(place, hidden, [(above, row(1)), (below, row(3))], total)
    total, ring[3], ring[-3] = lax.optimization_barrier((total, ring[3], ring[-3]))
    ends = halves(ring[3], ring[-3], 0, 1)
    total = project(place, hidden, [(ring[k], stack(k)) for k in (3, -3)], total)
    held = [(across[0], row(2, 0, 4)), (across[1], row(2, 4, 8))]
    held += [(ends[0], stack(4, 0, 2)), (ends[1], stack(4, 2, 4))]
    value = project(place, hidden, held, total, last=True)
    across = jnp.concatenate([part[:, FIRST:] for part in across], axis=0)
    taps = jnp.stack([mine[:, FIRST:], above[:, FIRST:], across, below[:, FIRST:]])
    return value, taps


def strip_kernel(place, taps, out):
    rows, step = 256, 512
    y, z, which = place[0], place[1], place[2]
    pick = lax.broadcasted_iota(jnp.int32, (TAP_ROWS, step), 0) == which

    def chunk(i, before):
        dy = lax.rem(lax.div(i, NZ) - y + NY, NY)
        dz = lax.rem(lax.rem(i, NZ) - z + NZ, NZ)
        held = taps[dy, dz].astype(jnp.float32)
        block = jnp.sum(jnp.where(pick, held, 0.0), axis=0, keepdims=True)
        window = jnp.concatenate([before, block], axis=1)
        window = jnp.broadcast_to(window, (rows, step + rows))
        rolled = pltpu.roll(window, 0, 1, stride=1, stride_axis=0)
        out[:, pl.ds(pl.multiple_of(i * step, step), step)] = rolled[:, rows:].astype(jnp.bfloat16)
        return block[:, step - rows :]

    lax.fori_loop(0, out.shape[1] // step, chunk, jnp.zeros((1, rows), jnp.float32))


def strip(place, taps):
    vmem = pl.BlockSpec(memory_space=pltpu.VMEM)
    return pl.pallas_call(
        strip_kernel,
        out_shape=jax.ShapeDtypeStruct((256, 16384), jnp.bfloat16),
        in_specs=[pl.BlockSpec(memory_space=pltpu.SMEM), vmem],
        out_specs=vmem,
        compiler_params=pltpu.CompilerParams(vmem_limit_bytes=VMEM_LIMIT),
        cost_estimate=pl.CostEstimate(flops=10 << 20, bytes_accessed=8 << 20, transcendentals=0),
        name="strip",
    )(place, taps)


def conv_kernel(value, strip_ref, out, stacked, total):
    for e in range(4):
        for b in range(64):
            rows = slice(16 * b, 16 * b + 16)
            cols = slice(256 * e, 256 * e + 256)
            if b - e < 0:
                stacked[rows, cols] = jnp.zeros((16, 256), jnp.bfloat16)
            else:
                j, m = divmod(b - e, 2)
                stacked[rows, cols] = value[j, :, 256 * m : 256 * m + 256]
    for g in range(16):
        taps = jnp.concatenate(
            [strip_ref[:, 256 * (4 * g + e) : 256 * (4 * g + e + 1)] for e in range(4)], axis=0
        )
        term = jnp.dot(stacked[: 1024 - 64 * g], taps, preferred_element_type=jnp.float32)
        if g == 0:
            total[...] = term
        else:
            total[64 * g :] += term
    for b in range(64):
        j, m = divmod(b, 2)
        out[j, :, 256 * m : 256 * m + 256] = total[16 * b : 16 * b + 16].astype(jnp.bfloat16)


def convolve(value, taps_strip):
    vmem = pl.BlockSpec(memory_space=pltpu.VMEM)
    return pl.pallas_call(
        conv_kernel,
        out_shape=jax.ShapeDtypeStruct((32, 16, 512), jnp.bfloat16),
        in_specs=[vmem, vmem],
        out_specs=vmem,
        scratch_shapes=[
            pltpu.VMEM((1024, 1024), jnp.bfloat16),
            pltpu.VMEM((1024, 256), jnp.float32),
        ],
        compiler_params=pltpu.CompilerParams(vmem_limit_bytes=VMEM_LIMIT),
        cost_estimate=pl.CostEstimate(
            flops=4_500_000_000, bytes_accessed=10 << 20, transcendentals=0
        ),
        name="convolve",
    )(value, taps_strip)


def mix_kernel(conv, value, gain, gate, out):
    column = jnp.transpose(jnp.broadcast_to(gain[...], (8, gain.shape[1])))[:, :1]
    total = conv[...].astype(jnp.float32) + column * value[...].astype(jnp.float32)
    out[...] = (gate[...].astype(jnp.float32) * total.T).astype(jnp.bfloat16)


def mix(conv, value, gain, gate):
    return pl.pallas_call(
        mix_kernel,
        out_shape=jax.ShapeDtypeStruct((512, 512), jnp.bfloat16),
        grid=(4,),
        in_specs=[
            pl.BlockSpec((128, 512), lambda i: (i, 0)),
            pl.BlockSpec((128, 512), lambda i: (i, 0)),
            pl.BlockSpec((1, 128), lambda i: (0, i)),
            pl.BlockSpec((512, 128), lambda i: (0, i)),
        ],
        out_specs=pl.BlockSpec((512, 128), lambda i: (0, i)),
        compiler_params=pltpu.CompilerParams(vmem_limit_bytes=VMEM_LIMIT),
        name="mix",
    )(conv, value, gain, gate)


def on_device(hidden, value_weight, gate, filters, skip_gain):
    index = lax.axis_index("seq")
    place = jnp.stack([index // NZ, index % NZ, index // 8]).astype(jnp.int32)
    whole = lax.all_gather(hidden, "tp", axis=1, tiled=True)
    value, taps = gather_and_project(place, whole, value_weight, filters)
    taps_strip = strip(place, taps)
    value, taps_strip = lax.optimization_barrier((value, taps_strip))
    moved = lax.all_to_all(value, "seq", split_axis=0, concat_axis=0, tiled=True)
    conv = convolve(moved, taps_strip)
    arrived = lax.all_to_all(conv, "seq", split_axis=0, concat_axis=0, tiled=True)
    return mix(arrived.reshape(512, 512), value.reshape(512, 512), skip_gain[None], gate)


def solution(mesh):
    in_specs = (P("seq", "tp"), P("seq", "tp"), P("seq", "tp"), P("seq", "tp"), P("tp"))
    out_specs = P("seq", "tp")
    return jax.shard_map(
        on_device, mesh=mesh, in_specs=in_specs, out_specs=out_specs, check_vma=False
    )
```

time: 169 us -> 158 us (0.935)
  waiting for transfers between devices: 48.7 us -> 31.7 us
  blocking collectives: 38.3 us -> 45.7 us
  Pallas kernels: 25.3 us -> 21.6 us
  starting transfers between devices: 32 us -> 34.6 us
    ppermute x24 -> x23, waiting for transfers between devices: 48 us -> 22.9 us  [take_from(): return lax.ppermute(array, 'seq', pairs)]
    all_gather x1, waiting for transfers between devices: 0.02 us -> 8.12 us  [on_device(): whole = lax.all_gather(hidden, 'tp', axis=1, tiled=True)]
    all_to_all x1, blocking collectives: 20.3 us -> 25.3 us  [on_device(): lax.all_to_all(value, 'seq', split_axis=0, concat_axis=0, tiled=True)]
    pallas_call x2 -> x5, Pallas kernels: 13.3 us -> 9.52 us  [project(): pl.pallas_call(functools.partial(project_kernel, parts, before is None, l...]
    unnamed x27 -> x17, local copies, waits for them, and re-layouts: 4.13 us -> 6.77 us
    ppermute x24 -> x23, starting transfers between devices: 32 us -> 34.6 us  [take_from(): return lax.ppermute(array, 'seq', pairs)]
    all_to_all x1, blocking collectives: 18 us -> 20.4 us  [on_device(): lax.all_to_all(conv, 'seq', split_axis=0, concat_axis=0, tiled=True)]
  transfers between devices with their start and end apart: 25 -> 24, of which waited for: 9 -> 13; matrix products, arithmetic and copies ran while one was open for 6% -> 5% of each run, Pallas kernels for 4% -> 8%
where the time goes in v2:
time: 158 us
  blocking collectives  45.7 us (29%)
  starting transfers between devices  34.6 us (22%)
  waiting for transfers between devices  31.7 us (20%)
  Pallas kernels  21.6 us (14%)
  between operations  13.6 us (9%)
  local copies, waits for them, and re-layouts  9.25 us (6%)
  other arithmetic  1.59 us (1%)
    ppermute x23, starting transfers between devices, take_from(): return lax.ppermute(array, 'seq', pairs)  34.6 us
    all_to_all x1, blocking collectives, on_device(): lax.all_to_all(value, 'seq', split_axis=0, concat_axis=0, tiled=True)  25.3 us
    ppermute x23, waiting for transfers between devices, take_from(): return lax.ppermute(array, 'seq', pairs)  22.9 us
    all_to_all x1, blocking collectives, on_device(): lax.all_to_all(conv, 'seq', split_axis=0, concat_axis=0, tiled=True)  20.4 us
    pallas_call x5, Pallas kernels, project(): pl.pallas_call(functools.partial(project_kernel, parts, before is None, l...  9.52 us
    all_gather x1, waiting for transfers between devices, on_device(): whole = lax.all_gather(hidden, 'tp', axis=1, tiled=True)  8.12 us
    unnamed x17, local copies, waits for them, and re-layouts  6.77 us
    pallas_call x1, Pallas kernels, strip(): pl.pallas_call(strip_kernel, out_shape=jax.ShapeDtypeStruct((256, 16384),...  4.92 us
  transfers between devices with their start and end apart: 24, of which 13 were waited for; matrix products, arithmetic and copies ran while one was open for 5% of the time, Pallas kernels for 8%

profile of v2, /device:TPU:32, one launch (start us, length us, event | category | flops | bytes accessed | tf_op | source)
XLA Modules:
  0.0 158.1 jit_solution(2509903972470184654)
XLA Ops:
  8.0 1.9 %collective-permute-start = (bf16[144,512]{1,0:T(8,128)(2,1)S(1)}, bf16[144,512]{1,0:T(8,128)(2,1)S(1)}, u32[]{:S(2)}, u32[]{:S(2)}) collective-permute-start(bf16[144,512]{1,0:T(8,128)(2,1)S(1)} %pad_maximum_fusion.2), channel_id=1, source_target_pairs={{8,0},{16,8},{24,16},{32,24},{40,32},{48,40},{56,48},{0,56},{72,64... | collective-permute-start | bytes 442376 | tf_op jit(solution)/shard_map/ppermute | solution.py:20
  10.1 3.2 %collective-permute-start.5 = (bf16[128,512]{1,0:T(8,128)(2,1)S(1)}, bf16[128,512]{1,0:T(8,128)(2,1)S(1)}, u32[]{:S(2)}, u32[]{:S(2)}) collective-permute-start(bf16[128,512]{1,0:T(8,128)(2,1)S(1)} %get-tuple-element.42), channel_id=1, source_target_pairs={{128,0},{136,8},{144,16},{152,24},{160,32},{168,40},{176,48},{184,... | collective-permute-start | bytes 393224 | tf_op jit(solution)/shard_map/ppermute | solution.py:20
  15.4 3.9 %collective-permute-start.1 = (bf16[144,512]{1,0:T(8,128)(2,1)S(1)}, bf16[144,512]{1,0:T(8,128)(2,1)S(1)}, u32[]{:S(2)}, u32[]{:S(2)}) collective-permute-start(bf16[144,512]{1,0:T(8,128)(2,1)S(1)} %collective-permute-done), channel_id=1, source_target_pairs={{8,0},{16,8},{24,16},{32,24},{40,32},{48,40},{56,48},{0,56},{72,64... | collective-permute-start | bytes 442376 | tf_op jit(solution)/shard_map/ppermute | solution.py:20
  20.6 1.3 collective-permute-done.1
  22.0 3.7 %collective-permute-done.3 = bf16[144,512]{1,0:T(8,128)(2,1)S(1)} collective-permute-done((bf16[144,512]{1,0:T(8,128)(2,1)S(1)}, bf16[144,512]{1,0:T(8,128)(2,1)S(1)}, u32[]{:S(2)}, u32[]{:S(2)}) %collective-permute-start.3) | collective-permute-done | bytes 147488 | tf_op jit(solution)/shard_map/ppermute | solution.py:20
  25.7 3.2 %collective-permute-start.9 = (bf16[4,128,512]{2,1,0:T(8,128)(2,1)S(1)}, bf16[4,128,512]{2,1,0:T(8,128)(2,1)}, u32[]{:S(2)}, u32[]{:S(2)}) collective-permute-start(bf16[4,128,512]{2,1,0:T(8,128)(2,1)S(1)} %pad_maximum_fusion.refs_1_), channel_id=1, source_target_pairs={{8,0},{16,8},{24,16},{32,24},{40,32},{48,40},{56,48},{0,56},{72,64... | collective-permute-start | bytes 1572872 | tf_op jit(solution)/shard_map/ppermute | solution.py:20
  30.2 3.2 %collective-permute-start.7 = (bf16[144,512]{1,0:T(8,128)(2,1)S(1)}, bf16[144,512]{1,0:T(8,128)(2,1)S(1)}, u32[]{:S(2)}, u32[]{:S(2)}) collective-permute-start(bf16[144,512]{1,0:T(8,128)(2,1)S(1)} %collective-permute-done.1), channel_id=1, source_target_pairs={{8,0},{16,8},{24,16},{32,24},{40,32},{48,40},{56,48},{0,56},{72,64... | collective-permute-start | bytes 442376 | tf_op jit(solution)/shard_map/ppermute | solution.py:20
  34.2 6.2 %collective-permute-done.7 = bf16[144,512]{1,0:T(8,128)(2,1)S(1)} collective-permute-done((bf16[144,512]{1,0:T(8,128)(2,1)S(1)}, bf16[144,512]{1,0:T(8,128)(2,1)S(1)}, u32[]{:S(2)}, u32[]{:S(2)}) %collective-permute-start.7) | collective-permute-done | bytes 147488 | tf_op jit(solution)/shard_map/ppermute | solution.py:20
  41.2 1.5 collective-permute-start.12
  42.6 1.6 %collective-permute-start.11 = (bf16[72,512]{1,0:T(8,128)(2,1)S(1)}, bf16[72,512]{1,0:T(8,128)(2,1)S(1)}, u32[]{:S(2)}, u32[]{:S(2)}) collective-permute-start(bf16[72,512]{1,0:T(8,128)(2,1)S(1)} %slice.41), channel_id=1, source_target_pairs={{8,0},{16,8},{24,16},{32,24},{40,32},{48,40},{56,48},{0,56},{72,64... | collective-permute-start | bytes 221192 | tf_op jit(solution)/shard_map/ppermute | solution.py:20
  45.0 1.6 collective-permute-done.12
  46.5 1.4 collective-permute-done.11
  51.0 2.9 %collective-permute-start.15 = (bf16[8,144,512]{2,1,0:T(8,128)(2,1)}, bf16[8,144,512]{2,1,0:T(8,128)(2,1)S(1)}, u32[]{:S(2)}, u32[]{:S(2)}) collective-permute-start(bf16[8,144,512]{2,1,0:T(8,128)(2,1)} %bitcast_dynamic-update-slice_fusion.refs_0_), channel_id=1, source_target_pairs={{64,0},{72,8},{80,16},{88,24},{96,32},{104,40},{112,48},{120,56},{... | collective-permute-start | bytes 3538952 | tf_op jit(solution)/shard_map/ppermute | solution.py:20
  53.9 1.8 %collective-permute-start.13 = (bf16[4,128,512]{2,1,0:T(8,128)(2,1)}, bf16[4,128,512]{2,1,0:T(8,128)(2,1)}, u32[]{:S(2)}, u32[]{:S(2)}) collective-permute-start(bf16[4,128,512]{2,1,0:T(8,128)(2,1)} %collective-permute-done.9.refs_2_), channel_id=1, source_target_pairs={{8,0},{16,8},{24,16},{32,24},{40,32},{48,40},{56,48},{0,56},{72,64... | collective-permute-start | bytes 1572872 | tf_op jit(solution)/shard_map/ppermute | solution.py:20
  56.0 8.1 %all-gather.2.cloned.1.call-done.hidden = bf16[512,8192]{1,0:T(8,128)(2,1)} async-done(((bf16[512,1024]{1,0:T(8,128)(2,1)}), bf16[512,8192]{1,0:T(8,128)(2,1)}) %all-gather.2.cloned.1.call-update) | async-done | bytes 8388624 | tf_op jit(solution)/shard_map/all_gather | solution.py:221
  64.1 3.4 %copy-done = bf16[512,8192]{1,0:T(8,128)(2,1)S(1)} copy-done((bf16[512,8192]{1,0:T(8,128)(2,1)S(1)}, bf16[512,8192]{1,0:T(8,128)(2,1)}, u32[]{:S(2)}) %copy-start) | copy-done | bytes 8388632
  67.5 2.9 %project_20.1.refs_2_ = f32[512,512]{1,0:T(8,128)S(1)} custom-call(s32[3]{0:T(128)S(1)} %pad_add_fusion.place, bf16[512,8192]{1,0:T(8,128)(2,1)S(1)} %copy-done, bf16[8,144,512]{2,1,0:T(8,128)(2,1)} %bitcast_dynamic-update-slice_fusion.refs_0_, bf16[4,128,512]{2,1,0:T(8,128)(2,1)S(1)} %pad_maximum_fusion.refs_1_, ...), custom_call_target="tpu_custom_call" | custom-call | flops 1342177280 | bytes 5242880 | tf_op jit(solution)/shard_map/project_20/pallas_call | solution.py:57
  71.0 1.6 collective-permute-start.20
  72.5 1.9 %project_8.2.refs_2_ = f32[512,512]{1,0:T(8,128)S(1)} custom-call(s32[3]{0:T(128)S(1)} %pad_add_fusion.place, bf16[512,8192]{1,0:T(8,128)(2,1)S(1)} %copy-done, bf16[4,128,512]{2,1,0:T(8,128)(2,1)} %collective-permute-done.13.refs_0_, bf16[4,128,512]{2,1,0:T(8,128)(2,1)} %collective-permute-done.14.refs_1_, f32[512,512]{1,0:T(8,128)S(1)} %project_20.1.refs_2_), custom_call_target="tpu_custom_call" | custom-call | flops 536870912 | bytes 2097152 | tf_op jit(solution)/shard_map/project_8/pallas_call | solution.py:57
  74.5 1.2 collective-permute-done.16.refs_1_
  76.3 2.7 %collective-permute-start.17 = (bf16[4,144,512]{2,1,0:T(8,128)(2,1)S(1)}, bf16[4,144,512]{2,1,0:T(8,128)(2,1)S(1)}, u32[]{:S(2)}, u32[]{:S(2)}) collective-permute-start(bf16[4,144,512]{2,1,0:T(8,128)(2,1)S(1)} %slice.43), channel_id=1, source_target_pairs={{64,0},{72,8},{80,16},{88,24},{96,32},{104,40},{112,48},{120,56},{... | collective-permute-start | bytes 1769480 | tf_op jit(solution)/shard_map/ppermute | solution.py:20
  80.0 1.8 %project_16.1.refs_2_ = f32[512,512]{1,0:T(8,128)S(1)} custom-call(s32[3]{0:T(128)S(1)} %pad_add_fusion.place, bf16[512,8192]{1,0:T(8,128)(2,1)S(1)} %copy-done, bf16[8,144,512]{2,1,0:T(8,128)(2,1)S(1)} %collective-permute-done.15.refs_0_, bf16[8,144,512]{2,1,0:T(8,128)(2,1)S(1)} %collective-permute-done.16.refs_1_, f32[512,512]{1,0:T(8,128)S(1)} %project_8.2.refs_2_), custom_call_target="tpu_custom_call" | custom-call | flops 1073741824 | bytes 4194304 | tf_op jit(solution)/shard_map/project_16/pallas_call | solution.py:57
  81.8 3.0 %collective-permute-done.19.refs_0_ = bf16[4,128,512]{2,1,0:T(8,128)(2,1)S(1)} collective-permute-done((bf16[4,128,512]{2,1,0:T(8,128)(2,1)}, bf16[4,128,512]{2,1,0:T(8,128)(2,1)S(1)}, u32[]{:S(2)}, u32[]{:S(2)}) %collective-permute-start.19) | collective-permute-done | bytes 524320 | tf_op jit(solution)/shard_map/ppermute | solution.py:20
  84.8 1.8 %collective-permute-done.20.refs_1_ = bf16[4,128,512]{2,1,0:T(8,128)(2,1)S(1)} collective-permute-done((bf16[4,128,512]{2,1,0:T(8,128)(2,1)}, bf16[4,128,512]{2,1,0:T(8,128)(2,1)S(1)}, u32[]{:S(2)}, u32[]{:S(2)}) %collective-permute-start.20) | collective-permute-done | bytes 524320 | tf_op jit(solution)/shard_map/ppermute | solution.py:20
  86.6 3.0 %collective-permute-start.21 = (bf16[2,128,512]{2,1,0:T(8,128)(2,1)S(1)}, bf16[2,128,512]{2,1,0:T(8,128)(2,1)S(1)}, u32[]{:S(2)}, u32[]{:S(2)}) collective-permute-start(bf16[2,128,512]{2,1,0:T(8,128)(2,1)S(1)} %slice.45), channel_id=1, source_target_pairs={{8,0},{16,8},{24,16},{32,24},{40,32},{48,40},{56,48},{0,56},{72,64... | collective-permute-start | bytes 786440 | tf_op jit(solution)/shard_map/ppermute | solution.py:20
  89.7 1.3 project_8.3.refs_4_
  91.1 4.9 %strip.1.strip_ref = bf16[256,16384]{1,0:T(8,128)(2,1)S(1)} custom-call(s32[3]{0:T(128)S(1)} %pad_add_fusion.place, bf16[4,8,16,512]{3,2,1,0:T(8,128)(2,1)S(1)} %pad_maximum_fusion.1.taps), custom_call_target="tpu_custom_call" | custom-call | flops 10485760 | bytes 8388608 | tf_op jit(solution)/shard_map/strip/pallas_call | solution.py:141
  96.7 1.6 %project_12.1 = bf16[32,16,512]{2,1,0:T(8,128)(2,1)S(1)} custom-call(s32[3]{0:T(128)S(1)} %pad_add_fusion.place, bf16[512,8192]{1,0:T(8,128)(2,1)S(1)} %bitcast.38, bf16[4,144,512]{2,1,0:T(8,128)(2,1)S(1)} %collective-permute-done.17.refs_0_, bf16[4,144,512]{2,1,0:T(8,128)(2,1)S(1)} %collective-permute-done.18.refs_1_, ...), custom_call_target="tpu_custom_call" | custom-call | flops 805306368 | bytes 3145728 | tf_op jit(solution)/shard_map/project_12/pallas_call | solution.py:57
  98.3 25.3 %all_to_all.10.value = bf16[32,16,512]{2,1,0:T(8,128)(2,1)S(1)} all-to-all(bf16[32,16,512]{2,1,0:T(8,128)(2,1)S(1)} %project_12.1), channel_id=1, replica_groups=mesh['seq'=32,'tp'=8] {'seq'}, dimensions={0} | all-to-all | bytes 1048576 | tf_op jit(solution)/shard_map/all_to_all | solution.py:225
  123.6 4.9 %convolve.1 = bf16[32,16,512]{2,1,0:T(8,128)(2,1)S(1)} custom-call(bf16[32,16,512]{2,1,0:T(8,128)(2,1)S(1)} %all_to_all.10.value, bf16[256,16384]{1,0:T(8,128)(2,1)S(1)} %strip.1.strip_ref), custom_call_target="tpu_custom_call" | custom-call | flops 4499999744 | bytes 10485760 | tf_op jit(solution)/shard_map/convolve/pallas_call | solution.py:178
  128.5 20.4 %all_to_all.11 = bf16[32,16,512]{2,1,0:T(8,128)(2,1)S(1)} all-to-all(bf16[32,16,512]{2,1,0:T(8,128)(2,1)S(1)} %convolve.1), channel_id=1, replica_groups=mesh['seq'=32,'tp'=8] {'seq'}, dimensions={0} | all-to-all | bytes 1048576 | tf_op jit(solution)/shard_map/all_to_all | solution.py:227
  149.0 2.2 %mix.1 = bf16[512,512]{1,0:T(8,128)(2,1)} custom-call(bf16[512,512]{1,0:T(8,128)(2,1)S(1)} %bitcast.40, bf16[512,512]{1,0:T(8,128)(2,1)S(1)} %bitcast.39, f32[1,512]{1,0:T(1,128)S(1)} %bitcast.41, bf16[512,512]{1,0:T(8,128)(2,1)S(1)} %copy-done.1), custom_call_target="tpu_custom_call" | custom-call | tf_op jit(solution)/shard_map/mix/pallas_call | solution.py:202
  (66 shorter events, 14.8 us)
Async XLA Ops:
  6.5 1.4 copy-start.3
  6.5 57.5 %all-gather.2.cloned.1.call-start = ((), (), s32[]{:S(2)}) async-start(), calls=%async_computation.2 | async-start | bytes 9437184 | tf_op jit(solution)/shard_map/all_gather | solution.py:221
  8.0 7.3 %collective-permute-start = (bf16[144,512]{1,0:T(8,128)(2,1)S(1)}, bf16[144,512]{1,0:T(8,128)(2,1)S(1)}, u32[]{:S(2)}, u32[]{:S(2)}) collective-permute-start(bf16[144,512]{1,0:T(8,128)(2,1)S(1)} %pad_maximum_fusion.2), channel_id=1, source_target_pairs={{8,0},{16,8},{24,16},{32,24},{40,32},{48,40},{56,48},{0,56},{72,64... | collective-permute-start | bytes 442376 | tf_op jit(solution)/shard_map/ppermute | solution.py:20
  10.0 9.3 %collective-permute-start.2 = (bf16[144,512]{1,0:T(8,128)(2,1)S(1)}, bf16[144,512]{1,0:T(8,128)(2,1)S(1)}, u32[]{:S(2)}, u32[]{:S(2)}) collective-permute-start(bf16[144,512]{1,0:T(8,128)(2,1)S(1)} %pad_maximum_fusion.2), channel_id=1, source_target_pairs={{56,0},{0,8},{8,16},{16,24},{24,32},{32,40},{40,48},{48,56},{120,6... | collective-permute-start | bytes 442376 | tf_op jit(solution)/shard_map/ppermute | solution.py:20
  10.1 9.2 %collective-permute-start.5 = (bf16[128,512]{1,0:T(8,128)(2,1)S(1)}, bf16[128,512]{1,0:T(8,128)(2,1)S(1)}, u32[]{:S(2)}, u32[]{:S(2)}) collective-permute-start(bf16[128,512]{1,0:T(8,128)(2,1)S(1)} %get-tuple-element.42), channel_id=1, source_target_pairs={{128,0},{136,8},{144,16},{152,24},{160,32},{168,40},{176,48},{184,... | collective-permute-start | bytes 393224 | tf_op jit(solution)/shard_map/ppermute | solution.py:20
  13.3 6.4 %collective-permute-start.4 = (bf16[128,512]{1,0:T(8,128)(2,1)S(1)}, bf16[128,512]{1,0:T(8,128)(2,1)S(1)}, u32[]{:S(2)}, u32[]{:S(2)}) collective-permute-start(bf16[128,512]{1,0:T(8,128)(2,1)S(1)} %get-tuple-element.42), channel_id=1, source_target_pairs={{64,0},{72,8},{80,16},{88,24},{96,32},{104,40},{112,48},{120,56},{... | collective-permute-start | bytes 393224 | tf_op jit(solution)/shard_map/ppermute | solution.py:20
  14.4 6.2 %collective-permute-start.6 = (bf16[128,512]{1,0:T(8,128)(2,1)S(1)}, bf16[128,512]{1,0:T(8,128)(2,1)S(1)}, u32[]{:S(2)}, u32[]{:S(2)}) collective-permute-start(bf16[128,512]{1,0:T(8,128)(2,1)S(1)} %get-tuple-element.42), channel_id=1, source_target_pairs={{192,0},{200,8},{208,16},{216,24},{224,32},{232,40},{240,48},{248,... | collective-permute-start | bytes 393224 | tf_op jit(solution)/shard_map/ppermute | solution.py:20
  15.4 6.6 %collective-permute-start.1 = (bf16[144,512]{1,0:T(8,128)(2,1)S(1)}, bf16[144,512]{1,0:T(8,128)(2,1)S(1)}, u32[]{:S(2)}, u32[]{:S(2)}) collective-permute-start(bf16[144,512]{1,0:T(8,128)(2,1)S(1)} %collective-permute-done), channel_id=1, source_target_pairs={{8,0},{16,8},{24,16},{32,24},{40,32},{48,40},{56,48},{0,56},{72,64... | collective-permute-start | bytes 442376 | tf_op jit(solution)/shard_map/ppermute | solution.py:20
  19.3 6.4 %collective-permute-start.3 = (bf16[144,512]{1,0:T(8,128)(2,1)S(1)}, bf16[144,512]{1,0:T(8,128)(2,1)S(1)}, u32[]{:S(2)}, u32[]{:S(2)}) collective-permute-start(bf16[144,512]{1,0:T(8,128)(2,1)S(1)} %collective-permute-done.2), channel_id=1, source_target_pairs={{56,0},{0,8},{8,16},{16,24},{24,32},{32,40},{40,48},{48,56},{120,6... | collective-permute-start | bytes 442376 | tf_op jit(solution)/shard_map/ppermute | solution.py:20
  25.7 15.5 %collective-permute-start.10 = (bf16[4,128,512]{2,1,0:T(8,128)(2,1)S(1)}, bf16[4,128,512]{2,1,0:T(8,128)(2,1)S(1)}, u32[]{:S(2)}, u32[]{:S(2)}) collective-permute-start(bf16[4,128,512]{2,1,0:T(8,128)(2,1)S(1)} %pad_maximum_fusion.refs_1_), channel_id=1, source_target_pairs={{56,0},{0,8},{8,16},{16,24},{24,32},{32,40},{40,48},{48,56},{120,6... | collective-permute-start | bytes 1572872 | tf_op jit(solution)/shard_map/ppermute | solution.py:20
  25.7 15.5 %collective-permute-start.9 = (bf16[4,128,512]{2,1,0:T(8,128)(2,1)S(1)}, bf16[4,128,512]{2,1,0:T(8,128)(2,1)}, u32[]{:S(2)}, u32[]{:S(2)}) collective-permute-start(bf16[4,128,512]{2,1,0:T(8,128)(2,1)S(1)} %pad_maximum_fusion.refs_1_), channel_id=1, source_target_pairs={{8,0},{16,8},{24,16},{32,24},{40,32},{48,40},{56,48},{0,56},{72,64... | collective-permute-start | bytes 1572872 | tf_op jit(solution)/shard_map/ppermute | solution.py:20
  30.2 10.2 %collective-permute-start.7 = (bf16[144,512]{1,0:T(8,128)(2,1)S(1)}, bf16[144,512]{1,0:T(8,128)(2,1)S(1)}, u32[]{:S(2)}, u32[]{:S(2)}) collective-permute-start(bf16[144,512]{1,0:T(8,128)(2,1)S(1)} %collective-permute-done.1), channel_id=1, source_target_pairs={{8,0},{16,8},{24,16},{32,24},{40,32},{48,40},{56,48},{0,56},{72,64... | collective-permute-start | bytes 442376 | tf_op jit(solution)/shard_map/ppermute | solution.py:20
  33.5 7.7 %collective-permute-start.8 = (bf16[144,512]{1,0:T(8,128)(2,1)S(1)}, bf16[144,512]{1,0:T(8,128)(2,1)S(1)}, u32[]{:S(2)}, u32[]{:S(2)}) collective-permute-start(bf16[144,512]{1,0:T(8,128)(2,1)S(1)} %collective-permute-done.3), channel_id=1, source_target_pairs={{56,0},{0,8},{8,16},{16,24},{24,32},{32,40},{40,48},{48,56},{120,6... | collective-permute-start | bytes 442376 | tf_op jit(solution)/shard_map/ppermute | solution.py:20
  41.2 5.4 %collective-permute-start.12 = (bf16[72,512]{1,0:T(8,128)(2,1)S(1)}, bf16[72,512]{1,0:T(8,128)(2,1)S(1)}, u32[]{:S(2)}, u32[]{:S(2)}) collective-permute-start(bf16[72,512]{1,0:T(8,128)(2,1)S(1)} %slice.42), channel_id=1, source_target_pairs={{56,0},{0,8},{8,16},{16,24},{24,32},{32,40},{40,48},{48,56},{120,6... | collective-permute-start | bytes 221192 | tf_op jit(solution)/shard_map/ppermute | solution.py:20
  42.6 5.3 %collective-permute-start.11 = (bf16[72,512]{1,0:T(8,128)(2,1)S(1)}, bf16[72,512]{1,0:T(8,128)(2,1)S(1)}, u32[]{:S(2)}, u32[]{:S(2)}) collective-permute-start(bf16[72,512]{1,0:T(8,128)(2,1)S(1)} %slice.41), channel_id=1, source_target_pairs={{8,0},{16,8},{24,16},{32,24},{40,32},{48,40},{56,48},{0,56},{72,64... | collective-permute-start | bytes 221192 | tf_op jit(solution)/shard_map/ppermute | solution.py:20
  50.6 25.0 %collective-permute-start.16 = (bf16[8,144,512]{2,1,0:T(8,128)(2,1)}, bf16[8,144,512]{2,1,0:T(8,128)(2,1)S(1)}, u32[]{:S(2)}, u32[]{:S(2)}) collective-permute-start(bf16[8,144,512]{2,1,0:T(8,128)(2,1)} %bitcast_dynamic-update-slice_fusion.refs_0_), channel_id=1, source_target_pairs={{192,0},{200,8},{208,16},{216,24},{224,32},{232,40},{240,48},{248,... | collective-permute-start | bytes 3538952 | tf_op jit(solution)/shard_map/ppermute | solution.py:20
  51.0 24.6 %collective-permute-start.15 = (bf16[8,144,512]{2,1,0:T(8,128)(2,1)}, bf16[8,144,512]{2,1,0:T(8,128)(2,1)S(1)}, u32[]{:S(2)}, u32[]{:S(2)}) collective-permute-start(bf16[8,144,512]{2,1,0:T(8,128)(2,1)} %bitcast_dynamic-update-slice_fusion.refs_0_), channel_id=1, source_target_pairs={{64,0},{72,8},{80,16},{88,24},{96,32},{104,40},{112,48},{120,56},{... | collective-permute-start | bytes 3538952 | tf_op jit(solution)/shard_map/ppermute | solution.py:20
  53.9 16.6 %collective-permute-start.13 = (bf16[4,128,512]{2,1,0:T(8,128)(2,1)}, bf16[4,128,512]{2,1,0:T(8,128)(2,1)}, u32[]{:S(2)}, u32[]{:S(2)}) collective-permute-start(bf16[4,128,512]{2,1,0:T(8,128)(2,1)} %collective-permute-done.9.refs_2_), channel_id=1, source_target_pairs={{8,0},{16,8},{24,16},{32,24},{40,32},{48,40},{56,48},{0,56},{72,64... | collective-permute-start | bytes 1572872 | tf_op jit(solution)/shard_map/ppermute | solution.py:20
  55.7 14.7 %collective-permute-start.14 = (bf16[4,128,512]{2,1,0:T(8,128)(2,1)S(1)}, bf16[4,128,512]{2,1,0:T(8,128)(2,1)}, u32[]{:S(2)}, u32[]{:S(2)}) collective-permute-start(bf16[4,128,512]{2,1,0:T(8,128)(2,1)S(1)} %collective-permute-done.10.refs_3_), channel_id=1, source_target_pairs={{56,0},{0,8},{8,16},{16,24},{24,32},{32,40},{40,48},{48,56},{120,6... | collective-permute-start | bytes 1572872 | tf_op jit(solution)/shard_map/ppermute | solution.py:20
  64.1 3.4 %copy-start = (bf16[512,8192]{1,0:T(8,128)(2,1)S(1)}, bf16[512,8192]{1,0:T(8,128)(2,1)}, u32[]{:S(2)}) copy-start(bf16[512,8192]{1,0:T(8,128)(2,1)} %all-gather.2.cloned.1.call-done.hidden) | copy-start | bytes 25165828
  70.4 14.4 %collective-permute-start.19 = (bf16[4,128,512]{2,1,0:T(8,128)(2,1)}, bf16[4,128,512]{2,1,0:T(8,128)(2,1)S(1)}, u32[]{:S(2)}, u32[]{:S(2)}) collective-permute-start(bf16[4,128,512]{2,1,0:T(8,128)(2,1)} %collective-permute-done.13.refs_0_), channel_id=1, source_target_pairs={{8,0},{16,8},{24,16},{32,24},{40,32},{48,40},{56,48},{0,56},{72,64... | collective-permute-start | bytes 1572872 | tf_op jit(solution)/shard_map/ppermute | solution.py:20
  71.0 15.6 %collective-permute-start.20 = (bf16[4,128,512]{2,1,0:T(8,128)(2,1)}, bf16[4,128,512]{2,1,0:T(8,128)(2,1)S(1)}, u32[]{:S(2)}, u32[]{:S(2)}) collective-permute-start(bf16[4,128,512]{2,1,0:T(8,128)(2,1)} %collective-permute-done.14.refs_1_), channel_id=1, source_target_pairs={{56,0},{0,8},{8,16},{16,24},{24,32},{32,40},{40,48},{48,56},{120,6... | collective-permute-start | bytes 1572872 | tf_op jit(solution)/shard_map/ppermute | solution.py:20
  75.7 15.2 %collective-permute-start.18 = (bf16[4,144,512]{2,1,0:T(8,128)(2,1)S(1)}, bf16[4,144,512]{2,1,0:T(8,128)(2,1)S(1)}, u32[]{:S(2)}, u32[]{:S(2)}) collective-permute-start(bf16[4,144,512]{2,1,0:T(8,128)(2,1)S(1)} %slice.44), channel_id=1, source_target_pairs={{192,0},{200,8},{208,16},{216,24},{224,32},{232,40},{240,48},{248,... | collective-permute-start | bytes 1769480 | tf_op jit(solution)/shard_map/ppermute | solution.py:20
  76.3 14.6 %collective-permute-start.17 = (bf16[4,144,512]{2,1,0:T(8,128)(2,1)S(1)}, bf16[4,144,512]{2,1,0:T(8,128)(2,1)S(1)}, u32[]{:S(2)}, u32[]{:S(2)}) collective-permute-start(bf16[4,144,512]{2,1,0:T(8,128)(2,1)S(1)} %slice.43), channel_id=1, source_target_pairs={{64,0},{72,8},{80,16},{88,24},{96,32},{104,40},{112,48},{120,56},{... | collective-permute-start | bytes 1769480 | tf_op jit(solution)/shard_map/ppermute | solution.py:20
  86.6 10.2 %slice-start = ((s8[8388608]{0:T(1024)(128)(4,1)}), s8[4194304]{0:T(1024)(128)(4,1)S(1)}, s32[]{:S(2)}) async-start(s8[8388608]{0:T(1024)(128)(4,1)} %bitcast.37), calls=%async_computation.3 | async-start | bytes 8388608
  86.6 10.1 %slice-start.1 = ((s8[8388608]{0:T(1024)(128)(4,1)}), s8[4194304]{0:T(1024)(128)(4,1)S(1)}, s32[]{:S(2)}) async-start(s8[8388608]{0:T(1024)(128)(4,1)} %bitcast.37), calls=%async_computation.4 | async-start | bytes 8388608
  86.6 9.4 %collective-permute-start.21 = (bf16[2,128,512]{2,1,0:T(8,128)(2,1)S(1)}, bf16[2,128,512]{2,1,0:T(8,128)(2,1)S(1)}, u32[]{:S(2)}, u32[]{:S(2)}) collective-permute-start(bf16[2,128,512]{2,1,0:T(8,128)(2,1)S(1)} %slice.45), channel_id=1, source_target_pairs={{8,0},{16,8},{24,16},{32,24},{40,32},{48,40},{56,48},{0,56},{72,64... | collective-permute-start | bytes 786440 | tf_op jit(solution)/shard_map/ppermute | solution.py:20
  89.7 7.1 %collective-permute-start.22 = (bf16[2,128,512]{2,1,0:T(8,128)(2,1)S(1)}, bf16[2,128,512]{2,1,0:T(8,128)(2,1)S(1)}, u32[]{:S(2)}, u32[]{:S(2)}) collective-permute-start(bf16[2,128,512]{2,1,0:T(8,128)(2,1)S(1)} %slice.46), channel_id=1, source_target_pairs={{56,0},{0,8},{8,16},{16,24},{24,32},{32,40},{40,48},{48,56},{120,6... | collective-permute-start | bytes 786440 | tf_op jit(solution)/shard_map/ppermute | solution.py:20
  123.6 25.3 %copy-start.2 = (f32[512]{0:T(512)S(1)}, f32[512]{0:T(512)}, u32[]{:S(2)}) copy-start(f32[512]{0:T(512)} %param.9) | copy-start | bytes 6148
  128.5 20.5 %copy-start.1 = (bf16[512,512]{1,0:T(8,128)(2,1)S(1)}, bf16[512,512]{1,0:T(8,128)(2,1)}, u32[]{:S(2)}) copy-start(bf16[512,512]{1,0:T(8,128)(2,1)} %gate.1) | copy-start | bytes 1572868
Sparse Core Ops, SparseCore 0:
  9.2 54.8 all-gather.1

commit v3 on v2

--- a/solution.py
+++ b/solution.py
@@ -9,7 +9,7 @@
 
 NY, NZ = 4, 8
 FIRST = 128
-TAP_ROWS = 16
+TAP_ROWS = 8
 VMEM_LIMIT = 16 * 1024 * 1024
 
 
@@ -20,16 +20,35 @@
     return lax.ppermute(array, "seq", pairs)
 
 
-def project_kernel(parts, first, last, place, hidden, *refs):
+def starts_kernel(place, out):
+    for dy in range(NY):
+        for dz in range(NZ):
+            block = lax.rem(place[0] + dy, NY) * NZ + lax.rem(place[1] + dz, NZ)
+            out[dy * NZ + dz] = block * 2 * FIRST
+
+
+def starts_of(place):
+    return pl.pallas_call(
+        starts_kernel,
+        out_shape=jax.ShapeDtypeStruct((NY * NZ,), jnp.int32),
+        in_specs=[pl.BlockSpec(memory_space=pltpu.SMEM)],
+        out_specs=pl.BlockSpec(memory_space=pltpu.SMEM),
+        compiler_params=pltpu.CompilerParams(vmem_limit_bytes=VMEM_LIMIT),
+        cost_estimate=pl.CostEstimate(
+            flops=8_000_000_000, bytes_accessed=1 << 20, transcendentals=0
+        ),
+        name="starts",
+    )(place)
+
+
+def project_kernel(parts, first, last, starts, hidden, *refs):
     refs = list(refs)
     out = refs.pop()
     total = jnp.zeros((512, 512), jnp.float32) if first else refs.pop()[...]
-    y, z = place[0], place[1]
     pieces = []
     for ref, part in zip(refs, parts, strict=True):
         for at, (dy, dz, second) in enumerate(part):
-            block = lax.rem(y + dy, NY) * NZ + lax.rem(z + dz, NZ)
-            start = pl.multiple_of(block * 256 + FIRST * second, FIRST)
+            start = pl.multiple_of(starts[dy * NZ + dz] + FIRST * second, FIRST)
             pieces.append((start, ref, at))
     for n in range(0, len(pieces), 8):
         group = pieces[n : n + 8]
@@ -43,7 +62,7 @@
     out[...] = total.T.reshape(32, 16, 512).astype(jnp.bfloat16) if last else total
 
 
-def project(place, hidden, held, before=None, last=False):
+def project(starts, hidden, held, before=None, last=False):
     arrays = [array for array, _ in held]
     parts = [part for _, part in held]
     count = sum(len(part) for part in parts)
@@ -66,7 +85,7 @@
             transcendentals=0,
         ),
         name=f"project_{count}",
-    )(place, hidden, *arrays, *extra)
+    )(starts, hidden, *arrays, *extra)
 
 
 def halves(one, other, dy, dz):
@@ -81,7 +100,6 @@
     line = {0: first, 1: take_from(first, 0, 1), -1: take_from(first, 0, -1)}
     column = jnp.stack([second, *(take_from(second, k, 0) for k in (1, 2, 3))])
     line[2], line[-2] = take_from(line[1], 0, 1), take_from(line[-1], 0, -1)
-    line[2], line[-2], column = lax.optimization_barrier((line[2], line[-2], column))
     line[3], line[-3] = take_from(line[2], 0, 1), take_from(line[-2], 0, -1)
     ring = {0: column, 1: take_from(column, 0, 1), -1: take_from(column, 0, -1)}
     line[3], line[-3], ring[1], ring[-1] = lax.optimization_barrier(
@@ -98,20 +116,22 @@
         return [(dy, dz % NZ, 1) for dy in range(start, stop)]
 
     ring[2], ring[-2] = take_from(ring[1], 0, 1), take_from(ring[-1], 0, -1)
+    place, ring[2], ring[-2] = lax.optimization_barrier((place, ring[2], ring[-2]))
+    starts = starts_of(place)
+    starts, ring[2], ring[-2] = lax.optimization_barrier((starts, ring[2], ring[-2]))
     held = [(mine, row(0))] + [(ring[k], stack(k)) for k in (0, 1, -1)]
-    total = project(place, hidden, held)
-    total, ring[2], ring[-2] = lax.optimization_barrier((total, ring[2], ring[-2]))
+    total = project(starts, hidden, held)
     ring[3], ring[-3] = take_from(ring[2], 0, 1), take_from(ring[-2], 0, -1)
-    total = project(place, hidden, [(ring[k], stack(k)) for k in (2, -2)], total)
+    total = project(starts, hidden, [(ring[k], stack(k)) for k in (2, -2)], total)
     total, above, below = lax.optimization_barrier((total, above, below))
     across = halves(above, below, 1, 0)
-    total = project(place, hidden, [(above, row(1)), (below, row(3))], total)
+    total = project(starts, hidden, [(above, row(1)), (below, row(3))], total)
     total, ring[3], ring[-3] = lax.optimization_barrier((total, ring[3], ring[-3]))
     ends = halves(ring[3], ring[-3], 0, 1)
-    total = project(place, hidden, [(ring[k], stack(k)) for k in (3, -3)], total)
+    total = project(starts, hidden, [(ring[k], stack(k)) for k in (3, -3)], total)
     held = [(across[0], row(2, 0, 4)), (across[1], row(2, 4, 8))]
     held += [(ends[0], stack(4, 0, 2)), (ends[1], stack(4, 2, 4))]
-    value = project(place, hidden, held, total, last=True)
+    value = project(starts, hidden, held, total, last=True)
     across = jnp.concatenate([part[:, FIRST:] for part in across], axis=0)
     taps = jnp.stack([mine[:, FIRST:], above[:, FIRST:], across, below[:, FIRST:]])
     return value, taps
@@ -119,21 +139,22 @@
 
 def strip_kernel(place, taps, out):
     rows, step = 256, 512
-    y, z, which = place[0], place[1], place[2]
-    pick = lax.broadcasted_iota(jnp.int32, (TAP_ROWS, step), 0) == which
-
-    def chunk(i, before):
+    y, z = place[0], place[1]
+
+    def block(i):
         dy = lax.rem(lax.div(i, NZ) - y + NY, NY)
         dz = lax.rem(lax.rem(i, NZ) - z + NZ, NZ)
-        held = taps[dy, dz].astype(jnp.float32)
-        block = jnp.sum(jnp.where(pick, held, 0.0), axis=0, keepdims=True)
-        window = jnp.concatenate([before, block], axis=1)
+        return taps[dy, dz]
+
+    def chunk(i, carry):
+        before = jnp.where(i == 0, 0.0, block(jnp.maximum(i - 1, 0))[:, step - rows :])
+        window = jnp.concatenate([before, block(i)], axis=1)
         window = jnp.broadcast_to(window, (rows, step + rows))
         rolled = pltpu.roll(window, 0, 1, stride=1, stride_axis=0)
         out[:, pl.ds(pl.multiple_of(i * step, step), step)] = rolled[:, rows:].astype(jnp.bfloat16)
-        return block[:, step - rows :]
-
-    lax.fori_loop(0, out.shape[1] // step, chunk, jnp.zeros((1, rows), jnp.float32))
+        return carry
+
+    lax.fori_loop(0, out.shape[1] // step, chunk, 0)
 
 
 def strip(place, taps):
@@ -220,6 +241,7 @@
     place = jnp.stack([index // NZ, index % NZ, index // 8]).astype(jnp.int32)
     whole = lax.all_gather(hidden, "tp", axis=1, tiled=True)
     value, taps = gather_and_project(place, whole, value_weight, filters)
+    taps = lax.dynamic_index_in_dim(taps, index // 8, 2).astype(jnp.float32)
     taps_strip = strip(place, taps)
     value, taps_strip = lax.optimization_barrier((value, taps_strip))
     moved = lax.all_to_all(value, "seq", split_axis=0, concat_axis=0, tiled=True)

time: 158 us -> 153 us (0.968)
  blocking collectives: 45.7 us -> 40.2 us
  waiting for transfers between devices: 31.7 us -> 26.3 us
  starting transfers between devices: 34.6 us -> 36.4 us
  Pallas kernels: 21.6 us -> 23.3 us
    all_gather x1, waiting for transfers between devices: 8.12 us -> 1.83 us  [on_device(): whole = lax.all_gather(hidden, 'tp', axis=1, tiled=True)]
    all_to_all x1, blocking collectives: 25.3 us -> 22.2 us  [on_device(): lax.all_to_all(value, 'seq', split_axis=0, concat_axis=0, tiled=True)]
    all_to_all x1, blocking collectives: 20.4 us -> 18.1 us  [on_device(): lax.all_to_all(conv, 'seq', split_axis=0, concat_axis=0, tiled=True)]
    ppermute x23, starting transfers between devices: 34.6 us -> 36.4 us  [take_from(): return lax.ppermute(array, 'seq', pairs)]
    unnamed x17 -> x23, local copies, waits for them, and re-layouts: 6.77 us -> 8.01 us
  transfers between devices with their start and end apart: 24 -> 24, of which waited for: 13 -> 10; matrix products, arithmetic and copies ran while one was open for 5% -> 5% of each run, Pallas kernels for 8% -> 10%
where the time goes in v3:
time: 153 us; the launch traced here: 152 us
  blocking collectives  40.2 us (26%)
  starting transfers between devices  36.4 us (24%)
  waiting for transfers between devices  26.3 us (17%)
  Pallas kernels  23.3 us (15%)
  between operations  13.7 us (9%)
  local copies, waits for them, and re-layouts  10.7 us (7%)
  other arithmetic  1.58 us (1%)
    ppermute x23, starting transfers between devices, take_from(): return lax.ppermute(array, 'seq', pairs)  36.4 us
    ppermute x23, waiting for transfers between devices, take_from(): return lax.ppermute(array, 'seq', pairs)  23.8 us
    all_to_all x1, blocking collectives, on_device(): lax.all_to_all(value, 'seq', split_axis=0, concat_axis=0, tiled=True)  22.2 us
    all_to_all x1, blocking collectives, on_device(): lax.all_to_all(conv, 'seq', split_axis=0, concat_axis=0, tiled=True)  18.1 us
    pallas_call x5, Pallas kernels, project(): pl.pallas_call(functools.partial(project_kernel, parts, before is None, l...  10.2 us
    unnamed x23, local copies, waits for them, and re-layouts  8.01 us
    pallas_call x1, Pallas kernels, convolve(): pl.pallas_call(conv_kernel, out_shape=jax.ShapeDtypeStruct((32, 16, 512),...  4.88 us
    pallas_call x1, Pallas kernels, strip(): pl.pallas_call(strip_kernel, out_shape=jax.ShapeDtypeStruct((256, 16384),...  4.8 us
  transfers between devices with their start and end apart: 24, of which 10 were waited for; matrix products, arithmetic and copies ran while one was open for 5% of the time, Pallas kernels for 10%

profile of v3, /device:TPU:32, one launch (start us, length us, event | category | flops | bytes accessed | tf_op | source)
XLA Modules:
  0.0 152.1 jit_solution(10029686472649771894)
XLA Ops:
  7.5 3.3 %collective-permute-start.7 = (bf16[128,512]{1,0:T(8,128)(2,1)S(1)}, bf16[128,512]{1,0:T(8,128)(2,1)S(1)}, u32[]{:S(2)}, u32[]{:S(2)}) collective-permute-start(bf16[128,512]{1,0:T(8,128)(2,1)S(1)} %get-tuple-element.42), channel_id=1, source_target_pairs={{128,0},{136,8},{144,16},{152,24},{160,32},{168,40},{176,48},{184,... | collective-permute-start | bytes 393224 | tf_op jit(solution)/shard_map/ppermute | solution.py:20
  12.9 2.0 %collective-permute-start.3 = (bf16[136,512]{1,0:T(8,128)(2,1)S(1)}, bf16[136,512]{1,0:T(8,128)(2,1)S(1)}, u32[]{:S(2)}, u32[]{:S(2)}) collective-permute-start(bf16[136,512]{1,0:T(8,128)(2,1)S(1)} %pad_maximum_fusion.1), channel_id=1, source_target_pairs={{56,0},{0,8},{8,16},{16,24},{24,32},{32,40},{40,48},{48,56},{120,6... | collective-permute-start | bytes 417800 | tf_op jit(solution)/shard_map/ppermute | solution.py:20
  15.0 2.5 %collective-permute-done.6 = bf16[128,512]{1,0:T(8,128)(2,1)S(1)} collective-permute-done((bf16[128,512]{1,0:T(8,128)(2,1)S(1)}, bf16[128,512]{1,0:T(8,128)(2,1)S(1)}, u32[]{:S(2)}, u32[]{:S(2)}) %collective-permute-start.6) | collective-permute-done | bytes 131104 | tf_op jit(solution)/shard_map/ppermute | solution.py:20
  18.1 2.0 %collective-permute-start.10 = (bf16[4,128,512]{2,1,0:T(8,128)(2,1)S(1)}, bf16[4,128,512]{2,1,0:T(8,128)(2,1)S(1)}, u32[]{:S(2)}, u32[]{:S(2)}) collective-permute-start(bf16[4,128,512]{2,1,0:T(8,128)(2,1)S(1)} %pad_maximum_fusion.refs_1_), channel_id=1, source_target_pairs={{56,0},{0,8},{8,16},{16,24},{24,32},{32,40},{40,48},{48,56},{120,6... | collective-permute-start | bytes 1572872 | tf_op jit(solution)/shard_map/ppermute | solution.py:20
  20.9 1.9 %collective-permute-start.4 = (bf16[136,512]{1,0:T(8,128)(2,1)S(1)}, bf16[136,512]{1,0:T(8,128)(2,1)S(1)}, u32[]{:S(2)}, u32[]{:S(2)}) collective-permute-start(bf16[136,512]{1,0:T(8,128)(2,1)S(1)} %collective-permute-done.3), channel_id=1, source_target_pairs={{56,0},{0,8},{8,16},{16,24},{24,32},{32,40},{40,48},{48,56},{120,6... | collective-permute-start | bytes 417800 | tf_op jit(solution)/shard_map/ppermute | solution.py:20
  22.8 2.2 %collective-permute-start.1 = (bf16[136,512]{1,0:T(8,128)(2,1)S(1)}, bf16[136,512]{1,0:T(8,128)(2,1)S(1)}, u32[]{:S(2)}, u32[]{:S(2)}) collective-permute-start(bf16[136,512]{1,0:T(8,128)(2,1)S(1)} %collective-permute-done), channel_id=1, source_target_pairs={{8,0},{16,8},{24,16},{32,24},{40,32},{48,40},{56,48},{0,56},{72,64... | collective-permute-start | bytes 417800 | tf_op jit(solution)/shard_map/ppermute | solution.py:20
  25.7 8.0 %collective-permute-done.4 = bf16[136,512]{1,0:T(8,128)(2,1)S(1)} collective-permute-done((bf16[136,512]{1,0:T(8,128)(2,1)S(1)}, bf16[136,512]{1,0:T(8,128)(2,1)S(1)}, u32[]{:S(2)}, u32[]{:S(2)}) %collective-permute-start.4) | collective-permute-done | bytes 139296 | tf_op jit(solution)/shard_map/ppermute | solution.py:20
  33.7 1.7 %collective-permute-start.5 = (bf16[136,512]{1,0:T(8,128)(2,1)S(1)}, bf16[136,512]{1,0:T(8,128)(2,1)S(1)}, u32[]{:S(2)}, u32[]{:S(2)}) collective-permute-start(bf16[136,512]{1,0:T(8,128)(2,1)S(1)} %collective-permute-done.4), channel_id=1, source_target_pairs={{56,0},{0,8},{8,16},{16,24},{24,32},{32,40},{40,48},{48,56},{120,6... | collective-permute-start | bytes 417800 | tf_op jit(solution)/shard_map/ppermute | solution.py:20
  35.3 2.3 %collective-permute-start.2 = (bf16[136,512]{1,0:T(8,128)(2,1)S(1)}, bf16[136,512]{1,0:T(8,128)(2,1)S(1)}, u32[]{:S(2)}, u32[]{:S(2)}) collective-permute-start(bf16[136,512]{1,0:T(8,128)(2,1)S(1)} %collective-permute-done.1), channel_id=1, source_target_pairs={{8,0},{16,8},{24,16},{32,24},{40,32},{48,40},{56,48},{0,56},{72,64... | collective-permute-start | bytes 417800 | tf_op jit(solution)/shard_map/ppermute | solution.py:20
  38.3 2.4 %collective-permute-done.5 = bf16[136,512]{1,0:T(8,128)(2,1)S(1)} collective-permute-done((bf16[136,512]{1,0:T(8,128)(2,1)S(1)}, bf16[136,512]{1,0:T(8,128)(2,1)S(1)}, u32[]{:S(2)}, u32[]{:S(2)}) %collective-permute-start.5) | collective-permute-done | bytes 139296 | tf_op jit(solution)/shard_map/ppermute | solution.py:20
  41.5 3.3 %collective-permute-start.14 = (bf16[68,512]{1,0:T(8,128)(2,1)S(1)}, bf16[68,512]{1,0:T(8,128)(2,1)S(1)}, u32[]{:S(2)}, u32[]{:S(2)}) collective-permute-start(bf16[68,512]{1,0:T(8,128)(2,1)S(1)} %slice.42), channel_id=1, source_target_pairs={{56,0},{0,8},{8,16},{16,24},{24,32},{32,40},{40,48},{48,56},{120,6... | collective-permute-start | bytes 208904 | tf_op jit(solution)/shard_map/ppermute | solution.py:20
  44.8 2.6 %collective-permute-start.11 = (bf16[4,128,512]{2,1,0:T(8,128)(2,1)}, bf16[4,128,512]{2,1,0:T(8,128)(2,1)}, u32[]{:S(2)}, u32[]{:S(2)}) collective-permute-start(bf16[4,128,512]{2,1,0:T(8,128)(2,1)} %collective-permute-done.9.refs_2_), channel_id=1, source_target_pairs={{8,0},{16,8},{24,16},{32,24},{40,32},{48,40},{56,48},{0,56},{72,64... | collective-permute-start | bytes 1572872 | tf_op jit(solution)/shard_map/ppermute | solution.py:20
  48.7 2.5 %collective-permute-done.13 = bf16[68,512]{1,0:T(8,128)(2,1)S(1)} collective-permute-done((bf16[68,512]{1,0:T(8,128)(2,1)S(1)}, bf16[68,512]{1,0:T(8,128)(2,1)S(1)}, u32[]{:S(2)}, u32[]{:S(2)}) %collective-permute-start.13) | collective-permute-done | bytes 69664 | tf_op jit(solution)/shard_map/ppermute | solution.py:20
  53.9 2.3 %collective-permute-start.16 = (bf16[8,136,512]{2,1,0:T(8,128)(2,1)}, bf16[8,136,512]{2,1,0:T(8,128)(2,1)S(1)}, u32[]{:S(2)}, u32[]{:S(2)}) collective-permute-start(bf16[8,136,512]{2,1,0:T(8,128)(2,1)} %bitcast_dynamic-update-slice_fusion.refs_0_), channel_id=1, source_target_pairs={{192,0},{200,8},{208,16},{216,24},{224,32},{232,40},{240,48},{248,... | collective-permute-start | bytes 3342344 | tf_op jit(solution)/shard_map/ppermute | solution.py:20
  56.1 1.4 collective-permute-start.15
  58.1 1.2 starts.1
  59.3 3.0 %collective-permute-start.19 = (bf16[4,128,512]{2,1,0:T(8,128)(2,1)}, bf16[4,128,512]{2,1,0:T(8,128)(2,1)S(1)}, u32[]{:S(2)}, u32[]{:S(2)}) collective-permute-start(bf16[4,128,512]{2,1,0:T(8,128)(2,1)} %collective-permute-done.11.refs_0_), channel_id=1, source_target_pairs={{8,0},{16,8},{24,16},{32,24},{40,32},{48,40},{56,48},{0,56},{72,64... | collective-permute-start | bytes 1572872 | tf_op jit(solution)/shard_map/ppermute | solution.py:20
  62.3 1.8 %all-gather.2.cloned.1.call-done.hidden = bf16[512,8192]{1,0:T(8,128)(2,1)} async-done(((bf16[512,1024]{1,0:T(8,128)(2,1)}), bf16[512,8192]{1,0:T(8,128)(2,1)}) %all-gather.2.cloned.1.call-update) | async-done | bytes 8388624 | tf_op jit(solution)/shard_map/all_gather | solution.py:242
  64.1 3.4 %copy-done = bf16[512,8192]{1,0:T(8,128)(2,1)S(1)} copy-done((bf16[512,8192]{1,0:T(8,128)(2,1)S(1)}, bf16[512,8192]{1,0:T(8,128)(2,1)}, u32[]{:S(2)}) %copy-start) | copy-done | bytes 8388632
  68.5 2.9 %project_20.1.refs_2_ = f32[512,512]{1,0:T(8,128)S(1)} custom-call(s32[32]{0:T(128)S(1)} %starts.1, bf16[512,8192]{1,0:T(8,128)(2,1)S(1)} %copy-done, bf16[8,136,512]{2,1,0:T(8,128)(2,1)} %bitcast_dynamic-update-slice_fusion.refs_0_, bf16[4,128,512]{2,1,0:T(8,128)(2,1)S(1)} %pad_maximum_fusion.refs_1_, bf16[4,128,512]{2,1,0:T(8,128)(2,1)} %collective-permute-done.9.refs_2_, ...), custom_call_target="tpu_custom_call" | custom-call | flops 1342177280 | bytes 5242880 | tf_op jit(solution)/shard_map/project_20/pallas_call | solution.py:76
  71.4 1.9 %project_8.2.refs_2_ = f32[512,512]{1,0:T(8,128)S(1)} custom-call(s32[32]{0:T(128)S(1)} %starts.1, bf16[512,8192]{1,0:T(8,128)(2,1)S(1)} %copy-done, bf16[4,128,512]{2,1,0:T(8,128)(2,1)} %collective-permute-done.11.refs_0_, bf16[4,128,512]{2,1,0:T(8,128)(2,1)} %collective-permute-done.12.refs_1_, f32[512,512]{1,0:T(8,128)S(1)} %project_20.1.refs_2_), custom_call_target="tpu_custom_call" | custom-call | flops 536870912 | bytes 2097152 | tf_op jit(solution)/shard_map/project_8/pallas_call | solution.py:76
  73.4 5.7 %collective-permute-done.16.refs_1_ = bf16[8,136,512]{2,1,0:T(8,128)(2,1)S(1)} collective-permute-done((bf16[8,136,512]{2,1,0:T(8,128)(2,1)}, bf16[8,136,512]{2,1,0:T(8,128)(2,1)S(1)}, u32[]{:S(2)}, u32[]{:S(2)}) %collective-permute-start.16) | collective-permute-done | bytes 1114144 | tf_op jit(solution)/shard_map/ppermute | solution.py:20
  80.6 2.7 %collective-permute-start.17 = (bf16[4,136,512]{2,1,0:T(8,128)(2,1)S(1)}, bf16[4,136,512]{2,1,0:T(8,128)(2,1)S(1)}, u32[]{:S(2)}, u32[]{:S(2)}) collective-permute-start(bf16[4,136,512]{2,1,0:T(8,128)(2,1)S(1)} %slice.43), channel_id=1, source_target_pairs={{64,0},{72,8},{80,16},{88,24},{96,32},{104,40},{112,48},{120,56},{... | collective-permute-start | bytes 1671176 | tf_op jit(solution)/shard_map/ppermute | solution.py:20
  84.2 1.8 %project_16.1.refs_2_ = f32[512,512]{1,0:T(8,128)S(1)} custom-call(s32[32]{0:T(128)S(1)} %starts.1, bf16[512,8192]{1,0:T(8,128)(2,1)S(1)} %copy-done, bf16[8,136,512]{2,1,0:T(8,128)(2,1)S(1)} %collective-permute-done.15.refs_0_, bf16[8,136,512]{2,1,0:T(8,128)(2,1)S(1)} %collective-permute-done.16.refs_1_, f32[512,512]{1,0:T(8,128)S(1)} %project_8.2.refs_2_), custom_call_target="tpu_custom_call" | custom-call | flops 1073741824 | bytes 4194304 | tf_op jit(solution)/shard_map/project_16/pallas_call | solution.py:76
  87.1 2.2 %collective-permute-start.22 = (bf16[2,128,512]{2,1,0:T(8,128)(2,1)S(1)}, bf16[2,128,512]{2,1,0:T(8,128)(2,1)S(1)}, u32[]{:S(2)}, u32[]{:S(2)}) collective-permute-start(bf16[2,128,512]{2,1,0:T(8,128)(2,1)S(1)} %slice.46), channel_id=1, source_target_pairs={{56,0},{0,8},{8,16},{16,24},{24,32},{32,40},{40,48},{48,56},{120,6... | collective-permute-start | bytes 786440 | tf_op jit(solution)/shard_map/ppermute | solution.py:20
  89.4 1.9 %project_8.3.refs_4_ = f32[512,512]{1,0:T(8,128)S(1)} custom-call(s32[32]{0:T(128)S(1)} %starts.1, bf16[512,8192]{1,0:T(8,128)(2,1)S(1)} %copy-done, bf16[4,128,512]{2,1,0:T(8,128)(2,1)S(1)} %collective-permute-done.19.refs_0_, bf16[4,128,512]{2,1,0:T(8,128)(2,1)} %collective-permute-done.20.refs_1_, f32[512,512]{1,0:T(8,128)S(1)} %project_16.1.refs_2_), custom_call_target="tpu_custom_call" | custom-call | flops 536870912 | bytes 2097152 | tf_op jit(solution)/shard_map/project_8/pallas_call | solution.py:76
  91.4 4.8 %strip.1.strip_ref = bf16[256,16384]{1,0:T(8,128)(2,1)S(1)} custom-call(s32[3]{0:T(128)S(1)} %pad_add_fusion.place, f32[4,8,1,512]{3,2,1,0:T(1,128)S(1)} %fusion.4.taps), custom_call_target="tpu_custom_call" | custom-call | flops 10485760 | bytes 8388608 | tf_op jit(solution)/shard_map/strip/pallas_call | solution.py:162
  96.3 1.6 %project_12.1 = bf16[32,16,512]{2,1,0:T(8,128)(2,1)S(1)} custom-call(s32[32]{0:T(128)S(1)} %starts.1, bf16[512,8192]{1,0:T(8,128)(2,1)S(1)} %bitcast.38, bf16[4,136,512]{2,1,0:T(8,128)(2,1)S(1)} %collective-permute-done.17.refs_0_, bf16[4,136,512]{2,1,0:T(8,128)(2,1)S(1)} %collective-permute-done.18.refs_1_, ...), custom_call_target="tpu_custom_call" | custom-call | flops 805306368 | bytes 3145728 | tf_op jit(solution)/shard_map/project_12/pallas_call | solution.py:76
  97.9 22.2 %all_to_all.10.value = bf16[32,16,512]{2,1,0:T(8,128)(2,1)S(1)} all-to-all(bf16[32,16,512]{2,1,0:T(8,128)(2,1)S(1)} %project_12.1), channel_id=1, replica_groups=mesh['seq'=32,'tp'=8] {'seq'}, dimensions={0} | all-to-all | bytes 1048576 | tf_op jit(solution)/shard_map/all_to_all | solution.py:247
  120.0 4.9 %convolve.1 = bf16[32,16,512]{2,1,0:T(8,128)(2,1)S(1)} custom-call(bf16[32,16,512]{2,1,0:T(8,128)(2,1)S(1)} %all_to_all.10.value, bf16[256,16384]{1,0:T(8,128)(2,1)S(1)} %strip.1.strip_ref), custom_call_target="tpu_custom_call" | custom-call | flops 4499999744 | bytes 10485760 | tf_op jit(solution)/shard_map/convolve/pallas_call | solution.py:199
  124.9 18.1 %all_to_all.11 = bf16[32,16,512]{2,1,0:T(8,128)(2,1)S(1)} all-to-all(bf16[32,16,512]{2,1,0:T(8,128)(2,1)S(1)} %convolve.1), channel_id=1, replica_groups=mesh['seq'=32,'tp'=8] {'seq'}, dimensions={0} | all-to-all | bytes 1048576 | tf_op jit(solution)/shard_map/all_to_all | solution.py:249
  143.0 2.2 %mix.1 = bf16[512,512]{1,0:T(8,128)(2,1)} custom-call(bf16[512,512]{1,0:T(8,128)(2,1)S(1)} %bitcast.40, bf16[512,512]{1,0:T(8,128)(2,1)S(1)} %bitcast.39, f32[1,512]{1,0:T(1,128)S(1)} %bitcast.41, bf16[512,512]{1,0:T(8,128)(2,1)S(1)} %copy-done.1), custom_call_target="tpu_custom_call" | custom-call | tf_op jit(solution)/shard_map/mix/pallas_call | solution.py:223
  (73 shorter events, 15.9 us)
Async XLA Ops:
  6.5 6.3 %copy-start.6 = (bf16[512,4]{0,1:T(4,128)(2,1)S(1)}, bf16[512,4]{0,1:T(4,128)(2,1)}, u32[]{:S(2)}) copy-start(bf16[512,4]{0,1:T(4,128)(2,1)} %param.8) | copy-start | bytes 12292
  6.5 57.5 %all-gather.2.cloned.1.call-start = ((), (), s32[]{:S(2)}) async-start(), calls=%async_computation.2 | async-start | bytes 9437184 | tf_op jit(solution)/shard_map/all_gather | solution.py:242
  7.5 7.5 %collective-permute-start.7 = (bf16[128,512]{1,0:T(8,128)(2,1)S(1)}, bf16[128,512]{1,0:T(8,128)(2,1)S(1)}, u32[]{:S(2)}, u32[]{:S(2)}) collective-permute-start(bf16[128,512]{1,0:T(8,128)(2,1)S(1)} %get-tuple-element.42), channel_id=1, source_target_pairs={{128,0},{136,8},{144,16},{152,24},{160,32},{168,40},{176,48},{184,... | collective-permute-start | bytes 393224 | tf_op jit(solution)/shard_map/ppermute | solution.py:20
  10.8 6.7 %collective-permute-start.6 = (bf16[128,512]{1,0:T(8,128)(2,1)S(1)}, bf16[128,512]{1,0:T(8,128)(2,1)S(1)}, u32[]{:S(2)}, u32[]{:S(2)}) collective-permute-start(bf16[128,512]{1,0:T(8,128)(2,1)S(1)} %get-tuple-element.42), channel_id=1, source_target_pairs={{64,0},{72,8},{80,16},{88,24},{96,32},{104,40},{112,48},{120,56},{... | collective-permute-start | bytes 393224 | tf_op jit(solution)/shard_map/ppermute | solution.py:20
  11.9 6.2 %collective-permute-start.8 = (bf16[128,512]{1,0:T(8,128)(2,1)S(1)}, bf16[128,512]{1,0:T(8,128)(2,1)S(1)}, u32[]{:S(2)}, u32[]{:S(2)}) collective-permute-start(bf16[128,512]{1,0:T(8,128)(2,1)S(1)} %get-tuple-element.42), channel_id=1, source_target_pairs={{192,0},{200,8},{208,16},{216,24},{224,32},{232,40},{240,48},{248,... | collective-permute-start | bytes 393224 | tf_op jit(solution)/shard_map/ppermute | solution.py:20
  12.9 8.0 %collective-permute-start.3 = (bf16[136,512]{1,0:T(8,128)(2,1)S(1)}, bf16[136,512]{1,0:T(8,128)(2,1)S(1)}, u32[]{:S(2)}, u32[]{:S(2)}) collective-permute-start(bf16[136,512]{1,0:T(8,128)(2,1)S(1)} %pad_maximum_fusion.1), channel_id=1, source_target_pairs={{56,0},{0,8},{8,16},{16,24},{24,32},{32,40},{40,48},{48,56},{120,6... | collective-permute-start | bytes 417800 | tf_op jit(solution)/shard_map/ppermute | solution.py:20
  14.9 7.9 %collective-permute-start = (bf16[136,512]{1,0:T(8,128)(2,1)S(1)}, bf16[136,512]{1,0:T(8,128)(2,1)S(1)}, u32[]{:S(2)}, u32[]{:S(2)}) collective-permute-start(bf16[136,512]{1,0:T(8,128)(2,1)S(1)} %pad_maximum_fusion.1), channel_id=1, source_target_pairs={{8,0},{16,8},{24,16},{32,24},{40,32},{48,40},{56,48},{0,56},{72,64... | collective-permute-start | bytes 417800 | tf_op jit(solution)/shard_map/ppermute | solution.py:20
  18.1 23.3 %collective-permute-start.10 = (bf16[4,128,512]{2,1,0:T(8,128)(2,1)S(1)}, bf16[4,128,512]{2,1,0:T(8,128)(2,1)S(1)}, u32[]{:S(2)}, u32[]{:S(2)}) collective-permute-start(bf16[4,128,512]{2,1,0:T(8,128)(2,1)S(1)} %pad_maximum_fusion.refs_1_), channel_id=1, source_target_pairs={{56,0},{0,8},{8,16},{16,24},{24,32},{32,40},{40,48},{48,56},{120,6... | collective-permute-start | bytes 1572872 | tf_op jit(solution)/shard_map/ppermute | solution.py:20
  20.1 21.3 %collective-permute-start.9 = (bf16[4,128,512]{2,1,0:T(8,128)(2,1)S(1)}, bf16[4,128,512]{2,1,0:T(8,128)(2,1)}, u32[]{:S(2)}, u32[]{:S(2)}) collective-permute-start(bf16[4,128,512]{2,1,0:T(8,128)(2,1)S(1)} %pad_maximum_fusion.refs_1_), channel_id=1, source_target_pairs={{8,0},{16,8},{24,16},{32,24},{40,32},{48,40},{56,48},{0,56},{72,64... | collective-permute-start | bytes 1572872 | tf_op jit(solution)/shard_map/ppermute | solution.py:20
  20.9 12.8 %collective-permute-start.4 = (bf16[136,512]{1,0:T(8,128)(2,1)S(1)}, bf16[136,512]{1,0:T(8,128)(2,1)S(1)}, u32[]{:S(2)}, u32[]{:S(2)}) collective-permute-start(bf16[136,512]{1,0:T(8,128)(2,1)S(1)} %collective-permute-done.3), channel_id=1, source_target_pairs={{56,0},{0,8},{8,16},{16,24},{24,32},{32,40},{40,48},{48,56},{120,6... | collective-permute-start | bytes 417800 | tf_op jit(solution)/shard_map/ppermute | solution.py:20
  22.8 12.5 %collective-permute-start.1 = (bf16[136,512]{1,0:T(8,128)(2,1)S(1)}, bf16[136,512]{1,0:T(8,128)(2,1)S(1)}, u32[]{:S(2)}, u32[]{:S(2)}) collective-permute-start(bf16[136,512]{1,0:T(8,128)(2,1)S(1)} %collective-permute-done), channel_id=1, source_target_pairs={{8,0},{16,8},{24,16},{32,24},{40,32},{48,40},{56,48},{0,56},{72,64... | collective-permute-start | bytes 417800 | tf_op jit(solution)/shard_map/ppermute | solution.py:20
  33.7 7.0 %collective-permute-start.5 = (bf16[136,512]{1,0:T(8,128)(2,1)S(1)}, bf16[136,512]{1,0:T(8,128)(2,1)S(1)}, u32[]{:S(2)}, u32[]{:S(2)}) collective-permute-start(bf16[136,512]{1,0:T(8,128)(2,1)S(1)} %collective-permute-done.4), channel_id=1, source_target_pairs={{56,0},{0,8},{8,16},{16,24},{24,32},{32,40},{40,48},{48,56},{120,6... | collective-permute-start | bytes 417800 | tf_op jit(solution)/shard_map/ppermute | solution.py:20
  35.3 6.1 %collective-permute-start.2 = (bf16[136,512]{1,0:T(8,128)(2,1)S(1)}, bf16[136,512]{1,0:T(8,128)(2,1)S(1)}, u32[]{:S(2)}, u32[]{:S(2)}) collective-permute-start(bf16[136,512]{1,0:T(8,128)(2,1)S(1)} %collective-permute-done.1), channel_id=1, source_target_pairs={{8,0},{16,8},{24,16},{32,24},{40,32},{48,40},{56,48},{0,56},{72,64... | collective-permute-start | bytes 417800 | tf_op jit(solution)/shard_map/ppermute | solution.py:20
  41.4 16.7 %copy-start.2 = (bf16[4,128,512]{2,1,0:T(8,128)(2,1)}, bf16[4,128,512]{2,1,0:T(8,128)(2,1)S(1)}, u32[]{:S(2)}) copy-start(bf16[4,128,512]{2,1,0:T(8,128)(2,1)S(1)} %collective-permute-done.10.refs_3_) | copy-start | bytes 1572868
  41.5 7.2 %collective-permute-start.14 = (bf16[68,512]{1,0:T(8,128)(2,1)S(1)}, bf16[68,512]{1,0:T(8,128)(2,1)S(1)}, u32[]{:S(2)}, u32[]{:S(2)}) collective-permute-start(bf16[68,512]{1,0:T(8,128)(2,1)S(1)} %slice.42), channel_id=1, source_target_pairs={{56,0},{0,8},{8,16},{16,24},{24,32},{32,40},{40,48},{48,56},{120,6... | collective-permute-start | bytes 208904 | tf_op jit(solution)/shard_map/ppermute | solution.py:20
  44.8 6.4 %collective-permute-start.13 = (bf16[68,512]{1,0:T(8,128)(2,1)S(1)}, bf16[68,512]{1,0:T(8,128)(2,1)S(1)}, u32[]{:S(2)}, u32[]{:S(2)}) collective-permute-start(bf16[68,512]{1,0:T(8,128)(2,1)S(1)} %slice.41), channel_id=1, source_target_pairs={{8,0},{16,8},{24,16},{32,24},{40,32},{48,40},{56,48},{0,56},{72,64... | collective-permute-start | bytes 208904 | tf_op jit(solution)/shard_map/ppermute | solution.py:20
  44.8 13.3 %collective-permute-start.11 = (bf16[4,128,512]{2,1,0:T(8,128)(2,1)}, bf16[4,128,512]{2,1,0:T(8,128)(2,1)}, u32[]{:S(2)}, u32[]{:S(2)}) collective-permute-start(bf16[4,128,512]{2,1,0:T(8,128)(2,1)} %collective-permute-done.9.refs_2_), channel_id=1, source_target_pairs={{8,0},{16,8},{24,16},{32,24},{40,32},{48,40},{56,48},{0,56},{72,64... | collective-permute-start | bytes 1572872 | tf_op jit(solution)/shard_map/ppermute | solution.py:20
  47.4 10.7 %collective-permute-start.12 = (bf16[4,128,512]{2,1,0:T(8,128)(2,1)S(1)}, bf16[4,128,512]{2,1,0:T(8,128)(2,1)}, u32[]{:S(2)}, u32[]{:S(2)}) collective-permute-start(bf16[4,128,512]{2,1,0:T(8,128)(2,1)S(1)} %collective-permute-done.10.refs_3_), channel_id=1, source_target_pairs={{56,0},{0,8},{8,16},{16,24},{24,32},{32,40},{40,48},{48,56},{120,6... | collective-permute-start | bytes 1572872 | tf_op jit(solution)/shard_map/ppermute | solution.py:20
  53.9 25.2 %collective-permute-start.16 = (bf16[8,136,512]{2,1,0:T(8,128)(2,1)}, bf16[8,136,512]{2,1,0:T(8,128)(2,1)S(1)}, u32[]{:S(2)}, u32[]{:S(2)}) collective-permute-start(bf16[8,136,512]{2,1,0:T(8,128)(2,1)} %bitcast_dynamic-update-slice_fusion.refs_0_), channel_id=1, source_target_pairs={{192,0},{200,8},{208,16},{216,24},{224,32},{232,40},{240,48},{248,... | collective-permute-start | bytes 3342344 | tf_op jit(solution)/shard_map/ppermute | solution.py:20
  56.1 23.8 %collective-permute-start.15 = (bf16[8,136,512]{2,1,0:T(8,128)(2,1)}, bf16[8,136,512]{2,1,0:T(8,128)(2,1)S(1)}, u32[]{:S(2)}, u32[]{:S(2)}) collective-permute-start(bf16[8,136,512]{2,1,0:T(8,128)(2,1)} %bitcast_dynamic-update-slice_fusion.refs_0_), channel_id=1, source_target_pairs={{64,0},{72,8},{80,16},{88,24},{96,32},{104,40},{112,48},{120,56},{... | collective-permute-start | bytes 3342344 | tf_op jit(solution)/shard_map/ppermute | solution.py:20
  59.3 26.7 %collective-permute-start.19 = (bf16[4,128,512]{2,1,0:T(8,128)(2,1)}, bf16[4,128,512]{2,1,0:T(8,128)(2,1)S(1)}, u32[]{:S(2)}, u32[]{:S(2)}) collective-permute-start(bf16[4,128,512]{2,1,0:T(8,128)(2,1)} %collective-permute-done.11.refs_0_), channel_id=1, source_target_pairs={{8,0},{16,8},{24,16},{32,24},{40,32},{48,40},{56,48},{0,56},{72,64... | collective-permute-start | bytes 1572872 | tf_op jit(solution)/shard_map/ppermute | solution.py:20
  62.3 23.8 %collective-permute-start.20 = (bf16[4,128,512]{2,1,0:T(8,128)(2,1)}, bf16[4,128,512]{2,1,0:T(8,128)(2,1)}, u32[]{:S(2)}, u32[]{:S(2)}) collective-permute-start(bf16[4,128,512]{2,1,0:T(8,128)(2,1)} %collective-permute-done.12.refs_1_), channel_id=1, source_target_pairs={{56,0},{0,8},{8,16},{16,24},{24,32},{32,40},{40,48},{48,56},{120,6... | collective-permute-start | bytes 1572872 | tf_op jit(solution)/shard_map/ppermute | solution.py:20
  64.1 3.4 %copy-start = (bf16[512,8192]{1,0:T(8,128)(2,1)S(1)}, bf16[512,8192]{1,0:T(8,128)(2,1)}, u32[]{:S(2)}) copy-start(bf16[512,8192]{1,0:T(8,128)(2,1)} %all-gather.2.cloned.1.call-done.hidden) | copy-start | bytes 25165828
  67.5 1.0 copy-start.3
  80.0 11.3 %collective-permute-start.18 = (bf16[4,136,512]{2,1,0:T(8,128)(2,1)S(1)}, bf16[4,136,512]{2,1,0:T(8,128)(2,1)S(1)}, u32[]{:S(2)}, u32[]{:S(2)}) collective-permute-start(bf16[4,136,512]{2,1,0:T(8,128)(2,1)S(1)} %slice.44), channel_id=1, source_target_pairs={{192,0},{200,8},{208,16},{216,24},{224,32},{232,40},{240,48},{248,... | collective-permute-start | bytes 1671176 | tf_op jit(solution)/shard_map/ppermute | solution.py:20
  80.6 10.7 %collective-permute-start.17 = (bf16[4,136,512]{2,1,0:T(8,128)(2,1)S(1)}, bf16[4,136,512]{2,1,0:T(8,128)(2,1)S(1)}, u32[]{:S(2)}, u32[]{:S(2)}) collective-permute-start(bf16[4,136,512]{2,1,0:T(8,128)(2,1)S(1)} %slice.43), channel_id=1, source_target_pairs={{64,0},{72,8},{80,16},{88,24},{96,32},{104,40},{112,48},{120,56},{... | collective-permute-start | bytes 1671176 | tf_op jit(solution)/shard_map/ppermute | solution.py:20
  87.0 9.3 %slice-start = ((s8[8388608]{0:T(1024)(128)(4,1)}), s8[4194304]{0:T(1024)(128)(4,1)S(1)}, s32[]{:S(2)}) async-start(s8[8388608]{0:T(1024)(128)(4,1)} %bitcast.37), calls=%async_computation.3 | async-start | bytes 8388608
  87.0 9.2 %collective-permute-start.21 = (bf16[2,128,512]{2,1,0:T(8,128)(2,1)S(1)}, bf16[2,128,512]{2,1,0:T(8,128)(2,1)S(1)}, u32[]{:S(2)}, u32[]{:S(2)}) collective-permute-start(bf16[2,128,512]{2,1,0:T(8,128)(2,1)S(1)} %slice.45), channel_id=1, source_target_pairs={{8,0},{16,8},{24,16},{32,24},{40,32},{48,40},{56,48},{0,56},{72,64... | collective-permute-start | bytes 786440 | tf_op jit(solution)/shard_map/ppermute | solution.py:20
  87.1 9.1 %collective-permute-start.22 = (bf16[2,128,512]{2,1,0:T(8,128)(2,1)S(1)}, bf16[2,128,512]{2,1,0:T(8,128)(2,1)S(1)}, u32[]{:S(2)}, u32[]{:S(2)}) collective-permute-start(bf16[2,128,512]{2,1,0:T(8,128)(2,1)S(1)} %slice.46), channel_id=1, source_target_pairs={{56,0},{0,8},{8,16},{16,24},{24,32},{32,40},{40,48},{48,56},{120,6... | collective-permute-start | bytes 786440 | tf_op jit(solution)/shard_map/ppermute | solution.py:20
  89.3 6.9 %slice-start.1 = ((s8[8388608]{0:T(1024)(128)(4,1)}), s8[4194304]{0:T(1024)(128)(4,1)S(1)}, s32[]{:S(2)}) async-start(s8[8388608]{0:T(1024)(128)(4,1)} %bitcast.37), calls=%async_computation.4 | async-start | bytes 8388608
  120.0 23.0 %copy-start.4 = (f32[512]{0:T(512)S(1)}, f32[512]{0:T(512)}, u32[]{:S(2)}) copy-start(f32[512]{0:T(512)} %param.9) | copy-start | bytes 6148
  124.9 18.1 %copy-start.1 = (bf16[512,512]{1,0:T(8,128)(2,1)S(1)}, bf16[512,512]{1,0:T(8,128)(2,1)}, u32[]{:S(2)}) copy-start(bf16[512,512]{1,0:T(8,128)(2,1)} %gate.1) | copy-start | bytes 1572868
  (1 other events, 0.9 us)
Sparse Core Ops, SparseCore 0:
  9.2 54.8 all-gather.1

commit v4 on v3

--- a/solution.py
+++ b/solution.py
@@ -10,6 +10,7 @@
 NY, NZ = 4, 8
 FIRST = 128
 TAP_ROWS = 8
+ORDER = (0, 1, 7, 2, 6, 3, 5, 4)
 VMEM_LIMIT = 16 * 1024 * 1024
 
 
@@ -106,17 +107,19 @@
         (line[3], line[-3], ring[1], ring[-1])
     )
     line[4] = jnp.concatenate(halves(line[3], line[-3], 0, 1), axis=0)
-    mine = jnp.stack([line[k] for k in (0, 1, 2, 3, 4, -3, -2, -1)])
+    mine = jnp.stack([line[k] for k in (0, 1, -1, 2, -2, 3, -3, 4)])
     above, below = take_from(mine, 1, 0), take_from(mine, -1, 0)
 
     def row(dy, start=0, stop=NZ):
-        return [(dy, dz, 0) for dz in range(start, stop)]
+        return [(dy, dz, 0) for dz in ORDER[start:stop]]
 
     def stack(dz, start=0, stop=NY):
         return [(dy, dz % NZ, 1) for dy in range(start, stop)]
 
     ring[2], ring[-2] = take_from(ring[1], 0, 1), take_from(ring[-1], 0, -1)
-    place, ring[2], ring[-2] = lax.optimization_barrier((place, ring[2], ring[-2]))
+    place, hidden, ring[2], ring[-2] = lax.optimization_barrier(
+        (place, hidden, ring[2], ring[-2])
+    )
     starts = starts_of(place)
     starts, ring[2], ring[-2] = lax.optimization_barrier((starts, ring[2], ring[-2]))
     held = [(mine, row(0))] + [(ring[k], stack(k)) for k in (0, 1, -1)]
@@ -144,17 +147,21 @@
     def block(i):
         dy = lax.rem(lax.div(i, NZ) - y + NY, NY)
         dz = lax.rem(lax.rem(i, NZ) - z + NZ, NZ)
-        return taps[dy, dz]
+        at = jnp.where(dz == 0, 0, jnp.where(dz <= 4, 2 * dz - 1, 16 - 2 * dz))
+        return taps[dy, at]
 
     def chunk(i, carry):
         before = jnp.where(i == 0, 0.0, block(jnp.maximum(i - 1, 0))[:, step - rows :])
         window = jnp.concatenate([before, block(i)], axis=1)
-        window = jnp.broadcast_to(window, (rows, step + rows))
-        rolled = pltpu.roll(window, 0, 1, stride=1, stride_axis=0)
-        out[:, pl.ds(pl.multiple_of(i * step, step), step)] = rolled[:, rows:].astype(jnp.bfloat16)
+        half = rows // 2
+        window = jnp.broadcast_to(window, (half, step + rows))
+        rolled = pltpu.roll(window, 0, 1, stride=1, stride_axis=0).astype(jnp.bfloat16)
+        start = pl.multiple_of(i * step, step)
+        out[:half, pl.ds(start, step)] = rolled[:, rows:]
+        out[half:, pl.ds(start, step)] = rolled[:, half : step + half]
         return carry
 
-    lax.fori_loop(0, out.shape[1] // step, chunk, 0)
+    lax.fori_loop(0, out.shape[1] // step, chunk, 0, unroll=4)
 
 
 def strip(place, taps):

time: 153 us -> 150 us (0.980)
  local copies, waits for them, and re-layouts: 10.7 us -> 5.35 us
  waiting for transfers between devices: 26.3 us -> 31 us
  Pallas kernels: 23.3 us -> 20.6 us
  blocking collectives: 40.2 us -> 42.2 us
    all_gather x1, waiting for transfers between devices: 1.83 us -> 6.01 us  [on_device(): whole = lax.all_gather(hidden, 'tp', axis=1, tiled=True)]
    unnamed x23 -> x16, local copies, waits for them, and re-layouts: 8.01 us -> 4.31 us
    pallas_call x1, Pallas kernels: 4.8 us -> 2.8 us  [strip(): pl.pallas_call(strip_kernel, out_shape=jax.ShapeDtypeStruct((256, 16384),...]
    all_to_all x1, blocking collectives: 22.2 us -> 23.8 us  [on_device(): lax.all_to_all(value, 'seq', split_axis=0, concat_axis=0, tiled=True)]
  transfers between devices with their start and end apart: 24 -> 24, of which waited for: 10 -> 11; matrix products, arithmetic and copies ran while one was open for 5% -> 4% of each run, Pallas kernels for 10% -> 8%
where the time goes in v4:
time: 150 us
  blocking collectives  42.2 us (28%)
  starting transfers between devices  35.3 us (24%)
  waiting for transfers between devices  31 us (21%)
  Pallas kernels  20.6 us (14%)
  between operations  13.6 us (9%)
  local copies, waits for them, and re-layouts  5.35 us (4%)
  other arithmetic  1.58 us (1%)
    ppermute x23, starting transfers between devices, take_from(): return lax.ppermute(array, 'seq', pairs)  35.3 us
    ppermute x23, waiting for transfers between devices, take_from(): return lax.ppermute(array, 'seq', pairs)  24.3 us
    all_to_all x1, blocking collectives, on_device(): lax.all_to_all(value, 'seq', split_axis=0, concat_axis=0, tiled=True)  23.8 us
    all_to_all x1, blocking collectives, on_device(): lax.all_to_all(conv, 'seq', split_axis=0, concat_axis=0, tiled=True)  18.4 us
    pallas_call x5, Pallas kernels, project(): pl.pallas_call(functools.partial(project_kernel, parts, before is None, l...  9.51 us
    all_gather x1, waiting for transfers between devices, on_device(): whole = lax.all_gather(hidden, 'tp', axis=1, tiled=True)  6.01 us
    pallas_call x1, Pallas kernels, convolve(): pl.pallas_call(conv_kernel, out_shape=jax.ShapeDtypeStruct((32, 16, 512),...  4.88 us
    unnamed x16, local copies, waits for them, and re-layouts  4.31 us
  transfers between devices with their start and end apart: 24, of which 11 were waited for; matrix products, arithmetic and copies ran while one was open for 4% of the time, Pallas kernels for 8%

profile of v4, /device:TPU:32, one launch (start us, length us, event | category | flops | bytes accessed | tf_op | source)
XLA Modules:
  0.0 149.6 jit_solution(1223108710063397428)
XLA Ops:
  7.5 3.3 %collective-permute-start.7 = (bf16[128,512]{1,0:T(8,128)(2,1)S(1)}, bf16[128,512]{1,0:T(8,128)(2,1)S(1)}, u32[]{:S(2)}, u32[]{:S(2)}) collective-permute-start(bf16[128,512]{1,0:T(8,128)(2,1)S(1)} %get-tuple-element.44), channel_id=1, source_target_pairs={{128,0},{136,8},{144,16},{152,24},{160,32},{168,40},{176,48},{184,... | collective-permute-start | bytes 393224 | tf_op jit(solution)/shard_map/ppermute | solution.py:21
  12.9 2.0 %collective-permute-start.3 = (bf16[136,512]{1,0:T(8,128)(2,1)S(1)}, bf16[136,512]{1,0:T(8,128)(2,1)S(1)}, u32[]{:S(2)}, u32[]{:S(2)}) collective-permute-start(bf16[136,512]{1,0:T(8,128)(2,1)S(1)} %pad_maximum_fusion.1), channel_id=1, source_target_pairs={{56,0},{0,8},{8,16},{16,24},{24,32},{32,40},{40,48},{48,56},{120,6... | collective-permute-start | bytes 417800 | tf_op jit(solution)/shard_map/ppermute | solution.py:21
  15.7 1.8 %collective-permute-done.6 = bf16[128,512]{1,0:T(8,128)(2,1)S(1)} collective-permute-done((bf16[128,512]{1,0:T(8,128)(2,1)S(1)}, bf16[128,512]{1,0:T(8,128)(2,1)S(1)}, u32[]{:S(2)}, u32[]{:S(2)}) %collective-permute-start.6) | collective-permute-done | bytes 131104 | tf_op jit(solution)/shard_map/ppermute | solution.py:21
  18.1 2.0 %collective-permute-start.10 = (bf16[4,128,512]{2,1,0:T(8,128)(2,1)S(1)}, bf16[4,128,512]{2,1,0:T(8,128)(2,1)S(1)}, u32[]{:S(2)}, u32[]{:S(2)}) collective-permute-start(bf16[4,128,512]{2,1,0:T(8,128)(2,1)S(1)} %pad_maximum_fusion.refs_1_), channel_id=1, source_target_pairs={{56,0},{0,8},{8,16},{16,24},{24,32},{32,40},{40,48},{48,56},{120,6... | collective-permute-start | bytes 1572872 | tf_op jit(solution)/shard_map/ppermute | solution.py:21
  20.2 1.9 %collective-permute-start.4 = (bf16[136,512]{1,0:T(8,128)(2,1)S(1)}, bf16[136,512]{1,0:T(8,128)(2,1)S(1)}, u32[]{:S(2)}, u32[]{:S(2)}) collective-permute-start(bf16[136,512]{1,0:T(8,128)(2,1)S(1)} %collective-permute-done.3), channel_id=1, source_target_pairs={{56,0},{0,8},{8,16},{16,24},{24,32},{32,40},{40,48},{48,56},{120,6... | collective-permute-start | bytes 417800 | tf_op jit(solution)/shard_map/ppermute | solution.py:21
  22.1 2.2 %collective-permute-start.1 = (bf16[136,512]{1,0:T(8,128)(2,1)S(1)}, bf16[136,512]{1,0:T(8,128)(2,1)S(1)}, u32[]{:S(2)}, u32[]{:S(2)}) collective-permute-start(bf16[136,512]{1,0:T(8,128)(2,1)S(1)} %collective-permute-done), channel_id=1, source_target_pairs={{8,0},{16,8},{24,16},{32,24},{40,32},{48,40},{56,48},{0,56},{72,64... | collective-permute-start | bytes 417800 | tf_op jit(solution)/shard_map/ppermute | solution.py:21
  25.7 8.0 %collective-permute-done.4 = bf16[136,512]{1,0:T(8,128)(2,1)S(1)} collective-permute-done((bf16[136,512]{1,0:T(8,128)(2,1)S(1)}, bf16[136,512]{1,0:T(8,128)(2,1)S(1)}, u32[]{:S(2)}, u32[]{:S(2)}) %collective-permute-start.4) | collective-permute-done | bytes 139296 | tf_op jit(solution)/shard_map/ppermute | solution.py:21
  33.7 1.7 %collective-permute-start.5 = (bf16[136,512]{1,0:T(8,128)(2,1)S(1)}, bf16[136,512]{1,0:T(8,128)(2,1)S(1)}, u32[]{:S(2)}, u32[]{:S(2)}) collective-permute-start(bf16[136,512]{1,0:T(8,128)(2,1)S(1)} %collective-permute-done.4), channel_id=1, source_target_pairs={{56,0},{0,8},{8,16},{16,24},{24,32},{32,40},{40,48},{48,56},{120,6... | collective-permute-start | bytes 417800 | tf_op jit(solution)/shard_map/ppermute | solution.py:21
  35.3 2.3 %collective-permute-start.2 = (bf16[136,512]{1,0:T(8,128)(2,1)S(1)}, bf16[136,512]{1,0:T(8,128)(2,1)S(1)}, u32[]{:S(2)}, u32[]{:S(2)}) collective-permute-start(bf16[136,512]{1,0:T(8,128)(2,1)S(1)} %collective-permute-done.1), channel_id=1, source_target_pairs={{8,0},{16,8},{24,16},{32,24},{40,32},{48,40},{56,48},{0,56},{72,64... | collective-permute-start | bytes 417800 | tf_op jit(solution)/shard_map/ppermute | solution.py:21
  39.0 1.7 %collective-permute-done.5 = bf16[136,512]{1,0:T(8,128)(2,1)S(1)} collective-permute-done((bf16[136,512]{1,0:T(8,128)(2,1)S(1)}, bf16[136,512]{1,0:T(8,128)(2,1)S(1)}, u32[]{:S(2)}, u32[]{:S(2)}) %collective-permute-start.5) | collective-permute-done | bytes 139296 | tf_op jit(solution)/shard_map/ppermute | solution.py:21
  41.4 3.3 %collective-permute-start.14 = (bf16[68,512]{1,0:T(8,128)(2,1)S(1)}, bf16[68,512]{1,0:T(8,128)(2,1)S(1)}, u32[]{:S(2)}, u32[]{:S(2)}) collective-permute-start(bf16[68,512]{1,0:T(8,128)(2,1)S(1)} %slice.42), channel_id=1, source_target_pairs={{56,0},{0,8},{8,16},{16,24},{24,32},{32,40},{40,48},{48,56},{120,6... | collective-permute-start | bytes 208904 | tf_op jit(solution)/shard_map/ppermute | solution.py:21
  44.8 2.6 %collective-permute-start.11 = (bf16[4,128,512]{2,1,0:T(8,128)(2,1)}, bf16[4,128,512]{2,1,0:T(8,128)(2,1)}, u32[]{:S(2)}, u32[]{:S(2)}) collective-permute-start(bf16[4,128,512]{2,1,0:T(8,128)(2,1)} %collective-permute-done.9.refs_2_), channel_id=1, source_target_pairs={{8,0},{16,8},{24,16},{32,24},{40,32},{48,40},{56,48},{0,56},{72,64... | collective-permute-start | bytes 1572872 | tf_op jit(solution)/shard_map/ppermute | solution.py:21
  49.3 1.9 %collective-permute-done.13 = bf16[68,512]{1,0:T(8,128)(2,1)S(1)} collective-permute-done((bf16[68,512]{1,0:T(8,128)(2,1)S(1)}, bf16[68,512]{1,0:T(8,128)(2,1)S(1)}, u32[]{:S(2)}, u32[]{:S(2)}) %collective-permute-start.13) | collective-permute-done | bytes 69664 | tf_op jit(solution)/shard_map/ppermute | solution.py:21
  51.9 2.3 %collective-permute-start.16 = (bf16[8,136,512]{2,1,0:T(8,128)(2,1)}, bf16[8,136,512]{2,1,0:T(8,128)(2,1)S(1)}, u32[]{:S(2)}, u32[]{:S(2)}) collective-permute-start(bf16[8,136,512]{2,1,0:T(8,128)(2,1)} %fusion.refs_0_), channel_id=1, source_target_pairs={{192,0},{200,8},{208,16},{216,24},{224,32},{232,40},{240,48},{248,... | collective-permute-start | bytes 3342344 | tf_op jit(solution)/shard_map/ppermute | solution.py:21
  54.1 1.4 collective-permute-start.15
  55.6 2.5 %collective-permute-done.11.refs_0_ = bf16[4,128,512]{2,1,0:T(8,128)(2,1)} collective-permute-done((bf16[4,128,512]{2,1,0:T(8,128)(2,1)}, bf16[4,128,512]{2,1,0:T(8,128)(2,1)}, u32[]{:S(2)}, u32[]{:S(2)}) %collective-permute-start.11) | collective-permute-done | bytes 524320 | tf_op jit(solution)/shard_map/ppermute | solution.py:21
  58.1 6.0 %all-gather.2.cloned.1.call-done.hidden = bf16[512,8192]{1,0:T(8,128)(2,1)} async-done(((bf16[512,1024]{1,0:T(8,128)(2,1)}), bf16[512,8192]{1,0:T(8,128)(2,1)}) %all-gather.2.cloned.1.call-update) | async-done | bytes 8388624 | tf_op jit(solution)/shard_map/all_gather | solution.py:249
  64.1 1.2 starts.1
  65.8 1.6 %collective-permute-start.20 = (bf16[4,128,512]{2,1,0:T(8,128)(2,1)}, bf16[4,128,512]{2,1,0:T(8,128)(2,1)S(1)}, u32[]{:S(2)}, u32[]{:S(2)}) collective-permute-start(bf16[4,128,512]{2,1,0:T(8,128)(2,1)} %collective-permute-done.12.refs_1_), channel_id=1, source_target_pairs={{56,0},{0,8},{8,16},{16,24},{24,32},{32,40},{40,48},{48,56},{120,6... | collective-permute-start | bytes 1572872 | tf_op jit(solution)/shard_map/ppermute | solution.py:21
  67.5 2.9 %project_20.1.refs_2_ = f32[512,512]{1,0:T(8,128)S(1)} custom-call(s32[32]{0:T(128)S(1)} %starts.1, bf16[512,8192]{1,0:T(8,128)(2,1)S(1)} %copy-done, bf16[8,136,512]{2,1,0:T(8,128)(2,1)} %fusion.refs_0_, bf16[4,128,512]{2,1,0:T(8,128)(2,1)S(1)} %pad_maximum_fusion.refs_1_, bf16[4,128,512]{2,1,0:T(8,128)(2,1)} %collective-permute-done.9.refs_2_, ...), custom_call_target="tpu_custom_call" | custom-call | flops 1342177280 | bytes 5242880 | tf_op jit(solution)/shard_map/project_20/pallas_call | solution.py:77
  70.4 1.9 %project_8.2.refs_2_ = f32[512,512]{1,0:T(8,128)S(1)} custom-call(s32[32]{0:T(128)S(1)} %starts.1, bf16[512,8192]{1,0:T(8,128)(2,1)S(1)} %copy-done, bf16[4,128,512]{2,1,0:T(8,128)(2,1)} %collective-permute-done.11.refs_0_, bf16[4,128,512]{2,1,0:T(8,128)(2,1)} %collective-permute-done.12.refs_1_, f32[512,512]{1,0:T(8,128)S(1)} %project_20.1.refs_2_), custom_call_target="tpu_custom_call" | custom-call | flops 536870912 | bytes 2097152 | tf_op jit(solution)/shard_map/project_8/pallas_call | solution.py:77
  72.3 4.7 %collective-permute-done.16.refs_1_ = bf16[8,136,512]{2,1,0:T(8,128)(2,1)S(1)} collective-permute-done((bf16[8,136,512]{2,1,0:T(8,128)(2,1)}, bf16[8,136,512]{2,1,0:T(8,128)(2,1)S(1)}, u32[]{:S(2)}, u32[]{:S(2)}) %collective-permute-start.16) | collective-permute-done | bytes 1114144 | tf_op jit(solution)/shard_map/ppermute | solution.py:21
  78.3 2.5 %collective-permute-start.17 = (bf16[4,136,512]{2,1,0:T(8,128)(2,1)S(1)}, bf16[4,136,512]{2,1,0:T(8,128)(2,1)S(1)}, u32[]{:S(2)}, u32[]{:S(2)}) collective-permute-start(bf16[4,136,512]{2,1,0:T(8,128)(2,1)S(1)} %slice.43), channel_id=1, source_target_pairs={{64,0},{72,8},{80,16},{88,24},{96,32},{104,40},{112,48},{120,56},{... | collective-permute-start | bytes 1671176 | tf_op jit(solution)/shard_map/ppermute | solution.py:21
  81.6 1.8 %project_16.1.refs_2_ = f32[512,512]{1,0:T(8,128)S(1)} custom-call(s32[32]{0:T(128)S(1)} %starts.1, bf16[512,8192]{1,0:T(8,128)(2,1)S(1)} %copy-done, bf16[8,136,512]{2,1,0:T(8,128)(2,1)S(1)} %collective-permute-done.15.refs_0_, bf16[8,136,512]{2,1,0:T(8,128)(2,1)S(1)} %collective-permute-done.16.refs_1_, f32[512,512]{1,0:T(8,128)S(1)} %project_8.2.refs_2_), custom_call_target="tpu_custom_call" | custom-call | flops 1073741824 | bytes 4194304 | tf_op jit(solution)/shard_map/project_16/pallas_call | solution.py:77
  85.6 1.3 project_8.3.refs_4_
  86.8 2.0 %collective-permute-done.18.refs_1_ = bf16[4,136,512]{2,1,0:T(8,128)(2,1)S(1)} collective-permute-done((bf16[4,136,512]{2,1,0:T(8,128)(2,1)S(1)}, bf16[4,136,512]{2,1,0:T(8,128)(2,1)S(1)}, u32[]{:S(2)}, u32[]{:S(2)}) %collective-permute-start.18) | collective-permute-done | bytes 557088 | tf_op jit(solution)/shard_map/ppermute | solution.py:21
  89.0 2.8 %strip.1.strip_ref = bf16[256,16384]{1,0:T(8,128)(2,1)S(1)} custom-call(s32[3]{0:T(128)S(1)} %pad_add_fusion.place, f32[4,8,1,512]{3,2,1,0:T(1,128)S(1)} %fusion.4.taps), custom_call_target="tpu_custom_call" | custom-call | flops 10485760 | bytes 8388608 | tf_op jit(solution)/shard_map/strip/pallas_call | solution.py:169
  91.8 1.6 %project_12.1 = bf16[32,16,512]{2,1,0:T(8,128)(2,1)S(1)} custom-call(s32[32]{0:T(128)S(1)} %starts.1, bf16[512,8192]{1,0:T(8,128)(2,1)S(1)} %copy-done, bf16[4,136,512]{2,1,0:T(8,128)(2,1)S(1)} %collective-permute-done.17.refs_0_, bf16[4,136,512]{2,1,0:T(8,128)(2,1)S(1)} %collective-permute-done.18.refs_1_, ...), custom_call_target="tpu_custom_call" | custom-call | flops 805306368 | bytes 3145728 | tf_op jit(solution)/shard_map/project_12/pallas_call | solution.py:77
  93.4 23.8 %all_to_all.10.value = bf16[32,16,512]{2,1,0:T(8,128)(2,1)S(1)} all-to-all(bf16[32,16,512]{2,1,0:T(8,128)(2,1)S(1)} %project_12.1), channel_id=1, replica_groups=mesh['seq'=32,'tp'=8] {'seq'}, dimensions={0} | all-to-all | bytes 1048576 | tf_op jit(solution)/shard_map/all_to_all | solution.py:254
  117.2 4.9 %convolve.1 = bf16[32,16,512]{2,1,0:T(8,128)(2,1)S(1)} custom-call(bf16[32,16,512]{2,1,0:T(8,128)(2,1)S(1)} %all_to_all.10.value, bf16[256,16384]{1,0:T(8,128)(2,1)S(1)} %strip.1.strip_ref), custom_call_target="tpu_custom_call" | custom-call | flops 4499999744 | bytes 10485760 | tf_op jit(solution)/shard_map/convolve/pallas_call | solution.py:206
  122.1 18.4 %all_to_all.11 = bf16[32,16,512]{2,1,0:T(8,128)(2,1)S(1)} all-to-all(bf16[32,16,512]{2,1,0:T(8,128)(2,1)S(1)} %convolve.1), channel_id=1, replica_groups=mesh['seq'=32,'tp'=8] {'seq'}, dimensions={0} | all-to-all | bytes 1048576 | tf_op jit(solution)/shard_map/all_to_all | solution.py:256
  140.5 2.2 %mix.1 = bf16[512,512]{1,0:T(8,128)(2,1)} custom-call(bf16[512,512]{1,0:T(8,128)(2,1)S(1)} %bitcast.38, bf16[512,512]{1,0:T(8,128)(2,1)S(1)} %bitcast.37, f32[1,512]{1,0:T(1,128)S(1)} %bitcast.39, bf16[512,512]{1,0:T(8,128)(2,1)S(1)} %copy-done.1), custom_call_target="tpu_custom_call" | custom-call | tf_op jit(solution)/shard_map/mix/pallas_call | solution.py:230
  (64 shorter events, 15.7 us)
Async XLA Ops:
  6.5 0.9 copy-start.3
  6.5 6.3 %copy-start.4 = (bf16[512,4]{0,1:T(4,128)(2,1)S(1)}, bf16[512,4]{0,1:T(4,128)(2,1)}, u32[]{:S(2)}) copy-start(bf16[512,4]{0,1:T(4,128)(2,1)} %param.8) | copy-start | bytes 12292
  6.5 57.5 %all-gather.2.cloned.1.call-start = ((), (), s32[]{:S(2)}) async-start(), calls=%async_computation.2 | async-start | bytes 9437184 | tf_op jit(solution)/shard_map/all_gather | solution.py:249
  7.5 8.1 %collective-permute-start.7 = (bf16[128,512]{1,0:T(8,128)(2,1)S(1)}, bf16[128,512]{1,0:T(8,128)(2,1)S(1)}, u32[]{:S(2)}, u32[]{:S(2)}) collective-permute-start(bf16[128,512]{1,0:T(8,128)(2,1)S(1)} %get-tuple-element.44), channel_id=1, source_target_pairs={{128,0},{136,8},{144,16},{152,24},{160,32},{168,40},{176,48},{184,... | collective-permute-start | bytes 393224 | tf_op jit(solution)/shard_map/ppermute | solution.py:21
  10.8 6.7 %collective-permute-start.6 = (bf16[128,512]{1,0:T(8,128)(2,1)S(1)}, bf16[128,512]{1,0:T(8,128)(2,1)S(1)}, u32[]{:S(2)}, u32[]{:S(2)}) collective-permute-start(bf16[128,512]{1,0:T(8,128)(2,1)S(1)} %get-tuple-element.44), channel_id=1, source_target_pairs={{64,0},{72,8},{80,16},{88,24},{96,32},{104,40},{112,48},{120,56},{... | collective-permute-start | bytes 393224 | tf_op jit(solution)/shard_map/ppermute | solution.py:21
  11.9 6.2 %collective-permute-start.8 = (bf16[128,512]{1,0:T(8,128)(2,1)S(1)}, bf16[128,512]{1,0:T(8,128)(2,1)S(1)}, u32[]{:S(2)}, u32[]{:S(2)}) collective-permute-start(bf16[128,512]{1,0:T(8,128)(2,1)S(1)} %get-tuple-element.44), channel_id=1, source_target_pairs={{192,0},{200,8},{208,16},{216,24},{224,32},{232,40},{240,48},{248,... | collective-permute-start | bytes 393224 | tf_op jit(solution)/shard_map/ppermute | solution.py:21
  12.9 7.3 %collective-permute-start.3 = (bf16[136,512]{1,0:T(8,128)(2,1)S(1)}, bf16[136,512]{1,0:T(8,128)(2,1)S(1)}, u32[]{:S(2)}, u32[]{:S(2)}) collective-permute-start(bf16[136,512]{1,0:T(8,128)(2,1)S(1)} %pad_maximum_fusion.1), channel_id=1, source_target_pairs={{56,0},{0,8},{8,16},{16,24},{24,32},{32,40},{40,48},{48,56},{120,6... | collective-permute-start | bytes 417800 | tf_op jit(solution)/shard_map/ppermute | solution.py:21
  14.9 7.3 %collective-permute-start = (bf16[136,512]{1,0:T(8,128)(2,1)S(1)}, bf16[136,512]{1,0:T(8,128)(2,1)S(1)}, u32[]{:S(2)}, u32[]{:S(2)}) collective-permute-start(bf16[136,512]{1,0:T(8,128)(2,1)S(1)} %pad_maximum_fusion.1), channel_id=1, source_target_pairs={{8,0},{16,8},{24,16},{32,24},{40,32},{48,40},{56,48},{0,56},{72,64... | collective-permute-start | bytes 417800 | tf_op jit(solution)/shard_map/ppermute | solution.py:21
  18.1 23.3 %collective-permute-start.10 = (bf16[4,128,512]{2,1,0:T(8,128)(2,1)S(1)}, bf16[4,128,512]{2,1,0:T(8,128)(2,1)S(1)}, u32[]{:S(2)}, u32[]{:S(2)}) collective-permute-start(bf16[4,128,512]{2,1,0:T(8,128)(2,1)S(1)} %pad_maximum_fusion.refs_1_), channel_id=1, source_target_pairs={{56,0},{0,8},{8,16},{16,24},{24,32},{32,40},{40,48},{48,56},{120,6... | collective-permute-start | bytes 1572872 | tf_op jit(solution)/shard_map/ppermute | solution.py:21
  20.1 21.3 %collective-permute-start.9 = (bf16[4,128,512]{2,1,0:T(8,128)(2,1)S(1)}, bf16[4,128,512]{2,1,0:T(8,128)(2,1)}, u32[]{:S(2)}, u32[]{:S(2)}) collective-permute-start(bf16[4,128,512]{2,1,0:T(8,128)(2,1)S(1)} %pad_maximum_fusion.refs_1_), channel_id=1, source_target_pairs={{8,0},{16,8},{24,16},{32,24},{40,32},{48,40},{56,48},{0,56},{72,64... | collective-permute-start | bytes 1572872 | tf_op jit(solution)/shard_map/ppermute | solution.py:21
  20.2 13.5 %collective-permute-start.4 = (bf16[136,512]{1,0:T(8,128)(2,1)S(1)}, bf16[136,512]{1,0:T(8,128)(2,1)S(1)}, u32[]{:S(2)}, u32[]{:S(2)}) collective-permute-start(bf16[136,512]{1,0:T(8,128)(2,1)S(1)} %collective-permute-done.3), channel_id=1, source_target_pairs={{56,0},{0,8},{8,16},{16,24},{24,32},{32,40},{40,48},{48,56},{120,6... | collective-permute-start | bytes 417800 | tf_op jit(solution)/shard_map/ppermute | solution.py:21
  22.1 13.2 %collective-permute-start.1 = (bf16[136,512]{1,0:T(8,128)(2,1)S(1)}, bf16[136,512]{1,0:T(8,128)(2,1)S(1)}, u32[]{:S(2)}, u32[]{:S(2)}) collective-permute-start(bf16[136,512]{1,0:T(8,128)(2,1)S(1)} %collective-permute-done), channel_id=1, source_target_pairs={{8,0},{16,8},{24,16},{32,24},{40,32},{48,40},{56,48},{0,56},{72,64... | collective-permute-start | bytes 417800 | tf_op jit(solution)/shard_map/ppermute | solution.py:21
  33.7 7.0 %collective-permute-start.5 = (bf16[136,512]{1,0:T(8,128)(2,1)S(1)}, bf16[136,512]{1,0:T(8,128)(2,1)S(1)}, u32[]{:S(2)}, u32[]{:S(2)}) collective-permute-start(bf16[136,512]{1,0:T(8,128)(2,1)S(1)} %collective-permute-done.4), channel_id=1, source_target_pairs={{56,0},{0,8},{8,16},{16,24},{24,32},{32,40},{40,48},{48,56},{120,6... | collective-permute-start | bytes 417800 | tf_op jit(solution)/shard_map/ppermute | solution.py:21
  35.3 6.1 %collective-permute-start.2 = (bf16[136,512]{1,0:T(8,128)(2,1)S(1)}, bf16[136,512]{1,0:T(8,128)(2,1)S(1)}, u32[]{:S(2)}, u32[]{:S(2)}) collective-permute-start(bf16[136,512]{1,0:T(8,128)(2,1)S(1)} %collective-permute-done.1), channel_id=1, source_target_pairs={{8,0},{16,8},{24,16},{32,24},{40,32},{48,40},{56,48},{0,56},{72,64... | collective-permute-start | bytes 417800 | tf_op jit(solution)/shard_map/ppermute | solution.py:21
  41.4 7.9 %collective-permute-start.14 = (bf16[68,512]{1,0:T(8,128)(2,1)S(1)}, bf16[68,512]{1,0:T(8,128)(2,1)S(1)}, u32[]{:S(2)}, u32[]{:S(2)}) collective-permute-start(bf16[68,512]{1,0:T(8,128)(2,1)S(1)} %slice.42), channel_id=1, source_target_pairs={{56,0},{0,8},{8,16},{16,24},{24,32},{32,40},{40,48},{48,56},{120,6... | collective-permute-start | bytes 208904 | tf_op jit(solution)/shard_map/ppermute | solution.py:21
  44.8 6.4 %collective-permute-start.13 = (bf16[68,512]{1,0:T(8,128)(2,1)S(1)}, bf16[68,512]{1,0:T(8,128)(2,1)S(1)}, u32[]{:S(2)}, u32[]{:S(2)}) collective-permute-start(bf16[68,512]{1,0:T(8,128)(2,1)S(1)} %slice.41), channel_id=1, source_target_pairs={{8,0},{16,8},{24,16},{32,24},{40,32},{48,40},{56,48},{0,56},{72,64... | collective-permute-start | bytes 208904 | tf_op jit(solution)/shard_map/ppermute | solution.py:21
  44.8 13.3 %collective-permute-start.11 = (bf16[4,128,512]{2,1,0:T(8,128)(2,1)}, bf16[4,128,512]{2,1,0:T(8,128)(2,1)}, u32[]{:S(2)}, u32[]{:S(2)}) collective-permute-start(bf16[4,128,512]{2,1,0:T(8,128)(2,1)} %collective-permute-done.9.refs_2_), channel_id=1, source_target_pairs={{8,0},{16,8},{24,16},{32,24},{40,32},{48,40},{56,48},{0,56},{72,64... | collective-permute-start | bytes 1572872 | tf_op jit(solution)/shard_map/ppermute | solution.py:21
  47.4 10.7 %collective-permute-start.12 = (bf16[4,128,512]{2,1,0:T(8,128)(2,1)S(1)}, bf16[4,128,512]{2,1,0:T(8,128)(2,1)}, u32[]{:S(2)}, u32[]{:S(2)}) collective-permute-start(bf16[4,128,512]{2,1,0:T(8,128)(2,1)S(1)} %collective-permute-done.10.refs_3_), channel_id=1, source_target_pairs={{56,0},{0,8},{8,16},{16,24},{24,32},{32,40},{40,48},{48,56},{120,6... | collective-permute-start | bytes 1572872 | tf_op jit(solution)/shard_map/ppermute | solution.py:21
  51.9 25.2 %collective-permute-start.16 = (bf16[8,136,512]{2,1,0:T(8,128)(2,1)}, bf16[8,136,512]{2,1,0:T(8,128)(2,1)S(1)}, u32[]{:S(2)}, u32[]{:S(2)}) collective-permute-start(bf16[8,136,512]{2,1,0:T(8,128)(2,1)} %fusion.refs_0_), channel_id=1, source_target_pairs={{192,0},{200,8},{208,16},{216,24},{224,32},{232,40},{240,48},{248,... | collective-permute-start | bytes 3342344 | tf_op jit(solution)/shard_map/ppermute | solution.py:21
  54.1 23.2 %collective-permute-start.15 = (bf16[8,136,512]{2,1,0:T(8,128)(2,1)}, bf16[8,136,512]{2,1,0:T(8,128)(2,1)S(1)}, u32[]{:S(2)}, u32[]{:S(2)}) collective-permute-start(bf16[8,136,512]{2,1,0:T(8,128)(2,1)} %fusion.refs_0_), channel_id=1, source_target_pairs={{64,0},{72,8},{80,16},{88,24},{96,32},{104,40},{112,48},{120,56},{... | collective-permute-start | bytes 3342344 | tf_op jit(solution)/shard_map/ppermute | solution.py:21
  64.1 3.4 %copy-start = (bf16[512,8192]{1,0:T(8,128)(2,1)S(1)}, bf16[512,8192]{1,0:T(8,128)(2,1)}, u32[]{:S(2)}) copy-start(bf16[512,8192]{1,0:T(8,128)(2,1)} %all-gather.2.cloned.1.call-done.hidden) | copy-start | bytes 25165828
  65.3 18.1 %collective-permute-start.19 = (bf16[4,128,512]{2,1,0:T(8,128)(2,1)}, bf16[4,128,512]{2,1,0:T(8,128)(2,1)S(1)}, u32[]{:S(2)}, u32[]{:S(2)}) collective-permute-start(bf16[4,128,512]{2,1,0:T(8,128)(2,1)} %collective-permute-done.11.refs_0_), channel_id=1, source_target_pairs={{8,0},{16,8},{24,16},{32,24},{40,32},{48,40},{56,48},{0,56},{72,64... | collective-permute-start | bytes 1572872 | tf_op jit(solution)/shard_map/ppermute | solution.py:21
  65.8 17.6 %collective-permute-start.20 = (bf16[4,128,512]{2,1,0:T(8,128)(2,1)}, bf16[4,128,512]{2,1,0:T(8,128)(2,1)S(1)}, u32[]{:S(2)}, u32[]{:S(2)}) collective-permute-start(bf16[4,128,512]{2,1,0:T(8,128)(2,1)} %collective-permute-done.12.refs_1_), channel_id=1, source_target_pairs={{56,0},{0,8},{8,16},{16,24},{24,32},{32,40},{40,48},{48,56},{120,6... | collective-permute-start | bytes 1572872 | tf_op jit(solution)/shard_map/ppermute | solution.py:21
  77.4 11.5 %collective-permute-start.18 = (bf16[4,136,512]{2,1,0:T(8,128)(2,1)S(1)}, bf16[4,136,512]{2,1,0:T(8,128)(2,1)S(1)}, u32[]{:S(2)}, u32[]{:S(2)}) collective-permute-start(bf16[4,136,512]{2,1,0:T(8,128)(2,1)S(1)} %slice.44), channel_id=1, source_target_pairs={{192,0},{200,8},{208,16},{216,24},{224,32},{232,40},{240,48},{248,... | collective-permute-start | bytes 1671176 | tf_op jit(solution)/shard_map/ppermute | solution.py:21
  78.3 10.7 %collective-permute-start.17 = (bf16[4,136,512]{2,1,0:T(8,128)(2,1)S(1)}, bf16[4,136,512]{2,1,0:T(8,128)(2,1)S(1)}, u32[]{:S(2)}, u32[]{:S(2)}) collective-permute-start(bf16[4,136,512]{2,1,0:T(8,128)(2,1)S(1)} %slice.43), channel_id=1, source_target_pairs={{64,0},{72,8},{80,16},{88,24},{96,32},{104,40},{112,48},{120,56},{... | collective-permute-start | bytes 1671176 | tf_op jit(solution)/shard_map/ppermute | solution.py:21
  83.5 8.4 %collective-permute-start.21 = (bf16[2,128,512]{2,1,0:T(8,128)(2,1)S(1)}, bf16[2,128,512]{2,1,0:T(8,128)(2,1)S(1)}, u32[]{:S(2)}, u32[]{:S(2)}) collective-permute-start(bf16[2,128,512]{2,1,0:T(8,128)(2,1)S(1)} %slice.45), channel_id=1, source_target_pairs={{8,0},{16,8},{24,16},{32,24},{40,32},{48,40},{56,48},{0,56},{72,64... | collective-permute-start | bytes 786440 | tf_op jit(solution)/shard_map/ppermute | solution.py:21
  84.5 7.3 %collective-permute-start.22 = (bf16[2,128,512]{2,1,0:T(8,128)(2,1)S(1)}, bf16[2,128,512]{2,1,0:T(8,128)(2,1)S(1)}, u32[]{:S(2)}, u32[]{:S(2)}) collective-permute-start(bf16[2,128,512]{2,1,0:T(8,128)(2,1)S(1)} %slice.46), channel_id=1, source_target_pairs={{56,0},{0,8},{8,16},{16,24},{24,32},{32,40},{40,48},{48,56},{120,6... | collective-permute-start | bytes 786440 | tf_op jit(solution)/shard_map/ppermute | solution.py:21
  117.2 23.3 %copy-start.2 = (f32[512]{0:T(512)S(1)}, f32[512]{0:T(512)}, u32[]{:S(2)}) copy-start(f32[512]{0:T(512)} %param.9) | copy-start | bytes 6148
  122.1 18.4 %copy-start.1 = (bf16[512,512]{1,0:T(8,128)(2,1)S(1)}, bf16[512,512]{1,0:T(8,128)(2,1)}, u32[]{:S(2)}) copy-start(bf16[512,512]{1,0:T(8,128)(2,1)} %gate.1) | copy-start | bytes 1572868
Sparse Core Ops, SparseCore 0:
  9.2 54.8 all-gather.1

commit v5 on v4

--- a/solution.py
+++ b/solution.py
@@ -161,7 +161,7 @@
         out[half:, pl.ds(start, step)] = rolled[:, half : step + half]
         return carry
 
-    lax.fori_loop(0, out.shape[1] // step, chunk, 0, unroll=4)
+    lax.fori_loop(0, out.shape[1] // step, chunk, 0, unroll=8)
 
 
 def strip(place, taps):
@@ -230,14 +230,14 @@
     return pl.pallas_call(
         mix_kernel,
         out_shape=jax.ShapeDtypeStruct((512, 512), jnp.bfloat16),
-        grid=(4,),
+        grid=(2,),
         in_specs=[
-            pl.BlockSpec((128, 512), lambda i: (i, 0)),
-            pl.BlockSpec((128, 512), lambda i: (i, 0)),
-            pl.BlockSpec((1, 128), lambda i: (0, i)),
-            pl.BlockSpec((512, 128), lambda i: (0, i)),
+            pl.BlockSpec((256, 512), lambda i: (i, 0)),
+            pl.BlockSpec((256, 512), lambda i: (i, 0)),
+            pl.BlockSpec((1, 256), lambda i: (0, i)),
+            pl.BlockSpec((512, 256), lambda i: (0, i)),
         ],
-        out_specs=pl.BlockSpec((512, 128), lambda i: (0, i)),
+        out_specs=pl.BlockSpec((512, 256), lambda i: (0, i)),
         compiler_params=pltpu.CompilerParams(vmem_limit_bytes=VMEM_LIMIT),
         name="mix",
     )(conv, value, gain, gate)

time: 150 us -> 149 us (level)
  transfers between devices with their start and end apart: 24 -> 24, of which waited for: 11 -> 12; matrix products, arithmetic and copies ran while one was open for 4% -> 4% of each run, Pallas kernels for 8% -> 8%
where the time goes in v5:
time: 149 us
  blocking collectives  42.1 us (28%)
  starting transfers between devices  35.3 us (24%)
  waiting for transfers between devices  31 us (21%)
  Pallas kernels  19.7 us (13%)
  between operations  13.6 us (9%)
  local copies, waits for them, and re-layouts  5.35 us (4%)
  other arithmetic  1.58 us (1%)
    ppermute x23, starting transfers between devices, take_from(): return lax.ppermute(array, 'seq', pairs)  35.3 us
    ppermute x23, waiting for transfers between devices, take_from(): return lax.ppermute(array, 'seq', pairs)  24.3 us
    all_to_all x1, blocking collectives, on_device(): lax.all_to_all(value, 'seq', split_axis=0, concat_axis=0, tiled=True)  23.7 us
    all_to_all x1, blocking collectives, on_device(): lax.all_to_all(conv, 'seq', split_axis=0, concat_axis=0, tiled=True)  18.4 us
    pallas_call x5, Pallas kernels, project(): pl.pallas_call(functools.partial(project_kernel, parts, before is None, l...  9.51 us
    all_gather x1, waiting for transfers between devices, on_device(): whole = lax.all_gather(hidden, 'tp', axis=1, tiled=True)  6.01 us
    pallas_call x1, Pallas kernels, convolve(): pl.pallas_call(conv_kernel, out_shape=jax.ShapeDtypeStruct((32, 16, 512),...  4.88 us
    unnamed x16, local copies, waits for them, and re-layouts  4.31 us
  transfers between devices with their start and end apart: 24, of which 12 were waited for; matrix products, arithmetic and copies ran while one was open for 4% of the time, Pallas kernels for 8%

profile of v5, /device:TPU:32, one launch (start us, length us, event | category | flops | bytes accessed | tf_op | source)
XLA Modules:
  0.0 148.7 jit_solution(13286075879652924895)
XLA Ops:
  7.5 3.3 %collective-permute-start.7 = (bf16[128,512]{1,0:T(8,128)(2,1)S(1)}, bf16[128,512]{1,0:T(8,128)(2,1)S(1)}, u32[]{:S(2)}, u32[]{:S(2)}) collective-permute-start(bf16[128,512]{1,0:T(8,128)(2,1)S(1)} %get-tuple-element.44), channel_id=1, source_target_pairs={{128,0},{136,8},{144,16},{152,24},{160,32},{168,40},{176,48},{184,... | collective-permute-start | bytes 393224 | tf_op jit(solution)/shard_map/ppermute | solution.py:21
  12.9 2.0 %collective-permute-start.3 = (bf16[136,512]{1,0:T(8,128)(2,1)S(1)}, bf16[136,512]{1,0:T(8,128)(2,1)S(1)}, u32[]{:S(2)}, u32[]{:S(2)}) collective-permute-start(bf16[136,512]{1,0:T(8,128)(2,1)S(1)} %pad_maximum_fusion.1), channel_id=1, source_target_pairs={{56,0},{0,8},{8,16},{16,24},{24,32},{32,40},{40,48},{48,56},{120,6... | collective-permute-start | bytes 417800 | tf_op jit(solution)/shard_map/ppermute | solution.py:21
  15.7 1.8 %collective-permute-done.6 = bf16[128,512]{1,0:T(8,128)(2,1)S(1)} collective-permute-done((bf16[128,512]{1,0:T(8,128)(2,1)S(1)}, bf16[128,512]{1,0:T(8,128)(2,1)S(1)}, u32[]{:S(2)}, u32[]{:S(2)}) %collective-permute-start.6) | collective-permute-done | bytes 131104 | tf_op jit(solution)/shard_map/ppermute | solution.py:21
  18.1 2.0 %collective-permute-start.10 = (bf16[4,128,512]{2,1,0:T(8,128)(2,1)S(1)}, bf16[4,128,512]{2,1,0:T(8,128)(2,1)S(1)}, u32[]{:S(2)}, u32[]{:S(2)}) collective-permute-start(bf16[4,128,512]{2,1,0:T(8,128)(2,1)S(1)} %pad_maximum_fusion.refs_1_), channel_id=1, source_target_pairs={{56,0},{0,8},{8,16},{16,24},{24,32},{32,40},{40,48},{48,56},{120,6... | collective-permute-start | bytes 1572872 | tf_op jit(solution)/shard_map/ppermute | solution.py:21
  20.2 1.9 %collective-permute-start.4 = (bf16[136,512]{1,0:T(8,128)(2,1)S(1)}, bf16[136,512]{1,0:T(8,128)(2,1)S(1)}, u32[]{:S(2)}, u32[]{:S(2)}) collective-permute-start(bf16[136,512]{1,0:T(8,128)(2,1)S(1)} %collective-permute-done.3), channel_id=1, source_target_pairs={{56,0},{0,8},{8,16},{16,24},{24,32},{32,40},{40,48},{48,56},{120,6... | collective-permute-start | bytes 417800 | tf_op jit(solution)/shard_map/ppermute | solution.py:21
  22.1 2.2 %collective-permute-start.1 = (bf16[136,512]{1,0:T(8,128)(2,1)S(1)}, bf16[136,512]{1,0:T(8,128)(2,1)S(1)}, u32[]{:S(2)}, u32[]{:S(2)}) collective-permute-start(bf16[136,512]{1,0:T(8,128)(2,1)S(1)} %collective-permute-done), channel_id=1, source_target_pairs={{8,0},{16,8},{24,16},{32,24},{40,32},{48,40},{56,48},{0,56},{72,64... | collective-permute-start | bytes 417800 | tf_op jit(solution)/shard_map/ppermute | solution.py:21
  25.7 8.0 %collective-permute-done.4 = bf16[136,512]{1,0:T(8,128)(2,1)S(1)} collective-permute-done((bf16[136,512]{1,0:T(8,128)(2,1)S(1)}, bf16[136,512]{1,0:T(8,128)(2,1)S(1)}, u32[]{:S(2)}, u32[]{:S(2)}) %collective-permute-start.4) | collective-permute-done | bytes 139296 | tf_op jit(solution)/shard_map/ppermute | solution.py:21
  33.7 1.7 %collective-permute-start.5 = (bf16[136,512]{1,0:T(8,128)(2,1)S(1)}, bf16[136,512]{1,0:T(8,128)(2,1)S(1)}, u32[]{:S(2)}, u32[]{:S(2)}) collective-permute-start(bf16[136,512]{1,0:T(8,128)(2,1)S(1)} %collective-permute-done.4), channel_id=1, source_target_pairs={{56,0},{0,8},{8,16},{16,24},{24,32},{32,40},{40,48},{48,56},{120,6... | collective-permute-start | bytes 417800 | tf_op jit(solution)/shard_map/ppermute | solution.py:21
  35.3 2.3 %collective-permute-start.2 = (bf16[136,512]{1,0:T(8,128)(2,1)S(1)}, bf16[136,512]{1,0:T(8,128)(2,1)S(1)}, u32[]{:S(2)}, u32[]{:S(2)}) collective-permute-start(bf16[136,512]{1,0:T(8,128)(2,1)S(1)} %collective-permute-done.1), channel_id=1, source_target_pairs={{8,0},{16,8},{24,16},{32,24},{40,32},{48,40},{56,48},{0,56},{72,64... | collective-permute-start | bytes 417800 | tf_op jit(solution)/shard_map/ppermute | solution.py:21
  39.0 1.7 %collective-permute-done.5 = bf16[136,512]{1,0:T(8,128)(2,1)S(1)} collective-permute-done((bf16[136,512]{1,0:T(8,128)(2,1)S(1)}, bf16[136,512]{1,0:T(8,128)(2,1)S(1)}, u32[]{:S(2)}, u32[]{:S(2)}) %collective-permute-start.5) | collective-permute-done | bytes 139296 | tf_op jit(solution)/shard_map/ppermute | solution.py:21
  41.4 3.3 %collective-permute-start.14 = (bf16[68,512]{1,0:T(8,128)(2,1)S(1)}, bf16[68,512]{1,0:T(8,128)(2,1)S(1)}, u32[]{:S(2)}, u32[]{:S(2)}) collective-permute-start(bf16[68,512]{1,0:T(8,128)(2,1)S(1)} %slice.42), channel_id=1, source_target_pairs={{56,0},{0,8},{8,16},{16,24},{24,32},{32,40},{40,48},{48,56},{120,6... | collective-permute-start | bytes 208904 | tf_op jit(solution)/shard_map/ppermute | solution.py:21
  44.8 2.6 %collective-permute-start.11 = (bf16[4,128,512]{2,1,0:T(8,128)(2,1)}, bf16[4,128,512]{2,1,0:T(8,128)(2,1)}, u32[]{:S(2)}, u32[]{:S(2)}) collective-permute-start(bf16[4,128,512]{2,1,0:T(8,128)(2,1)} %collective-permute-done.9.refs_2_), channel_id=1, source_target_pairs={{8,0},{16,8},{24,16},{32,24},{40,32},{48,40},{56,48},{0,56},{72,64... | collective-permute-start | bytes 1572872 | tf_op jit(solution)/shard_map/ppermute | solution.py:21
  49.3 1.9 %collective-permute-done.13 = bf16[68,512]{1,0:T(8,128)(2,1)S(1)} collective-permute-done((bf16[68,512]{1,0:T(8,128)(2,1)S(1)}, bf16[68,512]{1,0:T(8,128)(2,1)S(1)}, u32[]{:S(2)}, u32[]{:S(2)}) %collective-permute-start.13) | collective-permute-done | bytes 69664 | tf_op jit(solution)/shard_map/ppermute | solution.py:21
  51.9 2.3 %collective-permute-start.16 = (bf16[8,136,512]{2,1,0:T(8,128)(2,1)}, bf16[8,136,512]{2,1,0:T(8,128)(2,1)S(1)}, u32[]{:S(2)}, u32[]{:S(2)}) collective-permute-start(bf16[8,136,512]{2,1,0:T(8,128)(2,1)} %fusion.refs_0_), channel_id=1, source_target_pairs={{192,0},{200,8},{208,16},{216,24},{224,32},{232,40},{240,48},{248,... | collective-permute-start | bytes 3342344 | tf_op jit(solution)/shard_map/ppermute | solution.py:21
  54.1 1.4 collective-permute-start.15
  55.6 2.5 %collective-permute-done.11.refs_0_ = bf16[4,128,512]{2,1,0:T(8,128)(2,1)} collective-permute-done((bf16[4,128,512]{2,1,0:T(8,128)(2,1)}, bf16[4,128,512]{2,1,0:T(8,128)(2,1)}, u32[]{:S(2)}, u32[]{:S(2)}) %collective-permute-start.11) | collective-permute-done | bytes 524320 | tf_op jit(solution)/shard_map/ppermute | solution.py:21
  58.1 6.0 %all-gather.2.cloned.1.call-done.hidden = bf16[512,8192]{1,0:T(8,128)(2,1)} async-done(((bf16[512,1024]{1,0:T(8,128)(2,1)}), bf16[512,8192]{1,0:T(8,128)(2,1)}) %all-gather.2.cloned.1.call-update) | async-done | bytes 8388624 | tf_op jit(solution)/shard_map/all_gather | solution.py:249
  64.1 1.2 starts.1
  65.8 1.6 %collective-permute-start.20 = (bf16[4,128,512]{2,1,0:T(8,128)(2,1)}, bf16[4,128,512]{2,1,0:T(8,128)(2,1)S(1)}, u32[]{:S(2)}, u32[]{:S(2)}) collective-permute-start(bf16[4,128,512]{2,1,0:T(8,128)(2,1)} %collective-permute-done.12.refs_1_), channel_id=1, source_target_pairs={{56,0},{0,8},{8,16},{16,24},{24,32},{32,40},{40,48},{48,56},{120,6... | collective-permute-start | bytes 1572872 | tf_op jit(solution)/shard_map/ppermute | solution.py:21
  67.5 2.9 %project_20.1.refs_2_ = f32[512,512]{1,0:T(8,128)S(1)} custom-call(s32[32]{0:T(128)S(1)} %starts.1, bf16[512,8192]{1,0:T(8,128)(2,1)S(1)} %copy-done, bf16[8,136,512]{2,1,0:T(8,128)(2,1)} %fusion.refs_0_, bf16[4,128,512]{2,1,0:T(8,128)(2,1)S(1)} %pad_maximum_fusion.refs_1_, bf16[4,128,512]{2,1,0:T(8,128)(2,1)} %collective-permute-done.9.refs_2_, ...), custom_call_target="tpu_custom_call" | custom-call | flops 1342177280 | bytes 5242880 | tf_op jit(solution)/shard_map/project_20/pallas_call | solution.py:77
  70.4 1.9 %project_8.2.refs_2_ = f32[512,512]{1,0:T(8,128)S(1)} custom-call(s32[32]{0:T(128)S(1)} %starts.1, bf16[512,8192]{1,0:T(8,128)(2,1)S(1)} %copy-done, bf16[4,128,512]{2,1,0:T(8,128)(2,1)} %collective-permute-done.11.refs_0_, bf16[4,128,512]{2,1,0:T(8,128)(2,1)} %collective-permute-done.12.refs_1_, f32[512,512]{1,0:T(8,128)S(1)} %project_20.1.refs_2_), custom_call_target="tpu_custom_call" | custom-call | flops 536870912 | bytes 2097152 | tf_op jit(solution)/shard_map/project_8/pallas_call | solution.py:77
  72.3 4.7 %collective-permute-done.16.refs_1_ = bf16[8,136,512]{2,1,0:T(8,128)(2,1)S(1)} collective-permute-done((bf16[8,136,512]{2,1,0:T(8,128)(2,1)}, bf16[8,136,512]{2,1,0:T(8,128)(2,1)S(1)}, u32[]{:S(2)}, u32[]{:S(2)}) %collective-permute-start.16) | collective-permute-done | bytes 1114144 | tf_op jit(solution)/shard_map/ppermute | solution.py:21
  78.3 2.5 %collective-permute-start.17 = (bf16[4,136,512]{2,1,0:T(8,128)(2,1)S(1)}, bf16[4,136,512]{2,1,0:T(8,128)(2,1)S(1)}, u32[]{:S(2)}, u32[]{:S(2)}) collective-permute-start(bf16[4,136,512]{2,1,0:T(8,128)(2,1)S(1)} %slice.43), channel_id=1, source_target_pairs={{64,0},{72,8},{80,16},{88,24},{96,32},{104,40},{112,48},{120,56},{... | collective-permute-start | bytes 1671176 | tf_op jit(solution)/shard_map/ppermute | solution.py:21
  81.6 1.8 %project_16.1.refs_2_ = f32[512,512]{1,0:T(8,128)S(1)} custom-call(s32[32]{0:T(128)S(1)} %starts.1, bf16[512,8192]{1,0:T(8,128)(2,1)S(1)} %copy-done, bf16[8,136,512]{2,1,0:T(8,128)(2,1)S(1)} %collective-permute-done.15.refs_0_, bf16[8,136,512]{2,1,0:T(8,128)(2,1)S(1)} %collective-permute-done.16.refs_1_, f32[512,512]{1,0:T(8,128)S(1)} %project_8.2.refs_2_), custom_call_target="tpu_custom_call" | custom-call | flops 1073741824 | bytes 4194304 | tf_op jit(solution)/shard_map/project_16/pallas_call | solution.py:77
  85.6 1.3 project_8.3.refs_4_
  86.8 2.0 %collective-permute-done.18.refs_1_ = bf16[4,136,512]{2,1,0:T(8,128)(2,1)S(1)} collective-permute-done((bf16[4,136,512]{2,1,0:T(8,128)(2,1)S(1)}, bf16[4,136,512]{2,1,0:T(8,128)(2,1)S(1)}, u32[]{:S(2)}, u32[]{:S(2)}) %collective-permute-start.18) | collective-permute-done | bytes 557088 | tf_op jit(solution)/shard_map/ppermute | solution.py:21
  89.0 2.5 %strip.1.strip_ref = bf16[256,16384]{1,0:T(8,128)(2,1)S(1)} custom-call(s32[3]{0:T(128)S(1)} %pad_add_fusion.place, f32[4,8,1,512]{3,2,1,0:T(1,128)S(1)} %fusion.4.taps), custom_call_target="tpu_custom_call" | custom-call | flops 10485760 | bytes 8388608 | tf_op jit(solution)/shard_map/strip/pallas_call | solution.py:169
  91.6 1.6 %project_12.1 = bf16[32,16,512]{2,1,0:T(8,128)(2,1)S(1)} custom-call(s32[32]{0:T(128)S(1)} %starts.1, bf16[512,8192]{1,0:T(8,128)(2,1)S(1)} %copy-done, bf16[4,136,512]{2,1,0:T(8,128)(2,1)S(1)} %collective-permute-done.17.refs_0_, bf16[4,136,512]{2,1,0:T(8,128)(2,1)S(1)} %collective-permute-done.18.refs_1_, ...), custom_call_target="tpu_custom_call" | custom-call | flops 805306368 | bytes 3145728 | tf_op jit(solution)/shard_map/project_12/pallas_call | solution.py:77
  93.2 23.7 %all_to_all.10.value = bf16[32,16,512]{2,1,0:T(8,128)(2,1)S(1)} all-to-all(bf16[32,16,512]{2,1,0:T(8,128)(2,1)S(1)} %project_12.1), channel_id=1, replica_groups=mesh['seq'=32,'tp'=8] {'seq'}, dimensions={0} | all-to-all | bytes 1048576 | tf_op jit(solution)/shard_map/all_to_all | solution.py:254
  116.9 4.9 %convolve.1 = bf16[32,16,512]{2,1,0:T(8,128)(2,1)S(1)} custom-call(bf16[32,16,512]{2,1,0:T(8,128)(2,1)S(1)} %all_to_all.10.value, bf16[256,16384]{1,0:T(8,128)(2,1)S(1)} %strip.1.strip_ref), custom_call_target="tpu_custom_call" | custom-call | flops 4499999744 | bytes 10485760 | tf_op jit(solution)/shard_map/convolve/pallas_call | solution.py:206
  121.8 18.4 %all_to_all.11 = bf16[32,16,512]{2,1,0:T(8,128)(2,1)S(1)} all-to-all(bf16[32,16,512]{2,1,0:T(8,128)(2,1)S(1)} %convolve.1), channel_id=1, replica_groups=mesh['seq'=32,'tp'=8] {'seq'}, dimensions={0} | all-to-all | bytes 1048576 | tf_op jit(solution)/shard_map/all_to_all | solution.py:256
  140.2 1.6 %mix.1 = bf16[512,512]{1,0:T(8,128)(2,1)} custom-call(bf16[512,512]{1,0:T(8,128)(2,1)S(1)} %bitcast.38, bf16[512,512]{1,0:T(8,128)(2,1)S(1)} %bitcast.37, f32[1,512]{1,0:T(1,128)S(1)} %bitcast.39, bf16[512,512]{1,0:T(8,128)(2,1)S(1)} %copy-done.1), custom_call_target="tpu_custom_call" | custom-call | tf_op jit(solution)/shard_map/mix/pallas_call | solution.py:230
  (64 shorter events, 15.7 us)
Async XLA Ops:
  6.5 0.9 copy-start.3
  6.5 6.3 %copy-start.4 = (bf16[512,4]{0,1:T(4,128)(2,1)S(1)}, bf16[512,4]{0,1:T(4,128)(2,1)}, u32[]{:S(2)}) copy-start(bf16[512,4]{0,1:T(4,128)(2,1)} %param.8) | copy-start | bytes 12292
  6.5 57.5 %all-gather.2.cloned.1.call-start = ((), (), s32[]{:S(2)}) async-start(), calls=%async_computation.2 | async-start | bytes 9437184 | tf_op jit(solution)/shard_map/all_gather | solution.py:249
  7.5 8.1 %collective-permute-start.7 = (bf16[128,512]{1,0:T(8,128)(2,1)S(1)}, bf16[128,512]{1,0:T(8,128)(2,1)S(1)}, u32[]{:S(2)}, u32[]{:S(2)}) collective-permute-start(bf16[128,512]{1,0:T(8,128)(2,1)S(1)} %get-tuple-element.44), channel_id=1, source_target_pairs={{128,0},{136,8},{144,16},{152,24},{160,32},{168,40},{176,48},{184,... | collective-permute-start | bytes 393224 | tf_op jit(solution)/shard_map/ppermute | solution.py:21
  10.8 6.7 %collective-permute-start.6 = (bf16[128,512]{1,0:T(8,128)(2,1)S(1)}, bf16[128,512]{1,0:T(8,128)(2,1)S(1)}, u32[]{:S(2)}, u32[]{:S(2)}) collective-permute-start(bf16[128,512]{1,0:T(8,128)(2,1)S(1)} %get-tuple-element.44), channel_id=1, source_target_pairs={{64,0},{72,8},{80,16},{88,24},{96,32},{104,40},{112,48},{120,56},{... | collective-permute-start | bytes 393224 | tf_op jit(solution)/shard_map/ppermute | solution.py:21
  11.9 6.2 %collective-permute-start.8 = (bf16[128,512]{1,0:T(8,128)(2,1)S(1)}, bf16[128,512]{1,0:T(8,128)(2,1)S(1)}, u32[]{:S(2)}, u32[]{:S(2)}) collective-permute-start(bf16[128,512]{1,0:T(8,128)(2,1)S(1)} %get-tuple-element.44), channel_id=1, source_target_pairs={{192,0},{200,8},{208,16},{216,24},{224,32},{232,40},{240,48},{248,... | collective-permute-start | bytes 393224 | tf_op jit(solution)/shard_map/ppermute | solution.py:21
  12.9 7.3 %collective-permute-start.3 = (bf16[136,512]{1,0:T(8,128)(2,1)S(1)}, bf16[136,512]{1,0:T(8,128)(2,1)S(1)}, u32[]{:S(2)}, u32[]{:S(2)}) collective-permute-start(bf16[136,512]{1,0:T(8,128)(2,1)S(1)} %pad_maximum_fusion.1), channel_id=1, source_target_pairs={{56,0},{0,8},{8,16},{16,24},{24,32},{32,40},{40,48},{48,56},{120,6... | collective-permute-start | bytes 417800 | tf_op jit(solution)/shard_map/ppermute | solution.py:21
  14.9 7.3 %collective-permute-start = (bf16[136,512]{1,0:T(8,128)(2,1)S(1)}, bf16[136,512]{1,0:T(8,128)(2,1)S(1)}, u32[]{:S(2)}, u32[]{:S(2)}) collective-permute-start(bf16[136,512]{1,0:T(8,128)(2,1)S(1)} %pad_maximum_fusion.1), channel_id=1, source_target_pairs={{8,0},{16,8},{24,16},{32,24},{40,32},{48,40},{56,48},{0,56},{72,64... | collective-permute-start | bytes 417800 | tf_op jit(solution)/shard_map/ppermute | solution.py:21
  18.1 23.3 %collective-permute-start.10 = (bf16[4,128,512]{2,1,0:T(8,128)(2,1)S(1)}, bf16[4,128,512]{2,1,0:T(8,128)(2,1)S(1)}, u32[]{:S(2)}, u32[]{:S(2)}) collective-permute-start(bf16[4,128,512]{2,1,0:T(8,128)(2,1)S(1)} %pad_maximum_fusion.refs_1_), channel_id=1, source_target_pairs={{56,0},{0,8},{8,16},{16,24},{24,32},{32,40},{40,48},{48,56},{120,6... | collective-permute-start | bytes 1572872 | tf_op jit(solution)/shard_map/ppermute | solution.py:21
  20.1 21.3 %collective-permute-start.9 = (bf16[4,128,512]{2,1,0:T(8,128)(2,1)S(1)}, bf16[4,128,512]{2,1,0:T(8,128)(2,1)}, u32[]{:S(2)}, u32[]{:S(2)}) collective-permute-start(bf16[4,128,512]{2,1,0:T(8,128)(2,1)S(1)} %pad_maximum_fusion.refs_1_), channel_id=1, source_target_pairs={{8,0},{16,8},{24,16},{32,24},{40,32},{48,40},{56,48},{0,56},{72,64... | collective-permute-start | bytes 1572872 | tf_op jit(solution)/shard_map/ppermute | solution.py:21
  20.2 13.5 %collective-permute-start.4 = (bf16[136,512]{1,0:T(8,128)(2,1)S(1)}, bf16[136,512]{1,0:T(8,128)(2,1)S(1)}, u32[]{:S(2)}, u32[]{:S(2)}) collective-permute-start(bf16[136,512]{1,0:T(8,128)(2,1)S(1)} %collective-permute-done.3), channel_id=1, source_target_pairs={{56,0},{0,8},{8,16},{16,24},{24,32},{32,40},{40,48},{48,56},{120,6... | collective-permute-start | bytes 417800 | tf_op jit(solution)/shard_map/ppermute | solution.py:21
  22.1 13.2 %collective-permute-start.1 = (bf16[136,512]{1,0:T(8,128)(2,1)S(1)}, bf16[136,512]{1,0:T(8,128)(2,1)S(1)}, u32[]{:S(2)}, u32[]{:S(2)}) collective-permute-start(bf16[136,512]{1,0:T(8,128)(2,1)S(1)} %collective-permute-done), channel_id=1, source_target_pairs={{8,0},{16,8},{24,16},{32,24},{40,32},{48,40},{56,48},{0,56},{72,64... | collective-permute-start | bytes 417800 | tf_op jit(solution)/shard_map/ppermute | solution.py:21
  33.7 7.0 %collective-permute-start.5 = (bf16[136,512]{1,0:T(8,128)(2,1)S(1)}, bf16[136,512]{1,0:T(8,128)(2,1)S(1)}, u32[]{:S(2)}, u32[]{:S(2)}) collective-permute-start(bf16[136,512]{1,0:T(8,128)(2,1)S(1)} %collective-permute-done.4), channel_id=1, source_target_pairs={{56,0},{0,8},{8,16},{16,24},{24,32},{32,40},{40,48},{48,56},{120,6... | collective-permute-start | bytes 417800 | tf_op jit(solution)/shard_map/ppermute | solution.py:21
  35.3 6.1 %collective-permute-start.2 = (bf16[136,512]{1,0:T(8,128)(2,1)S(1)}, bf16[136,512]{1,0:T(8,128)(2,1)S(1)}, u32[]{:S(2)}, u32[]{:S(2)}) collective-permute-start(bf16[136,512]{1,0:T(8,128)(2,1)S(1)} %collective-permute-done.1), channel_id=1, source_target_pairs={{8,0},{16,8},{24,16},{32,24},{40,32},{48,40},{56,48},{0,56},{72,64... | collective-permute-start | bytes 417800 | tf_op jit(solution)/shard_map/ppermute | solution.py:21
  41.4 7.9 %collective-permute-start.14 = (bf16[68,512]{1,0:T(8,128)(2,1)S(1)}, bf16[68,512]{1,0:T(8,128)(2,1)S(1)}, u32[]{:S(2)}, u32[]{:S(2)}) collective-permute-start(bf16[68,512]{1,0:T(8,128)(2,1)S(1)} %slice.42), channel_id=1, source_target_pairs={{56,0},{0,8},{8,16},{16,24},{24,32},{32,40},{40,48},{48,56},{120,6... | collective-permute-start | bytes 208904 | tf_op jit(solution)/shard_map/ppermute | solution.py:21
  44.8 6.4 %collective-permute-start.13 = (bf16[68,512]{1,0:T(8,128)(2,1)S(1)}, bf16[68,512]{1,0:T(8,128)(2,1)S(1)}, u32[]{:S(2)}, u32[]{:S(2)}) collective-permute-start(bf16[68,512]{1,0:T(8,128)(2,1)S(1)} %slice.41), channel_id=1, source_target_pairs={{8,0},{16,8},{24,16},{32,24},{40,32},{48,40},{56,48},{0,56},{72,64... | collective-permute-start | bytes 208904 | tf_op jit(solution)/shard_map/ppermute | solution.py:21
  44.8 13.3 %collective-permute-start.11 = (bf16[4,128,512]{2,1,0:T(8,128)(2,1)}, bf16[4,128,512]{2,1,0:T(8,128)(2,1)}, u32[]{:S(2)}, u32[]{:S(2)}) collective-permute-start(bf16[4,128,512]{2,1,0:T(8,128)(2,1)} %collective-permute-done.9.refs_2_), channel_id=1, source_target_pairs={{8,0},{16,8},{24,16},{32,24},{40,32},{48,40},{56,48},{0,56},{72,64... | collective-permute-start | bytes 1572872 | tf_op jit(solution)/shard_map/ppermute | solution.py:21
  47.4 10.7 %collective-permute-start.12 = (bf16[4,128,512]{2,1,0:T(8,128)(2,1)S(1)}, bf16[4,128,512]{2,1,0:T(8,128)(2,1)}, u32[]{:S(2)}, u32[]{:S(2)}) collective-permute-start(bf16[4,128,512]{2,1,0:T(8,128)(2,1)S(1)} %collective-permute-done.10.refs_3_), channel_id=1, source_target_pairs={{56,0},{0,8},{8,16},{16,24},{24,32},{32,40},{40,48},{48,56},{120,6... | collective-permute-start | bytes 1572872 | tf_op jit(solution)/shard_map/ppermute | solution.py:21
  51.9 25.2 %collective-permute-start.16 = (bf16[8,136,512]{2,1,0:T(8,128)(2,1)}, bf16[8,136,512]{2,1,0:T(8,128)(2,1)S(1)}, u32[]{:S(2)}, u32[]{:S(2)}) collective-permute-start(bf16[8,136,512]{2,1,0:T(8,128)(2,1)} %fusion.refs_0_), channel_id=1, source_target_pairs={{192,0},{200,8},{208,16},{216,24},{224,32},{232,40},{240,48},{248,... | collective-permute-start | bytes 3342344 | tf_op jit(solution)/shard_map/ppermute | solution.py:21
  54.1 23.2 %collective-permute-start.15 = (bf16[8,136,512]{2,1,0:T(8,128)(2,1)}, bf16[8,136,512]{2,1,0:T(8,128)(2,1)S(1)}, u32[]{:S(2)}, u32[]{:S(2)}) collective-permute-start(bf16[8,136,512]{2,1,0:T(8,128)(2,1)} %fusion.refs_0_), channel_id=1, source_target_pairs={{64,0},{72,8},{80,16},{88,24},{96,32},{104,40},{112,48},{120,56},{... | collective-permute-start | bytes 3342344 | tf_op jit(solution)/shard_map/ppermute | solution.py:21
  64.1 3.4 %copy-start = (bf16[512,8192]{1,0:T(8,128)(2,1)S(1)}, bf16[512,8192]{1,0:T(8,128)(2,1)}, u32[]{:S(2)}) copy-start(bf16[512,8192]{1,0:T(8,128)(2,1)} %all-gather.2.cloned.1.call-done.hidden) | copy-start | bytes 25165828
  65.3 18.1 %collective-permute-start.19 = (bf16[4,128,512]{2,1,0:T(8,128)(2,1)}, bf16[4,128,512]{2,1,0:T(8,128)(2,1)S(1)}, u32[]{:S(2)}, u32[]{:S(2)}) collective-permute-start(bf16[4,128,512]{2,1,0:T(8,128)(2,1)} %collective-permute-done.11.refs_0_), channel_id=1, source_target_pairs={{8,0},{16,8},{24,16},{32,24},{40,32},{48,40},{56,48},{0,56},{72,64... | collective-permute-start | bytes 1572872 | tf_op jit(solution)/shard_map/ppermute | solution.py:21
  65.8 17.6 %collective-permute-start.20 = (bf16[4,128,512]{2,1,0:T(8,128)(2,1)}, bf16[4,128,512]{2,1,0:T(8,128)(2,1)S(1)}, u32[]{:S(2)}, u32[]{:S(2)}) collective-permute-start(bf16[4,128,512]{2,1,0:T(8,128)(2,1)} %collective-permute-done.12.refs_1_), channel_id=1, source_target_pairs={{56,0},{0,8},{8,16},{16,24},{24,32},{32,40},{40,48},{48,56},{120,6... | collective-permute-start | bytes 1572872 | tf_op jit(solution)/shard_map/ppermute | solution.py:21
  77.4 11.5 %collective-permute-start.18 = (bf16[4,136,512]{2,1,0:T(8,128)(2,1)S(1)}, bf16[4,136,512]{2,1,0:T(8,128)(2,1)S(1)}, u32[]{:S(2)}, u32[]{:S(2)}) collective-permute-start(bf16[4,136,512]{2,1,0:T(8,128)(2,1)S(1)} %slice.44), channel_id=1, source_target_pairs={{192,0},{200,8},{208,16},{216,24},{224,32},{232,40},{240,48},{248,... | collective-permute-start | bytes 1671176 | tf_op jit(solution)/shard_map/ppermute | solution.py:21
  78.3 10.7 %collective-permute-start.17 = (bf16[4,136,512]{2,1,0:T(8,128)(2,1)S(1)}, bf16[4,136,512]{2,1,0:T(8,128)(2,1)S(1)}, u32[]{:S(2)}, u32[]{:S(2)}) collective-permute-start(bf16[4,136,512]{2,1,0:T(8,128)(2,1)S(1)} %slice.43), channel_id=1, source_target_pairs={{64,0},{72,8},{80,16},{88,24},{96,32},{104,40},{112,48},{120,56},{... | collective-permute-start | bytes 1671176 | tf_op jit(solution)/shard_map/ppermute | solution.py:21
  83.5 8.0 %collective-permute-start.21 = (bf16[2,128,512]{2,1,0:T(8,128)(2,1)S(1)}, bf16[2,128,512]{2,1,0:T(8,128)(2,1)S(1)}, u32[]{:S(2)}, u32[]{:S(2)}) collective-permute-start(bf16[2,128,512]{2,1,0:T(8,128)(2,1)S(1)} %slice.45), channel_id=1, source_target_pairs={{8,0},{16,8},{24,16},{32,24},{40,32},{48,40},{56,48},{0,56},{72,64... | collective-permute-start | bytes 786440 | tf_op jit(solution)/shard_map/ppermute | solution.py:21
  84.5 7.1 %collective-permute-start.22 = (bf16[2,128,512]{2,1,0:T(8,128)(2,1)S(1)}, bf16[2,128,512]{2,1,0:T(8,128)(2,1)S(1)}, u32[]{:S(2)}, u32[]{:S(2)}) collective-permute-start(bf16[2,128,512]{2,1,0:T(8,128)(2,1)S(1)} %slice.46), channel_id=1, source_target_pairs={{56,0},{0,8},{8,16},{16,24},{24,32},{32,40},{40,48},{48,56},{120,6... | collective-permute-start | bytes 786440 | tf_op jit(solution)/shard_map/ppermute | solution.py:21
  116.9 23.3 %copy-start.2 = (f32[512]{0:T(512)S(1)}, f32[512]{0:T(512)}, u32[]{:S(2)}) copy-start(f32[512]{0:T(512)} %param.9) | copy-start | bytes 6148
  121.8 18.4 %copy-start.1 = (bf16[512,512]{1,0:T(8,128)(2,1)S(1)}, bf16[512,512]{1,0:T(8,128)(2,1)}, u32[]{:S(2)}) copy-start(bf16[512,512]{1,0:T(8,128)(2,1)} %gate.1) | copy-start | bytes 1572868
Sparse Core Ops, SparseCore 0:
  9.2 54.8 all-gather.1

commit v6 on v5

--- a/solution.py
+++ b/solution.py
@@ -129,7 +129,6 @@
     total, above, below = lax.optimization_barrier((total, above, below))
     across = halves(above, below, 1, 0)
     total = project(starts, hidden, [(above, row(1)), (below, row(3))], total)
-    total, ring[3], ring[-3] = lax.optimization_barrier((total, ring[3], ring[-3]))
     ends = halves(ring[3], ring[-3], 0, 1)
     total = project(starts, hidden, [(ring[k], stack(k)) for k in (3, -3)], total)
     held = [(across[0], row(2, 0, 4)), (across[1], row(2, 4, 8))]

time: 149 us -> 149 us (level)
  transfers between devices with their start and end apart: 24 -> 24, of which waited for: 12 -> 11; matrix products, arithmetic and copies ran while one was open for 4% -> 4% of each run, Pallas kernels for 8% -> 8%
where the time goes in v6:
time: 149 us
  blocking collectives  42.2 us (28%)
  starting transfers between devices  35.4 us (24%)
  waiting for transfers between devices  30.9 us (21%)
  Pallas kernels  19.7 us (13%)
  between operations  13.6 us (9%)
  local copies, waits for them, and re-layouts  5.35 us (4%)
  other arithmetic  1.58 us (1%)
    ppermute x23, starting transfers between devices, take_from(): return lax.ppermute(array, 'seq', pairs)  35.4 us
    ppermute x23, waiting for transfers between devices, take_from(): return lax.ppermute(array, 'seq', pairs)  24.2 us
    all_to_all x1, blocking collectives, on_device(): lax.all_to_all(value, 'seq', split_axis=0, concat_axis=0, tiled=True)  23.8 us
    all_to_all x1, blocking collectives, on_device(): lax.all_to_all(conv, 'seq', split_axis=0, concat_axis=0, tiled=True)  18.4 us
    pallas_call x5, Pallas kernels, project(): pl.pallas_call(functools.partial(project_kernel, parts, before is None, l...  9.51 us
    all_gather x1, waiting for transfers between devices, on_device(): whole = lax.all_gather(hidden, 'tp', axis=1, tiled=True)  6.01 us
    pallas_call x1, Pallas kernels, convolve(): pl.pallas_call(conv_kernel, out_shape=jax.ShapeDtypeStruct((32, 16, 512),...  4.88 us
    unnamed x16, local copies, waits for them, and re-layouts  4.31 us
  transfers between devices with their start and end apart: 24, of which 11 were waited for; matrix products, arithmetic and copies ran while one was open for 4% of the time, Pallas kernels for 8%

profile of v6, /device:TPU:32, one launch (start us, length us, event | category | flops | bytes accessed | tf_op | source)
XLA Modules:
  0.0 148.7 jit_solution(6660658714948368627)
XLA Ops:
  7.5 3.3 %collective-permute-start.7 = (bf16[128,512]{1,0:T(8,128)(2,1)S(1)}, bf16[128,512]{1,0:T(8,128)(2,1)S(1)}, u32[]{:S(2)}, u32[]{:S(2)}) collective-permute-start(bf16[128,512]{1,0:T(8,128)(2,1)S(1)} %get-tuple-element.38), channel_id=1, source_target_pairs={{128,0},{136,8},{144,16},{152,24},{160,32},{168,40},{176,48},{184,... | collective-permute-start | bytes 393224 | tf_op jit(solution)/shard_map/ppermute | solution.py:21
  12.9 2.0 %collective-permute-start.3 = (bf16[136,512]{1,0:T(8,128)(2,1)S(1)}, bf16[136,512]{1,0:T(8,128)(2,1)S(1)}, u32[]{:S(2)}, u32[]{:S(2)}) collective-permute-start(bf16[136,512]{1,0:T(8,128)(2,1)S(1)} %pad_maximum_fusion.1), channel_id=1, source_target_pairs={{56,0},{0,8},{8,16},{16,24},{24,32},{32,40},{40,48},{48,56},{120,6... | collective-permute-start | bytes 417800 | tf_op jit(solution)/shard_map/ppermute | solution.py:21
  15.7 1.8 %collective-permute-done.6 = bf16[128,512]{1,0:T(8,128)(2,1)S(1)} collective-permute-done((bf16[128,512]{1,0:T(8,128)(2,1)S(1)}, bf16[128,512]{1,0:T(8,128)(2,1)S(1)}, u32[]{:S(2)}, u32[]{:S(2)}) %collective-permute-start.6) | collective-permute-done | bytes 131104 | tf_op jit(solution)/shard_map/ppermute | solution.py:21
  18.1 2.0 %collective-permute-start.10 = (bf16[4,128,512]{2,1,0:T(8,128)(2,1)S(1)}, bf16[4,128,512]{2,1,0:T(8,128)(2,1)S(1)}, u32[]{:S(2)}, u32[]{:S(2)}) collective-permute-start(bf16[4,128,512]{2,1,0:T(8,128)(2,1)S(1)} %pad_maximum_fusion.refs_1_), channel_id=1, source_target_pairs={{56,0},{0,8},{8,16},{16,24},{24,32},{32,40},{40,48},{48,56},{120,6... | collective-permute-start | bytes 1572872 | tf_op jit(solution)/shard_map/ppermute | solution.py:21
  20.2 1.9 %collective-permute-start.4 = (bf16[136,512]{1,0:T(8,128)(2,1)S(1)}, bf16[136,512]{1,0:T(8,128)(2,1)S(1)}, u32[]{:S(2)}, u32[]{:S(2)}) collective-permute-start(bf16[136,512]{1,0:T(8,128)(2,1)S(1)} %collective-permute-done.3), channel_id=1, source_target_pairs={{56,0},{0,8},{8,16},{16,24},{24,32},{32,40},{40,48},{48,56},{120,6... | collective-permute-start | bytes 417800 | tf_op jit(solution)/shard_map/ppermute | solution.py:21
  22.1 2.2 %collective-permute-start.1 = (bf16[136,512]{1,0:T(8,128)(2,1)S(1)}, bf16[136,512]{1,0:T(8,128)(2,1)S(1)}, u32[]{:S(2)}, u32[]{:S(2)}) collective-permute-start(bf16[136,512]{1,0:T(8,128)(2,1)S(1)} %collective-permute-done), channel_id=1, source_target_pairs={{8,0},{16,8},{24,16},{32,24},{40,32},{48,40},{56,48},{0,56},{72,64... | collective-permute-start | bytes 417800 | tf_op jit(solution)/shard_map/ppermute | solution.py:21
  25.7 8.0 %collective-permute-done.4 = bf16[136,512]{1,0:T(8,128)(2,1)S(1)} collective-permute-done((bf16[136,512]{1,0:T(8,128)(2,1)S(1)}, bf16[136,512]{1,0:T(8,128)(2,1)S(1)}, u32[]{:S(2)}, u32[]{:S(2)}) %collective-permute-start.4) | collective-permute-done | bytes 139296 | tf_op jit(solution)/shard_map/ppermute | solution.py:21
  33.7 1.7 %collective-permute-start.5 = (bf16[136,512]{1,0:T(8,128)(2,1)S(1)}, bf16[136,512]{1,0:T(8,128)(2,1)S(1)}, u32[]{:S(2)}, u32[]{:S(2)}) collective-permute-start(bf16[136,512]{1,0:T(8,128)(2,1)S(1)} %collective-permute-done.4), channel_id=1, source_target_pairs={{56,0},{0,8},{8,16},{16,24},{24,32},{32,40},{40,48},{48,56},{120,6... | collective-permute-start | bytes 417800 | tf_op jit(solution)/shard_map/ppermute | solution.py:21
  35.3 2.3 %collective-permute-start.2 = (bf16[136,512]{1,0:T(8,128)(2,1)S(1)}, bf16[136,512]{1,0:T(8,128)(2,1)S(1)}, u32[]{:S(2)}, u32[]{:S(2)}) collective-permute-start(bf16[136,512]{1,0:T(8,128)(2,1)S(1)} %collective-permute-done.1), channel_id=1, source_target_pairs={{8,0},{16,8},{24,16},{32,24},{40,32},{48,40},{56,48},{0,56},{72,64... | collective-permute-start | bytes 417800 | tf_op jit(solution)/shard_map/ppermute | solution.py:21
  39.0 1.7 %collective-permute-done.5 = bf16[136,512]{1,0:T(8,128)(2,1)S(1)} collective-permute-done((bf16[136,512]{1,0:T(8,128)(2,1)S(1)}, bf16[136,512]{1,0:T(8,128)(2,1)S(1)}, u32[]{:S(2)}, u32[]{:S(2)}) %collective-permute-start.5) | collective-permute-done | bytes 139296 | tf_op jit(solution)/shard_map/ppermute | solution.py:21
  41.4 3.3 %collective-permute-start.14 = (bf16[68,512]{1,0:T(8,128)(2,1)S(1)}, bf16[68,512]{1,0:T(8,128)(2,1)S(1)}, u32[]{:S(2)}, u32[]{:S(2)}) collective-permute-start(bf16[68,512]{1,0:T(8,128)(2,1)S(1)} %slice.42), channel_id=1, source_target_pairs={{56,0},{0,8},{8,16},{16,24},{24,32},{32,40},{40,48},{48,56},{120,6... | collective-permute-start | bytes 208904 | tf_op jit(solution)/shard_map/ppermute | solution.py:21
  44.8 2.6 %collective-permute-start.11 = (bf16[4,128,512]{2,1,0:T(8,128)(2,1)}, bf16[4,128,512]{2,1,0:T(8,128)(2,1)}, u32[]{:S(2)}, u32[]{:S(2)}) collective-permute-start(bf16[4,128,512]{2,1,0:T(8,128)(2,1)} %collective-permute-done.9.refs_2_), channel_id=1, source_target_pairs={{8,0},{16,8},{24,16},{32,24},{40,32},{48,40},{56,48},{0,56},{72,64... | collective-permute-start | bytes 1572872 | tf_op jit(solution)/shard_map/ppermute | solution.py:21
  49.3 1.9 %collective-permute-done.13 = bf16[68,512]{1,0:T(8,128)(2,1)S(1)} collective-permute-done((bf16[68,512]{1,0:T(8,128)(2,1)S(1)}, bf16[68,512]{1,0:T(8,128)(2,1)S(1)}, u32[]{:S(2)}, u32[]{:S(2)}) %collective-permute-start.13) | collective-permute-done | bytes 69664 | tf_op jit(solution)/shard_map/ppermute | solution.py:21
  51.9 2.3 %collective-permute-start.16 = (bf16[8,136,512]{2,1,0:T(8,128)(2,1)}, bf16[8,136,512]{2,1,0:T(8,128)(2,1)S(1)}, u32[]{:S(2)}, u32[]{:S(2)}) collective-permute-start(bf16[8,136,512]{2,1,0:T(8,128)(2,1)} %fusion.refs_0_), channel_id=1, source_target_pairs={{192,0},{200,8},{208,16},{216,24},{224,32},{232,40},{240,48},{248,... | collective-permute-start | bytes 3342344 | tf_op jit(solution)/shard_map/ppermute | solution.py:21
  54.1 1.4 collective-permute-start.15
  55.6 2.5 %collective-permute-done.11.refs_0_ = bf16[4,128,512]{2,1,0:T(8,128)(2,1)} collective-permute-done((bf16[4,128,512]{2,1,0:T(8,128)(2,1)}, bf16[4,128,512]{2,1,0:T(8,128)(2,1)}, u32[]{:S(2)}, u32[]{:S(2)}) %collective-permute-start.11) | collective-permute-done | bytes 524320 | tf_op jit(solution)/shard_map/ppermute | solution.py:21
  58.1 6.0 %all-gather.2.cloned.1.call-done.hidden = bf16[512,8192]{1,0:T(8,128)(2,1)} async-done(((bf16[512,1024]{1,0:T(8,128)(2,1)}), bf16[512,8192]{1,0:T(8,128)(2,1)}) %all-gather.2.cloned.1.call-update) | async-done | bytes 8388624 | tf_op jit(solution)/shard_map/all_gather | solution.py:248
  65.8 1.6 %collective-permute-start.21 = (bf16[4,128,512]{2,1,0:T(8,128)(2,1)}, bf16[4,128,512]{2,1,0:T(8,128)(2,1)S(1)}, u32[]{:S(2)}, u32[]{:S(2)}) collective-permute-start(bf16[4,128,512]{2,1,0:T(8,128)(2,1)} %collective-permute-done.12.refs_1_), channel_id=1, source_target_pairs={{56,0},{0,8},{8,16},{16,24},{24,32},{32,40},{40,48},{48,56},{120,6... | collective-permute-start | bytes 1572872 | tf_op jit(solution)/shard_map/ppermute | solution.py:21
  67.5 2.9 %project_20.1.refs_2_ = f32[512,512]{1,0:T(8,128)S(1)} custom-call(s32[32]{0:T(128)S(1)} %starts.1, bf16[512,8192]{1,0:T(8,128)(2,1)S(1)} %copy-done, bf16[8,136,512]{2,1,0:T(8,128)(2,1)} %fusion.refs_0_, bf16[4,128,512]{2,1,0:T(8,128)(2,1)S(1)} %pad_maximum_fusion.refs_1_, bf16[4,128,512]{2,1,0:T(8,128)(2,1)} %collective-permute-done.9.refs_2_, ...), custom_call_target="tpu_custom_call" | custom-call | flops 1342177280 | bytes 5242880 | tf_op jit(solution)/shard_map/project_20/pallas_call | solution.py:77
  70.4 1.9 %project_8.2.refs_2_ = f32[512,512]{1,0:T(8,128)S(1)} custom-call(s32[32]{0:T(128)S(1)} %starts.1, bf16[512,8192]{1,0:T(8,128)(2,1)S(1)} %copy-done, bf16[4,128,512]{2,1,0:T(8,128)(2,1)} %collective-permute-done.11.refs_0_, bf16[4,128,512]{2,1,0:T(8,128)(2,1)} %collective-permute-done.12.refs_1_, f32[512,512]{1,0:T(8,128)S(1)} %project_20.1.refs_2_), custom_call_target="tpu_custom_call" | custom-call | flops 536870912 | bytes 2097152 | tf_op jit(solution)/shard_map/project_8/pallas_call | solution.py:77
  72.3 4.7 %collective-permute-done.16.refs_1_ = bf16[8,136,512]{2,1,0:T(8,128)(2,1)S(1)} collective-permute-done((bf16[8,136,512]{2,1,0:T(8,128)(2,1)}, bf16[8,136,512]{2,1,0:T(8,128)(2,1)S(1)}, u32[]{:S(2)}, u32[]{:S(2)}) %collective-permute-start.16) | collective-permute-done | bytes 1114144 | tf_op jit(solution)/shard_map/ppermute | solution.py:21
  78.3 2.5 %collective-permute-start.17 = (bf16[4,136,512]{2,1,0:T(8,128)(2,1)S(1)}, bf16[4,136,512]{2,1,0:T(8,128)(2,1)S(1)}, u32[]{:S(2)}, u32[]{:S(2)}) collective-permute-start(bf16[4,136,512]{2,1,0:T(8,128)(2,1)S(1)} %slice.43), channel_id=1, source_target_pairs={{64,0},{72,8},{80,16},{88,24},{96,32},{104,40},{112,48},{120,56},{... | collective-permute-start | bytes 1671176 | tf_op jit(solution)/shard_map/ppermute | solution.py:21
  81.6 1.8 %project_16.1.refs_2_ = f32[512,512]{1,0:T(8,128)S(1)} custom-call(s32[32]{0:T(128)S(1)} %starts.1, bf16[512,8192]{1,0:T(8,128)(2,1)S(1)} %copy-done, bf16[8,136,512]{2,1,0:T(8,128)(2,1)S(1)} %collective-permute-done.15.refs_0_, bf16[8,136,512]{2,1,0:T(8,128)(2,1)S(1)} %collective-permute-done.16.refs_1_, f32[512,512]{1,0:T(8,128)S(1)} %project_8.2.refs_2_), custom_call_target="tpu_custom_call" | custom-call | flops 1073741824 | bytes 4194304 | tf_op jit(solution)/shard_map/project_16/pallas_call | solution.py:77
  83.8 1.8 %collective-permute-start.22 = (bf16[2,128,512]{2,1,0:T(8,128)(2,1)S(1)}, bf16[2,128,512]{2,1,0:T(8,128)(2,1)S(1)}, u32[]{:S(2)}, u32[]{:S(2)}) collective-permute-start(bf16[2,128,512]{2,1,0:T(8,128)(2,1)S(1)} %slice.53), channel_id=1, source_target_pairs={{56,0},{0,8},{8,16},{16,24},{24,32},{32,40},{40,48},{48,56},{120,6... | collective-permute-start | bytes 786440 | tf_op jit(solution)/shard_map/ppermute | solution.py:21
  85.6 1.3 project_8.3.refs_4_
  86.9 2.0 %collective-permute-done.18.refs_1_ = bf16[4,136,512]{2,1,0:T(8,128)(2,1)S(1)} collective-permute-done((bf16[4,136,512]{2,1,0:T(8,128)(2,1)S(1)}, bf16[4,136,512]{2,1,0:T(8,128)(2,1)S(1)}, u32[]{:S(2)}, u32[]{:S(2)}) %collective-permute-start.18) | collective-permute-done | bytes 557088 | tf_op jit(solution)/shard_map/ppermute | solution.py:21
  89.0 2.5 %strip.1.strip_ref = bf16[256,16384]{1,0:T(8,128)(2,1)S(1)} custom-call(s32[3]{0:T(128)S(1)} %pad_add_fusion.place, f32[4,8,1,512]{3,2,1,0:T(1,128)S(1)} %fusion.4.taps), custom_call_target="tpu_custom_call" | custom-call | flops 10485760 | bytes 8388608 | tf_op jit(solution)/shard_map/strip/pallas_call | solution.py:168
  91.5 1.6 %project_12.1 = bf16[32,16,512]{2,1,0:T(8,128)(2,1)S(1)} custom-call(s32[32]{0:T(128)S(1)} %starts.1, bf16[512,8192]{1,0:T(8,128)(2,1)S(1)} %copy-done, bf16[4,136,512]{2,1,0:T(8,128)(2,1)S(1)} %collective-permute-done.17.refs_0_, bf16[4,136,512]{2,1,0:T(8,128)(2,1)S(1)} %collective-permute-done.18.refs_1_, ...), custom_call_target="tpu_custom_call" | custom-call | flops 805306368 | bytes 3145728 | tf_op jit(solution)/shard_map/project_12/pallas_call | solution.py:77
  93.1 23.8 %all_to_all.10.value = bf16[32,16,512]{2,1,0:T(8,128)(2,1)S(1)} all-to-all(bf16[32,16,512]{2,1,0:T(8,128)(2,1)S(1)} %project_12.1), channel_id=1, replica_groups=mesh['seq'=32,'tp'=8] {'seq'}, dimensions={0} | all-to-all | bytes 1048576 | tf_op jit(solution)/shard_map/all_to_all | solution.py:253
  117.0 4.9 %convolve.1 = bf16[32,16,512]{2,1,0:T(8,128)(2,1)S(1)} custom-call(bf16[32,16,512]{2,1,0:T(8,128)(2,1)S(1)} %all_to_all.10.value, bf16[256,16384]{1,0:T(8,128)(2,1)S(1)} %strip.1.strip_ref), custom_call_target="tpu_custom_call" | custom-call | flops 4499999744 | bytes 10485760 | tf_op jit(solution)/shard_map/convolve/pallas_call | solution.py:205
  121.9 18.4 %all_to_all.11 = bf16[32,16,512]{2,1,0:T(8,128)(2,1)S(1)} all-to-all(bf16[32,16,512]{2,1,0:T(8,128)(2,1)S(1)} %convolve.1), channel_id=1, replica_groups=mesh['seq'=32,'tp'=8] {'seq'}, dimensions={0} | all-to-all | bytes 1048576 | tf_op jit(solution)/shard_map/all_to_all | solution.py:255
  140.2 1.6 %mix.1 = bf16[512,512]{1,0:T(8,128)(2,1)} custom-call(bf16[512,512]{1,0:T(8,128)(2,1)S(1)} %bitcast.38, bf16[512,512]{1,0:T(8,128)(2,1)S(1)} %bitcast.37, f32[1,512]{1,0:T(1,128)S(1)} %bitcast.39, bf16[512,512]{1,0:T(8,128)(2,1)S(1)} %copy-done.1), custom_call_target="tpu_custom_call" | custom-call | tf_op jit(solution)/shard_map/mix/pallas_call | solution.py:229
  (64 shorter events, 15.1 us)
Async XLA Ops:
  6.5 0.9 copy-start.3
  6.5 6.3 %copy-start.4 = (bf16[512,4]{0,1:T(4,128)(2,1)S(1)}, bf16[512,4]{0,1:T(4,128)(2,1)}, u32[]{:S(2)}) copy-start(bf16[512,4]{0,1:T(4,128)(2,1)} %param.8) | copy-start | bytes 12292
  6.5 57.5 %all-gather.2.cloned.1.call-start = ((), (), s32[]{:S(2)}) async-start(), calls=%async_computation.2 | async-start | bytes 9437184 | tf_op jit(solution)/shard_map/all_gather | solution.py:248
  7.5 8.1 %collective-permute-start.7 = (bf16[128,512]{1,0:T(8,128)(2,1)S(1)}, bf16[128,512]{1,0:T(8,128)(2,1)S(1)}, u32[]{:S(2)}, u32[]{:S(2)}) collective-permute-start(bf16[128,512]{1,0:T(8,128)(2,1)S(1)} %get-tuple-element.38), channel_id=1, source_target_pairs={{128,0},{136,8},{144,16},{152,24},{160,32},{168,40},{176,48},{184,... | collective-permute-start | bytes 393224 | tf_op jit(solution)/shard_map/ppermute | solution.py:21
  10.8 6.7 %collective-permute-start.6 = (bf16[128,512]{1,0:T(8,128)(2,1)S(1)}, bf16[128,512]{1,0:T(8,128)(2,1)S(1)}, u32[]{:S(2)}, u32[]{:S(2)}) collective-permute-start(bf16[128,512]{1,0:T(8,128)(2,1)S(1)} %get-tuple-element.38), channel_id=1, source_target_pairs={{64,0},{72,8},{80,16},{88,24},{96,32},{104,40},{112,48},{120,56},{... | collective-permute-start | bytes 393224 | tf_op jit(solution)/shard_map/ppermute | solution.py:21
  11.9 6.2 %collective-permute-start.8 = (bf16[128,512]{1,0:T(8,128)(2,1)S(1)}, bf16[128,512]{1,0:T(8,128)(2,1)S(1)}, u32[]{:S(2)}, u32[]{:S(2)}) collective-permute-start(bf16[128,512]{1,0:T(8,128)(2,1)S(1)} %get-tuple-element.38), channel_id=1, source_target_pairs={{192,0},{200,8},{208,16},{216,24},{224,32},{232,40},{240,48},{248,... | collective-permute-start | bytes 393224 | tf_op jit(solution)/shard_map/ppermute | solution.py:21
  12.9 7.3 %collective-permute-start.3 = (bf16[136,512]{1,0:T(8,128)(2,1)S(1)}, bf16[136,512]{1,0:T(8,128)(2,1)S(1)}, u32[]{:S(2)}, u32[]{:S(2)}) collective-permute-start(bf16[136,512]{1,0:T(8,128)(2,1)S(1)} %pad_maximum_fusion.1), channel_id=1, source_target_pairs={{56,0},{0,8},{8,16},{16,24},{24,32},{32,40},{40,48},{48,56},{120,6... | collective-permute-start | bytes 417800 | tf_op jit(solution)/shard_map/ppermute | solution.py:21
  14.9 7.3 %collective-permute-start = (bf16[136,512]{1,0:T(8,128)(2,1)S(1)}, bf16[136,512]{1,0:T(8,128)(2,1)S(1)}, u32[]{:S(2)}, u32[]{:S(2)}) collective-permute-start(bf16[136,512]{1,0:T(8,128)(2,1)S(1)} %pad_maximum_fusion.1), channel_id=1, source_target_pairs={{8,0},{16,8},{24,16},{32,24},{40,32},{48,40},{56,48},{0,56},{72,64... | collective-permute-start | bytes 417800 | tf_op jit(solution)/shard_map/ppermute | solution.py:21
  18.1 23.3 %collective-permute-start.10 = (bf16[4,128,512]{2,1,0:T(8,128)(2,1)S(1)}, bf16[4,128,512]{2,1,0:T(8,128)(2,1)S(1)}, u32[]{:S(2)}, u32[]{:S(2)}) collective-permute-start(bf16[4,128,512]{2,1,0:T(8,128)(2,1)S(1)} %pad_maximum_fusion.refs_1_), channel_id=1, source_target_pairs={{56,0},{0,8},{8,16},{16,24},{24,32},{32,40},{40,48},{48,56},{120,6... | collective-permute-start | bytes 1572872 | tf_op jit(solution)/shard_map/ppermute | solution.py:21
  20.1 21.3 %collective-permute-start.9 = (bf16[4,128,512]{2,1,0:T(8,128)(2,1)S(1)}, bf16[4,128,512]{2,1,0:T(8,128)(2,1)}, u32[]{:S(2)}, u32[]{:S(2)}) collective-permute-start(bf16[4,128,512]{2,1,0:T(8,128)(2,1)S(1)} %pad_maximum_fusion.refs_1_), channel_id=1, source_target_pairs={{8,0},{16,8},{24,16},{32,24},{40,32},{48,40},{56,48},{0,56},{72,64... | collective-permute-start | bytes 1572872 | tf_op jit(solution)/shard_map/ppermute | solution.py:21
  20.2 13.5 %collective-permute-start.4 = (bf16[136,512]{1,0:T(8,128)(2,1)S(1)}, bf16[136,512]{1,0:T(8,128)(2,1)S(1)}, u32[]{:S(2)}, u32[]{:S(2)}) collective-permute-start(bf16[136,512]{1,0:T(8,128)(2,1)S(1)} %collective-permute-done.3), channel_id=1, source_target_pairs={{56,0},{0,8},{8,16},{16,24},{24,32},{32,40},{40,48},{48,56},{120,6... | collective-permute-start | bytes 417800 | tf_op jit(solution)/shard_map/ppermute | solution.py:21
  22.1 13.2 %collective-permute-start.1 = (bf16[136,512]{1,0:T(8,128)(2,1)S(1)}, bf16[136,512]{1,0:T(8,128)(2,1)S(1)}, u32[]{:S(2)}, u32[]{:S(2)}) collective-permute-start(bf16[136,512]{1,0:T(8,128)(2,1)S(1)} %collective-permute-done), channel_id=1, source_target_pairs={{8,0},{16,8},{24,16},{32,24},{40,32},{48,40},{56,48},{0,56},{72,64... | collective-permute-start | bytes 417800 | tf_op jit(solution)/shard_map/ppermute | solution.py:21
  33.7 7.0 %collective-permute-start.5 = (bf16[136,512]{1,0:T(8,128)(2,1)S(1)}, bf16[136,512]{1,0:T(8,128)(2,1)S(1)}, u32[]{:S(2)}, u32[]{:S(2)}) collective-permute-start(bf16[136,512]{1,0:T(8,128)(2,1)S(1)} %collective-permute-done.4), channel_id=1, source_target_pairs={{56,0},{0,8},{8,16},{16,24},{24,32},{32,40},{40,48},{48,56},{120,6... | collective-permute-start | bytes 417800 | tf_op jit(solution)/shard_map/ppermute | solution.py:21
  35.3 6.1 %collective-permute-start.2 = (bf16[136,512]{1,0:T(8,128)(2,1)S(1)}, bf16[136,512]{1,0:T(8,128)(2,1)S(1)}, u32[]{:S(2)}, u32[]{:S(2)}) collective-permute-start(bf16[136,512]{1,0:T(8,128)(2,1)S(1)} %collective-permute-done.1), channel_id=1, source_target_pairs={{8,0},{16,8},{24,16},{32,24},{40,32},{48,40},{56,48},{0,56},{72,64... | collective-permute-start | bytes 417800 | tf_op jit(solution)/shard_map/ppermute | solution.py:21
  41.4 7.9 %collective-permute-start.14 = (bf16[68,512]{1,0:T(8,128)(2,1)S(1)}, bf16[68,512]{1,0:T(8,128)(2,1)S(1)}, u32[]{:S(2)}, u32[]{:S(2)}) collective-permute-start(bf16[68,512]{1,0:T(8,128)(2,1)S(1)} %slice.42), channel_id=1, source_target_pairs={{56,0},{0,8},{8,16},{16,24},{24,32},{32,40},{40,48},{48,56},{120,6... | collective-permute-start | bytes 208904 | tf_op jit(solution)/shard_map/ppermute | solution.py:21
  44.8 6.4 %collective-permute-start.13 = (bf16[68,512]{1,0:T(8,128)(2,1)S(1)}, bf16[68,512]{1,0:T(8,128)(2,1)S(1)}, u32[]{:S(2)}, u32[]{:S(2)}) collective-permute-start(bf16[68,512]{1,0:T(8,128)(2,1)S(1)} %slice.41), channel_id=1, source_target_pairs={{8,0},{16,8},{24,16},{32,24},{40,32},{48,40},{56,48},{0,56},{72,64... | collective-permute-start | bytes 208904 | tf_op jit(solution)/shard_map/ppermute | solution.py:21
  44.8 13.3 %collective-permute-start.11 = (bf16[4,128,512]{2,1,0:T(8,128)(2,1)}, bf16[4,128,512]{2,1,0:T(8,128)(2,1)}, u32[]{:S(2)}, u32[]{:S(2)}) collective-permute-start(bf16[4,128,512]{2,1,0:T(8,128)(2,1)} %collective-permute-done.9.refs_2_), channel_id=1, source_target_pairs={{8,0},{16,8},{24,16},{32,24},{40,32},{48,40},{56,48},{0,56},{72,64... | collective-permute-start | bytes 1572872 | tf_op jit(solution)/shard_map/ppermute | solution.py:21
  47.4 10.7 %collective-permute-start.12 = (bf16[4,128,512]{2,1,0:T(8,128)(2,1)S(1)}, bf16[4,128,512]{2,1,0:T(8,128)(2,1)}, u32[]{:S(2)}, u32[]{:S(2)}) collective-permute-start(bf16[4,128,512]{2,1,0:T(8,128)(2,1)S(1)} %collective-permute-done.10.refs_3_), channel_id=1, source_target_pairs={{56,0},{0,8},{8,16},{16,24},{24,32},{32,40},{40,48},{48,56},{120,6... | collective-permute-start | bytes 1572872 | tf_op jit(solution)/shard_map/ppermute | solution.py:21
  51.9 25.2 %collective-permute-start.16 = (bf16[8,136,512]{2,1,0:T(8,128)(2,1)}, bf16[8,136,512]{2,1,0:T(8,128)(2,1)S(1)}, u32[]{:S(2)}, u32[]{:S(2)}) collective-permute-start(bf16[8,136,512]{2,1,0:T(8,128)(2,1)} %fusion.refs_0_), channel_id=1, source_target_pairs={{192,0},{200,8},{208,16},{216,24},{224,32},{232,40},{240,48},{248,... | collective-permute-start | bytes 3342344 | tf_op jit(solution)/shard_map/ppermute | solution.py:21
  54.1 23.2 %collective-permute-start.15 = (bf16[8,136,512]{2,1,0:T(8,128)(2,1)}, bf16[8,136,512]{2,1,0:T(8,128)(2,1)S(1)}, u32[]{:S(2)}, u32[]{:S(2)}) collective-permute-start(bf16[8,136,512]{2,1,0:T(8,128)(2,1)} %fusion.refs_0_), channel_id=1, source_target_pairs={{64,0},{72,8},{80,16},{88,24},{96,32},{104,40},{112,48},{120,56},{... | collective-permute-start | bytes 3342344 | tf_op jit(solution)/shard_map/ppermute | solution.py:21
  64.1 3.4 %copy-start = (bf16[512,8192]{1,0:T(8,128)(2,1)S(1)}, bf16[512,8192]{1,0:T(8,128)(2,1)}, u32[]{:S(2)}) copy-start(bf16[512,8192]{1,0:T(8,128)(2,1)} %all-gather.2.cloned.1.call-done.hidden) | copy-start | bytes 25165828
  65.3 18.1 %collective-permute-start.19 = (bf16[4,128,512]{2,1,0:T(8,128)(2,1)}, bf16[4,128,512]{2,1,0:T(8,128)(2,1)S(1)}, u32[]{:S(2)}, u32[]{:S(2)}) collective-permute-start(bf16[4,128,512]{2,1,0:T(8,128)(2,1)} %collective-permute-done.11.refs_0_), channel_id=1, source_target_pairs={{8,0},{16,8},{24,16},{32,24},{40,32},{48,40},{56,48},{0,56},{72,64... | collective-permute-start | bytes 1572872 | tf_op jit(solution)/shard_map/ppermute | solution.py:21
  65.8 17.9 %collective-permute-start.21 = (bf16[4,128,512]{2,1,0:T(8,128)(2,1)}, bf16[4,128,512]{2,1,0:T(8,128)(2,1)S(1)}, u32[]{:S(2)}, u32[]{:S(2)}) collective-permute-start(bf16[4,128,512]{2,1,0:T(8,128)(2,1)} %collective-permute-done.12.refs_1_), channel_id=1, source_target_pairs={{56,0},{0,8},{8,16},{16,24},{24,32},{32,40},{40,48},{48,56},{120,6... | collective-permute-start | bytes 1572872 | tf_op jit(solution)/shard_map/ppermute | solution.py:21
  77.4 11.5 %collective-permute-start.18 = (bf16[4,136,512]{2,1,0:T(8,128)(2,1)S(1)}, bf16[4,136,512]{2,1,0:T(8,128)(2,1)S(1)}, u32[]{:S(2)}, u32[]{:S(2)}) collective-permute-start(bf16[4,136,512]{2,1,0:T(8,128)(2,1)S(1)} %slice.44), channel_id=1, source_target_pairs={{192,0},{200,8},{208,16},{216,24},{224,32},{232,40},{240,48},{248,... | collective-permute-start | bytes 1671176 | tf_op jit(solution)/shard_map/ppermute | solution.py:21
  78.3 10.7 %collective-permute-start.17 = (bf16[4,136,512]{2,1,0:T(8,128)(2,1)S(1)}, bf16[4,136,512]{2,1,0:T(8,128)(2,1)S(1)}, u32[]{:S(2)}, u32[]{:S(2)}) collective-permute-start(bf16[4,136,512]{2,1,0:T(8,128)(2,1)S(1)} %slice.43), channel_id=1, source_target_pairs={{64,0},{72,8},{80,16},{88,24},{96,32},{104,40},{112,48},{120,56},{... | collective-permute-start | bytes 1671176 | tf_op jit(solution)/shard_map/ppermute | solution.py:21
  83.4 8.1 %collective-permute-start.20 = (bf16[2,128,512]{2,1,0:T(8,128)(2,1)S(1)}, bf16[2,128,512]{2,1,0:T(8,128)(2,1)S(1)}, u32[]{:S(2)}, u32[]{:S(2)}) collective-permute-start(bf16[2,128,512]{2,1,0:T(8,128)(2,1)S(1)} %slice.52), channel_id=1, source_target_pairs={{8,0},{16,8},{24,16},{32,24},{40,32},{48,40},{56,48},{0,56},{72,64... | collective-permute-start | bytes 786440 | tf_op jit(solution)/shard_map/ppermute | solution.py:21
  83.8 7.7 %collective-permute-start.22 = (bf16[2,128,512]{2,1,0:T(8,128)(2,1)S(1)}, bf16[2,128,512]{2,1,0:T(8,128)(2,1)S(1)}, u32[]{:S(2)}, u32[]{:S(2)}) collective-permute-start(bf16[2,128,512]{2,1,0:T(8,128)(2,1)S(1)} %slice.53), channel_id=1, source_target_pairs={{56,0},{0,8},{8,16},{16,24},{24,32},{32,40},{40,48},{48,56},{120,6... | collective-permute-start | bytes 786440 | tf_op jit(solution)/shard_map/ppermute | solution.py:21
  117.0 23.3 %copy-start.2 = (f32[512]{0:T(512)S(1)}, f32[512]{0:T(512)}, u32[]{:S(2)}) copy-start(f32[512]{0:T(512)} %param.9) | copy-start | bytes 6148
  121.8 18.4 %copy-start.1 = (bf16[512,512]{1,0:T(8,128)(2,1)S(1)}, bf16[512,512]{1,0:T(8,128)(2,1)}, u32[]{:S(2)}) copy-start(bf16[512,512]{1,0:T(8,128)(2,1)} %gate.1) | copy-start | bytes 1572868
Sparse Core Ops, SparseCore 0:
  9.2 54.8 all-gather.1
